TPU v7x, 256 devices: a whole 4x4x8 slice. The times are simulated.
256 devices in a mesh: tm: 8 (over x, z_lo), chan: 32 (over z_hi, y, core).
Axes of the slice: x: 4, y: 4, z: 8 (z_hi: 4, z_lo: 2; z = z_hi * 2 + z_lo), core: 2. Of those that a mesh axis runs over, the one named last changes fastest.
Arguments:
- strain: bfloat16 [16384, 2048], P('tm', 'chan'), may hold values from -6 to 6
Outputs:
- covariances: float32 [16, 2048, 2048], P(None, 'chan', 'tm')
All inputs are finite; a program needn't handle non-finite values.
Results may differ from a plain program's by a relative error of at most 0.0003.
Values may be sent and summed in bfloat16 or wider, within the bound.
No kernel may reach another device: no remote copies, remote signals or barrier semaphores. Data moves between devices by JAX's collectives and lax.ppermute only.
A program may use at most 64 MiB of HBM per device.

v0:
```python
import jax
import jax.numpy as jnp
from jax import lax
from jax.sharding import PartitionSpec as P

LAGS = 16


def shifted(value, axis, steps):
    count = lax.axis_size(axis)
    leading, last = (max(0, -steps), min(count, count - steps))
    return lax.ppermute(value, axis, [(source, source + steps) for source in range(leading, last)])


def lagged_products(own_rows, columns, samples):
    blocks = []
    for lag in range(LAGS):
        later = own_rows[lag : lag + samples]
        summed = lax.dot_general(
            later, columns, (((0,), (0,)), ((), ())), preferred_element_type=jnp.float32
        )
        blocks.append(summed)
    return jnp.stack(blocks, axis=0)


def normalize(sums, total):
    counts = jnp.float32(total) - jnp.arange(LAGS, dtype=jnp.float32)
    return sums / counts[:, None, None]


def on_device(strain):
    samples = strain.shape[0]
    total = samples * lax.axis_size("tm")
    gathered = lax.all_gather(strain, "chan", axis=1, tiled=True)
    following = shifted(strain[: LAGS - 1], "tm", -1)
    extended = jnp.concatenate([strain, following], axis=0)
    terms = lagged_products(extended, gathered, samples)
    summed = lax.psum_scatter(terms, "tm", scatter_dimension=2, tiled=True)
    return normalize(summed, total)


def solution(mesh):
    placed = (P("tm", "chan"),)
    return jax.shard_map(
        on_device, mesh=mesh, in_specs=placed, out_specs=P(None, "chan", "tm"), check_vma=False
    )
```

profile of v0, /device:TPU:1, one launch (start us, length us, event | category | flops | bytes accessed | tf_op | source)
XLA Modules:
  0.0 331.6 jit_solution(15269813046023177405)
XLA Ops:
  6.5 0.0 all-gather.2.cloned.1.call-start
  6.5 0.7 all-gather.2.cloned.1.call-update
  7.3 0.0 reduce-scatter.2.cloned.1.call-start
  7.3 0.7 slice.48
  8.0 1.3 collective-permute-start
  9.3 1.0 constant_dynamic-update-slice_fusion.1
  10.3 3.2 collective-permute-done
  13.5 76.7 %all-gather.2.cloned.1.call-done = bf16[2048,2048]{0,1:T(8,128)(2,1)} async-done(((bf16[2048,64]{0,1:T(8,128)(2,1)}), bf16[2048,2048]{0,1:T(8,128)(2,1)}) %all-gather.2.cloned.1.call-update) | async-done | bytes 8388624 | tf_op jit(solution)/shard_map/all_gather | solution.py:34
  90.3 0.0 copy-start
  90.3 7.1 %fusion.15 = f32[16,64,2048]{2,1,0:T(8,128)} fusion(bf16[2048,64]{0,1:T(8,128)(2,1)} %param.1, bf16[2048,2048]{0,1:T(8,128)(2,1)} %all-gather.2.cloned.1.call-done), kind=kOutput, calls=%fused_computation.31 | convolution fusion | flops 536870912 | bytes 9175040 | tf_op jit(solution)/shard_map/dot_general | solution.py:19
  97.3 0.0 copy-done
  97.3 3.5 %fusion.14 = f32[16,64,2048]{2,1,0:T(8,128)} fusion(f32[16,64,2048]{2,1,0:T(8,128)} %fusion.15, bf16[2048,2048]{0,1:T(8,128)(2,1)S(1)} %copy-done, bf16[2063,64]{0,1:T(8,128)(2,1)S(1)} %constant_dynamic-update-slice_fusion), kind=kOutput, calls=%fused_computation.29 | convolution fusion | flops 536870912 | bytes 9175040 | tf_op jit(solution)/shard_map/dot_general | solution.py:19
  100.8 3.5 %fusion.13 = f32[16,64,2048]{2,1,0:T(8,128)} fusion(f32[16,64,2048]{2,1,0:T(8,128)} %fusion.14, bf16[2048,2048]{0,1:T(8,128)(2,1)S(1)} %copy-done, bf16[2063,64]{0,1:T(8,128)(2,1)S(1)} %constant_dynamic-update-slice_fusion), kind=kOutput, calls=%fused_computation.27 | convolution fusion | flops 536870912 | bytes 9175040 | tf_op jit(solution)/shard_map/dot_general | solution.py:19
  104.3 3.5 %fusion.12 = f32[16,64,2048]{2,1,0:T(8,128)} fusion(f32[16,64,2048]{2,1,0:T(8,128)} %fusion.13, bf16[2048,2048]{0,1:T(8,128)(2,1)S(1)} %copy-done, bf16[2063,64]{0,1:T(8,128)(2,1)S(1)} %constant_dynamic-update-slice_fusion), kind=kOutput, calls=%fused_computation.25 | convolution fusion | flops 536870912 | bytes 9175040 | tf_op jit(solution)/shard_map/dot_general | solution.py:19
  107.7 3.5 %fusion.11 = f32[16,64,2048]{2,1,0:T(8,128)} fusion(f32[16,64,2048]{2,1,0:T(8,128)} %fusion.12, bf16[2048,2048]{0,1:T(8,128)(2,1)S(1)} %copy-done, bf16[2063,64]{0,1:T(8,128)(2,1)S(1)} %constant_dynamic-update-slice_fusion), kind=kOutput, calls=%fused_computation.23 | convolution fusion | flops 536870912 | bytes 9175040 | tf_op jit(solution)/shard_map/dot_general | solution.py:19
  111.2 3.5 %fusion.10 = f32[16,64,2048]{2,1,0:T(8,128)} fusion(f32[16,64,2048]{2,1,0:T(8,128)} %fusion.11, bf16[2048,2048]{0,1:T(8,128)(2,1)S(1)} %copy-done, bf16[2063,64]{0,1:T(8,128)(2,1)S(1)} %constant_dynamic-update-slice_fusion), kind=kOutput, calls=%fused_computation.21 | convolution fusion | flops 536870912 | bytes 9175040 | tf_op jit(solution)/shard_map/dot_general | solution.py:19
  114.7 3.6 %fusion.9 = f32[16,64,2048]{2,1,0:T(8,128)} fusion(f32[16,64,2048]{2,1,0:T(8,128)} %fusion.10, bf16[2048,2048]{0,1:T(8,128)(2,1)S(1)} %copy-done, bf16[2063,64]{0,1:T(8,128)(2,1)S(1)} %constant_dynamic-update-slice_fusion), kind=kOutput, calls=%fused_computation.19 | convolution fusion | flops 536870912 | bytes 9175040 | tf_op jit(solution)/shard_map/dot_general | solution.py:19
  118.3 3.5 %fusion.8 = f32[16,64,2048]{2,1,0:T(8,128)} fusion(f32[16,64,2048]{2,1,0:T(8,128)} %fusion.9, bf16[2048,2048]{0,1:T(8,128)(2,1)S(1)} %copy-done, bf16[2063,64]{0,1:T(8,128)(2,1)S(1)} %constant_dynamic-update-slice_fusion), kind=kOutput, calls=%fused_computation.17 | convolution fusion | flops 536870912 | bytes 9175040 | tf_op jit(solution)/shard_map/dot_general | solution.py:19
  121.8 3.5 %fusion.7 = f32[16,64,2048]{2,1,0:T(8,128)} fusion(f32[16,64,2048]{2,1,0:T(8,128)} %fusion.8, bf16[2048,2048]{0,1:T(8,128)(2,1)S(1)} %copy-done, bf16[2063,64]{0,1:T(8,128)(2,1)S(1)} %constant_dynamic-update-slice_fusion), kind=kOutput, calls=%fused_computation.15 | convolution fusion | flops 536870912 | bytes 9175040 | tf_op jit(solution)/shard_map/dot_general | solution.py:19
  125.3 3.5 %fusion.6 = f32[16,64,2048]{2,1,0:T(8,128)} fusion(f32[16,64,2048]{2,1,0:T(8,128)} %fusion.7, bf16[2048,2048]{0,1:T(8,128)(2,1)S(1)} %copy-done, bf16[2063,64]{0,1:T(8,128)(2,1)S(1)} %constant_dynamic-update-slice_fusion), kind=kOutput, calls=%fused_computation.13 | convolution fusion | flops 536870912 | bytes 9175040 | tf_op jit(solution)/shard_map/dot_general | solution.py:19
  128.8 3.5 %fusion.5 = f32[16,64,2048]{2,1,0:T(8,128)} fusion(f32[16,64,2048]{2,1,0:T(8,128)} %fusion.6, bf16[2048,2048]{0,1:T(8,128)(2,1)S(1)} %copy-done, bf16[2063,64]{0,1:T(8,128)(2,1)S(1)} %constant_dynamic-update-slice_fusion), kind=kOutput, calls=%fused_computation.11 | convolution fusion | flops 536870912 | bytes 9175040 | tf_op jit(solution)/shard_map/dot_general | solution.py:19
  132.3 3.5 %fusion.4 = f32[16,64,2048]{2,1,0:T(8,128)} fusion(f32[16,64,2048]{2,1,0:T(8,128)} %fusion.5, bf16[2048,2048]{0,1:T(8,128)(2,1)S(1)} %copy-done, bf16[2063,64]{0,1:T(8,128)(2,1)S(1)} %constant_dynamic-update-slice_fusion), kind=kOutput, calls=%fused_computation.9 | convolution fusion | flops 536870912 | bytes 9175040 | tf_op jit(solution)/shard_map/dot_general | solution.py:19
  135.7 3.5 %fusion.3 = f32[16,64,2048]{2,1,0:T(8,128)} fusion(f32[16,64,2048]{2,1,0:T(8,128)} %fusion.4, bf16[2048,2048]{0,1:T(8,128)(2,1)S(1)} %copy-done, bf16[2063,64]{0,1:T(8,128)(2,1)S(1)} %constant_dynamic-update-slice_fusion), kind=kOutput, calls=%fused_computation.7 | convolution fusion | flops 536870912 | bytes 9175040 | tf_op jit(solution)/shard_map/dot_general | solution.py:19
  139.2 3.7 %fusion.2 = f32[16,64,2048]{2,1,0:T(8,128)} fusion(f32[16,64,2048]{2,1,0:T(8,128)} %fusion.3, bf16[2048,2048]{0,1:T(8,128)(2,1)S(1)} %copy-done, bf16[2063,64]{0,1:T(8,128)(2,1)S(1)} %constant_dynamic-update-slice_fusion), kind=kOutput, calls=%fused_computation.5 | convolution fusion | flops 536870912 | bytes 9175040 | tf_op jit(solution)/shard_map/dot_general | solution.py:19
  142.9 3.4 %fusion.1 = f32[16,64,2048]{2,1,0:T(8,128)} fusion(f32[16,64,2048]{2,1,0:T(8,128)} %fusion.2, bf16[2048,2048]{0,1:T(8,128)(2,1)S(1)} %copy-done, bf16[2063,64]{0,1:T(8,128)(2,1)S(1)} %constant_dynamic-update-slice_fusion), kind=kOutput, calls=%fused_computation.3 | convolution fusion | flops 536870912 | bytes 9175040 | tf_op jit(solution)/shard_map/dot_general | solution.py:19
  146.3 3.5 %fusion = f32[16,64,2048]{2,1,0:T(8,128)} fusion(f32[16,64,2048]{2,1,0:T(8,128)} %fusion.1, bf16[2048,2048]{0,1:T(8,128)(2,1)S(1)} %copy-done, bf16[2063,64]{0,1:T(8,128)(2,1)S(1)} %constant_dynamic-update-slice_fusion), kind=kOutput, calls=%fused_computation.1 | convolution fusion | flops 536870912 | bytes 9175040 | tf_op jit(solution)/shard_map/dot_general | solution.py:19
  149.9 0.0 reduce-scatter.2.cloned.1.call-update
  149.9 172.5 %reduce-scatter.2.cloned.1.call-done = f32[16,64,256]{2,1,0:T(8,128)} async-done(((f32[16,64,2048]{2,1,0:T(8,128)}), f32[16,64,256]{2,1,0:T(8,128)}) %reduce-scatter.2.cloned.1.call-update) | async-done | bytes 1048592 | tf_op jit(solution)/shard_map/reduce_scatter | solution.py:38
  322.4 2.4 broadcast_divide_fusion
  (2 shorter events, 0.0 us)
Async XLA Ops:
  6.5 83.7 %all-gather.2.cloned.1.call-start = ((), (), s32[]{:S(2)}) async-start(), calls=%async_computation.1 | async-start | bytes 8650752 | tf_op jit(solution)/shard_map/all_gather | solution.py:34
  7.3 315.1 %reduce-scatter.2.cloned.1.call-start = ((), (), s32[]{:S(2)}) async-start(), calls=%async_computation.2 | async-start | bytes 9437184 | tf_op jit(solution)/shard_map/reduce_scatter | solution.py:38
  8.0 5.5 %collective-permute-start = (bf16[15,64]{0,1:T(8,128)(2,1)S(1)}, bf16[15,64]{0,1:T(8,128)(2,1)S(1)}, u32[]{:S(2)}, u32[]{:S(2)}) collective-permute-start(bf16[15,64]{0,1:T(8,128)(2,1)S(1)} %slice.48), channel_id=1, source_target_pairs={{32,0},{64,32},{96,64},{128,96},{160,128},{192,160},{224,192},{33,... | collective-permute-start | bytes 5768 | tf_op jit(solution)/shard_map/ppermute | solution.py:12
  90.3 7.1 %copy-start = (bf16[2048,2048]{0,1:T(8,128)(2,1)S(1)}, bf16[2048,2048]{0,1:T(8,128)(2,1)}, u32[]{:S(2)}) copy-start(bf16[2048,2048]{0,1:T(8,128)(2,1)} %all-gather.2.cloned.1.call-done) | copy-start | bytes 25165828
Sparse Core Ops, SparseCore 0:
  9.9 80.3 all-gather.1
  150.0 172.3 reduce-scatter.1
where the time goes:
time: 332 us
  waiting for transfers between devices  253 us (76%)
  matrix products  59.6 us (18%)
  between operations  13.4 us (4%)
    reduce_scatter x1, waiting for transfers between devices, on_device(): summed = lax.psum_scatter(terms, 'tm', scatter_dimension=2, tiled=True)  172 us
    all_gather x1, waiting for transfers between devices, on_device(): gathered = lax.all_gather(strain, 'chan', axis=1, tiled=True)  76.7 us
    dot_general x16, matrix products, lagged_products(): lax.dot_general(later, columns, (((0,), (0,)), ((), ())), preferred_eleme...  59.6 us
  transfers between devices with their start and end apart: 3, of which 3 were waited for; matrix products, arithmetic and copies ran while one was open for 1% of the time, Pallas kernels for 0%

commit v1 on v0

v1 whole, which is shorter than its diff:
```python
import jax
import jax.numpy as jnp
from jax import lax
from jax.experimental import pallas as pl
from jax.experimental.pallas import tpu as pltpu
from jax.sharding import Mesh, PartitionSpec as P

LAGS = 16
TOTAL = 16384
AXES = ("x", "zl", "zh", "y", "c")
SIZES = (4, 2, 4, 4, 2)
CH, SPAN, QUARTER, LANES = 128, 1024, 256, 128
OFFSETS = (0, 1, 3, 2)


def device_of(x, zl, zh, y, c):
    return (((x * 2 + zl) * 4 + zh) * 4 + y) * 2 + c


def scatter_pairs(quarter):
    pairs = []
    for x in range(4):
        for zl in range(2):
            for zh in range(4):
                for y in range(4):
                    to_zl = y // 2
                    to_y = y if zl == to_zl else (y + 2) % 4
                    for c in range(2):
                        target = device_of(zh, to_zl, (x + quarter) % 4, to_y, c)
                        pairs.append((device_of(x, zl, zh, y, c), target))
    return pairs


def pull(value, axis, offset, count):
    return lax.ppermute(value, axis, [((i + offset) % count, i) for i in range(count)])


def swap(value, axis, bits, count):
    return lax.ppermute(value, axis, [(i, i ^ bits) for i in range(count)])


def kernel(ix, rows_0, rows_1, rows_3, rows_2, *refs):
    cols, (keep, send, rows, later, earlier, total) = refs[:16], refs[16:]
    x, zl, zh, y, c = (ix[i] for i in range(5))
    for offset, slabs in zip(OFFSETS, (rows_0, rows_1, rows_3, rows_2)):
        for m in range(2):
            rows[lax.rem(x + offset, 4), lax.rem(zl + m, 2)] = slabs[m]
    half = lax.rem(y, 2)
    zl_own = lax.select(lax.div(y, 2) == zl, zl, 1 - zl)
    for at, offset in enumerate(OFFSETS):
        for pair in range(2):
            zl_slab = zl_own if pair == 0 else 1 - zl_own
            for q in range(4):
                x_slab = lax.rem(zh + offset - q + 8, 4)
                window = rows[x_slab, zl_slab, :, pl.ds(QUARTER * q, QUARTER + LANES)]
                for lag in range(LAGS):
                    later[lag * CH : (lag + 1) * CH, QUARTER * q : QUARTER * (q + 1)] = window[:, lag : lag + QUARTER]
            same, other = cols[4 * at + 2 * pair : 4 * at + 2 * pair + 2]
            earlier[pl.ds(pl.multiple_of(half * CH, CH), CH), :] = same[...]
            earlier[pl.ds(pl.multiple_of((1 - half) * CH, CH), CH), :] = other[...]
            part = lax.dot_general(
                later[...], earlier[...], (((1,), (1,)), ((), ())), preferred_element_type=jnp.float32
            )
            if at == 0 and pair == 0:
                total[...] = part
            else:
                total[...] += part
    for lag in range(LAGS):
        keep[lag] = total[pl.ds(pl.multiple_of(lag * CH + c * 64, 64), 64), :]
        send[lag] = total[pl.ds(pl.multiple_of(lag * CH + (1 - c) * 64, 64), 64), :]


def products(ix, rows, cols):
    vmem = pl.BlockSpec(memory_space=pltpu.VMEM)
    half = jax.ShapeDtypeStruct((LAGS, 64, 256), jnp.float32)
    return pl.pallas_call(
        kernel,
        out_shape=(half, half),
        in_specs=[pl.BlockSpec(memory_space=pltpu.SMEM)] + [vmem] * 20,
        out_specs=(vmem, vmem),
        scratch_shapes=[
            pltpu.VMEM((4, 2, CH, SPAN + LANES), jnp.bfloat16),
            pltpu.VMEM((LAGS * CH, SPAN), jnp.bfloat16),
            pltpu.VMEM((256, SPAN), jnp.bfloat16),
            pltpu.VMEM((LAGS * CH, 256), jnp.float32),
        ],
        compiler_params=pltpu.CompilerParams(vmem_limit_bytes=48 * 2**20),
        cost_estimate=pl.CostEstimate(flops=2 * 2048 * 256 * 8192, bytes_accessed=8 * 2**20, transcendentals=0),
    )(ix, *rows, *cols)


def spread(one, two):
    one_1, two_1 = swap(one, "y", 1, 4), swap(two, "y", 1, 4)
    one_3, two_3 = swap(one, "y", 3, 4), swap(two, "y", 3, 4)
    one_2, two_2 = swap(one_1, "y", 3, 4), swap(two_3, "y", 1, 4)
    return [one, one_1, one_2, one_3], [two, two_1, two_2, two_3]


def on_device(strain):
    c = lax.axis_index("c")
    own = strain.T
    mine = lax.dynamic_slice(own, (0, c * SPAN), (64, SPAN))
    others = lax.dynamic_slice(own, (0, (1 - c) * SPAN), (64, SPAN))
    got = swap(others, "c", 1, 2)
    block = jnp.where(c == 0, jnp.concatenate([mine, got]), jnp.concatenate([got, mine]))

    quarters = [
        lax.ppermute(block[:, QUARTER * q : QUARTER * (q + 1)], AXES, scatter_pairs(q)) for q in range(4)
    ]
    held = jnp.concatenate(quarters, axis=1)

    head = lax.ppermute(block[:, :LANES], ("x", "zl", "c"), [(i, i - 1) for i in range(1, 16)])
    slab = jnp.concatenate([block, head], axis=1)
    slabs = jnp.stack([slab, swap(slab, "zl", 1, 2)])
    rows = [slabs] + [pull(slabs, "x", offset, 4) for offset in OFFSETS[1:]]

    above, below = pull(held, "zh", 1, 4), pull(held, "zh", 3, 4)
    across = pull(held, "zh", 2, 4)
    cols_1, cols_3 = spread(above, below)
    cols_0, cols_2 = spread(held, across)

    ix = jnp.stack([lax.axis_index(name) for name in AXES]).astype(jnp.int32)
    order = [c4[i] for c4 in (cols_0, cols_1, cols_3, cols_2) for i in (0, 1, 2, 3)]
    keep, send = products(ix, rows, order)
    summed = keep + swap(send, "c", 1, 2)
    counts = jnp.float32(TOTAL) - jnp.arange(LAGS, dtype=jnp.float32)
    return summed / counts[:, None, None]


def solution(mesh):
    fine = Mesh(mesh.devices.reshape(SIZES), AXES)
    return jax.shard_map(
        on_device,
        mesh=fine,
        in_specs=(P(("x", "zl"), ("zh", "y", "c")),),
        out_specs=P(None, ("zh", "y", "c"), ("x", "zl")),
        check_vma=False,
    )
```

time: 332 us -> 146 us (0.44)
  waiting for transfers between devices: 253 us -> 55.6 us
  matrix products: 59.6 us -> 0 us
  starting transfers between devices: 1.32 us -> 54.2 us
  Pallas kernels: 0 us -> 20.3 us
  between operations: 13.4 us -> 0.18 us
  local copies, waits for them, and re-layouts: 1.7 us -> 10.3 us
    reduce_scatter x1 -> x0, waiting for transfers between devices: 172 us -> none  [on_device(): summed = lax.psum_scatter(terms, 'tm', scatter_dimension=2, tiled=True)]
    all_gather x1 -> x0, waiting for transfers between devices: 76.7 us -> none  [on_device(): gathered = lax.all_gather(strain, 'chan', axis=1, tiled=True)]
    dot_general x16 -> x0, matrix products: 59.6 us -> none  [lagged_products(): lax.dot_general(later, columns, (((0,), (0,)), ((), ())), preferred_eleme...]
    ppermute x1 -> x26, starting transfers between devices: 1.28 us -> 54.2 us  [the longest x6 20 us: pull(): lax.ppermute(value, axis, [((i + offset) % count, i) for i in range(count)])]
    ppermute x1 -> x26, waiting for transfers between devices: 3.22 us -> 55.6 us  [the longest x6 24.2 us: pull(): lax.ppermute(value, axis, [((i + offset) % count, i) for i in range(count)])]
    pallas_call x0 -> x1, Pallas kernels: none -> 20.3 us  [products(): pl.pallas_call(kernel, out_shape=(half, half), in_specs=[pl.BlockSpec(mem...]
    unnamed x3 -> x27, local copies, waits for them, and re-layouts: 0.97 us -> 9.21 us
  transfers between devices with their start and end apart: 3 -> 26, of which waited for: 3 -> 12; matrix products, arithmetic and copies ran while one was open for 1% -> 0% of each run, Pallas kernels for 0% -> 0%
where the time goes in v1:
time: 146 us; the launch traced here: 143 us
  waiting for transfers between devices  55.6 us (38%)
  starting transfers between devices  54.2 us (37%)
  Pallas kernels  20.3 us (14%)
  local copies, waits for them, and re-layouts  10.3 us (7%)
  other arithmetic  2.56 us (2%)
    ppermute x6, waiting for transfers between devices, pull(): lax.ppermute(value, axis, [((i + offset) % count, i) for i in range(count)])  24.2 us
    ppermute x15, waiting for transfers between devices, swap(): return lax.ppermute(value, axis, [(i, i ^ bits) for i in range(count)])  23.5 us
    pallas_call x1, Pallas kernels, products(): pl.pallas_call(kernel, out_shape=(half, half), in_specs=[pl.BlockSpec(mem...  20.3 us
    ppermute x6, starting transfers between devices, pull(): lax.ppermute(value, axis, [((i + offset) % count, i) for i in range(count)])  20 us
    ppermute x15, starting transfers between devices, swap(): return lax.ppermute(value, axis, [(i, i ^ bits) for i in range(count)])  15.7 us
    ppermute x4, starting transfers between devices, on_device(): lax.ppermute(block[:, QUARTER * q:QUARTER * (q + 1)], AXES, scatter_pairs...  15.2 us
    unnamed x27, local copies, waits for them, and re-layouts  9.21 us
    ppermute x1, waiting for transfers between devices, on_device(): lax.ppermute(block[:, :LANES], ('x', 'zl', 'c'), [(i, i - 1) for i in ran...  7.91 us
  transfers between devices with their start and end apart: 26, of which 12 were waited for; matrix products, arithmetic and copies ran while one was open for 0% of the time, Pallas kernels for 0%

profile of v1, /device:TPU:1, one launch (start us, length us, event | category | flops | bytes accessed | tf_op | source)
XLA Modules:
  0.0 143.1 jit_solution(1529302226346153960)
XLA Ops:
  0.0 1.0 dynamic-slice_bitcast_fusion.1
  1.0 3.3 %collective-permute-start = (bf16[64,1024]{1,0:T(8,128)(2,1)S(1)}, bf16[64,1024]{1,0:T(8,128)(2,1)S(1)}, u32[]{:S(2)}, u32[]{:S(2)}) collective-permute-start(bf16[64,1024]{1,0:T(8,128)(2,1)S(1)} %get-tuple-element.16), channel_id=1, source_target_pairs={{0,1},{1,0},{2,3},{3,2},{4,5},{5,4},{6,7},{7,6},{8,9},{9,8},{10,11... | collective-permute-start | bytes 393224 | tf_op jit(solution)/shard_map/ppermute | solution.py:39
  4.3 1.0 collective-permute-done
  6.1 2.9 %collective-permute-start.7 = (bf16[128,256]{1,0:T(8,128)(2,1)S(1)}, bf16[128,256]{1,0:T(8,128)(2,1)S(1)}, u32[]{:S(2)}, u32[]{:S(2)}) collective-permute-start(bf16[128,256]{1,0:T(8,128)(2,1)S(1)} %get-tuple-element.13), channel_id=1, source_target_pairs={{0,8},{1,9},{2,10},{3,11},{4,40},{5,41},{6,42},{7,43},{8,72},{9,73... | collective-permute-start | bytes 196616 | tf_op jit(solution)/shard_map/ppermute | solution.py:108
  9.0 9.6 %collective-permute-start.8 = (bf16[128,256]{1,0:T(8,128)(2,1)S(1)}, bf16[128,256]{1,0:T(8,128)(2,1)S(1)}, u32[]{:S(2)}, u32[]{:S(2)}) collective-permute-start(bf16[128,256]{1,0:T(8,128)(2,1)S(1)} %get-tuple-element.12), channel_id=1, source_target_pairs={{0,16},{1,17},{2,18},{3,19},{4,48},{5,49},{6,50},{7,51},{8,80},{9,... | collective-permute-start | bytes 196616 | tf_op jit(solution)/shard_map/ppermute | solution.py:108
  18.6 2.1 %collective-permute-start.9 = (bf16[128,256]{1,0:T(8,128)(2,1)S(1)}, bf16[128,256]{1,0:T(8,128)(2,1)S(1)}, u32[]{:S(2)}, u32[]{:S(2)}) collective-permute-start(bf16[128,256]{1,0:T(8,128)(2,1)S(1)} %get-tuple-element.11), channel_id=1, source_target_pairs={{0,24},{1,25},{2,26},{3,27},{4,56},{5,57},{6,58},{7,59},{8,88},{9,... | collective-permute-start | bytes 196616 | tf_op jit(solution)/shard_map/ppermute | solution.py:108
  20.6 3.4 %collective-permute-start.1 = (bf16[128,128]{1,0:T(8,128)(2,1)S(1)}, bf16[128,128]{1,0:T(8,128)(2,1)S(1)}, u32[]{:S(2)}, u32[]{:S(2)}) collective-permute-start(bf16[128,128]{1,0:T(8,128)(2,1)S(1)} %slice.20), channel_id=1, source_target_pairs={{1,0},{32,1},{33,32},{64,33},{65,64},{96,65},{97,96},{128,97},{129... | collective-permute-start | bytes 98312 | tf_op jit(solution)/shard_map/ppermute | solution.py:112
  24.1 2.2 %collective-permute-start.13 = (bf16[128,1024]{1,0:T(8,128)(2,1)S(1)}, bf16[128,1024]{1,0:T(8,128)(2,1)S(1)}, u32[]{:S(2)}, u32[]{:S(2)}) collective-permute-start(bf16[128,1024]{1,0:T(8,128)(2,1)S(1)} %constant_dynamic-update-slice_fusion.refs_0_), channel_id=1, source_target_pairs={{8,0},{16,8},{24,16},{0,24},{9,1},{17,9},{25,17},{1,25},{10,2},{18... | collective-permute-start | bytes 786440 | tf_op jit(solution)/shard_map/ppermute | solution.py:35
  26.6 7.9 %collective-permute-done.1 = bf16[128,128]{1,0:T(8,128)(2,1)S(1)} collective-permute-done((bf16[128,128]{1,0:T(8,128)(2,1)S(1)}, bf16[128,128]{1,0:T(8,128)(2,1)S(1)}, u32[]{:S(2)}, u32[]{:S(2)}) %collective-permute-start.1) | collective-permute-done | bytes 32800 | tf_op jit(solution)/shard_map/ppermute | solution.py:112
  34.6 7.2 %collective-permute-start.21 = (bf16[128,1024]{1,0:T(8,128)(2,1)S(1)}, bf16[128,1024]{1,0:T(8,128)(2,1)S(1)}, u32[]{:S(2)}, u32[]{:S(2)}) collective-permute-start(bf16[128,1024]{1,0:T(8,128)(2,1)S(1)} %constant_dynamic-update-slice_fusion.refs_0_), channel_id=1, source_target_pairs={{16,0},{24,8},{0,16},{8,24},{17,1},{25,9},{1,17},{9,25},{18,2},{26... | collective-permute-start | bytes 786440 | tf_op jit(solution)/shard_map/ppermute | solution.py:35
  42.2 2.2 %collective-permute-start.14 = (bf16[128,1024]{1,0:T(8,128)(2,1)S(1)}, bf16[128,1024]{1,0:T(8,128)(2,1)S(1)}, u32[]{:S(2)}, u32[]{:S(2)}) collective-permute-start(bf16[128,1024]{1,0:T(8,128)(2,1)S(1)} %collective-permute-done.13.refs_4_), channel_id=1, source_target_pairs={{0,2},{2,0},{4,6},{6,4},{1,3},{3,1},{5,7},{7,5},{8,10},{10,8},{12,... | collective-permute-start | bytes 786440 | tf_op jit(solution)/shard_map/ppermute | solution.py:39
  44.5 19.7 %collective-permute-done.21.refs_12_ = bf16[128,1024]{1,0:T(8,128)(2,1)S(1)} collective-permute-done((bf16[128,1024]{1,0:T(8,128)(2,1)S(1)}, bf16[128,1024]{1,0:T(8,128)(2,1)S(1)}, u32[]{:S(2)}, u32[]{:S(2)}) %collective-permute-start.21) | collective-permute-done | bytes 262176 | tf_op jit(solution)/shard_map/ppermute | solution.py:35
  64.2 2.7 %collective-permute-start.23 = (bf16[128,1024]{1,0:T(8,128)(2,1)S(1)}, bf16[128,1024]{1,0:T(8,128)(2,1)}, u32[]{:S(2)}, u32[]{:S(2)}) collective-permute-start(bf16[128,1024]{1,0:T(8,128)(2,1)S(1)} %collective-permute-done.21.refs_12_), channel_id=1, source_target_pairs={{0,6},{2,4},{4,2},{6,0},{1,7},{3,5},{5,3},{7,1},{8,14},{10,12},{12... | collective-permute-start | bytes 786440 | tf_op jit(solution)/shard_map/ppermute | solution.py:39
  67.0 2.6 %collective-permute-start.16 = (bf16[128,1024]{1,0:T(8,128)(2,1)S(1)}, bf16[128,1024]{1,0:T(8,128)(2,1)S(1)}, u32[]{:S(2)}, u32[]{:S(2)}) collective-permute-start(bf16[128,1024]{1,0:T(8,128)(2,1)S(1)} %collective-permute-done.13.refs_4_), channel_id=1, source_target_pairs={{0,6},{2,4},{4,2},{6,0},{1,7},{3,5},{5,3},{7,1},{8,14},{10,12},{12... | collective-permute-start | bytes 786440 | tf_op jit(solution)/shard_map/ppermute | solution.py:39
  69.6 1.5 %collective-permute-done.19.refs_11_ = bf16[128,1024]{1,0:T(8,128)(2,1)} collective-permute-done((bf16[128,1024]{1,0:T(8,128)(2,1)S(1)}, bf16[128,1024]{1,0:T(8,128)(2,1)}, u32[]{:S(2)}, u32[]{:S(2)}) %collective-permute-start.19) | collective-permute-done | bytes 262176 | tf_op jit(solution)/shard_map/ppermute | solution.py:39
  71.1 7.3 %collective-permute-start.3 = (bf16[2,128,1152]{2,1,0:T(8,128)(2,1)S(1)}, bf16[2,128,1152]{2,1,0:T(8,128)(2,1)S(1)}, u32[]{:S(2)}, u32[]{:S(2)}) collective-permute-start(bf16[2,128,1152]{2,1,0:T(8,128)(2,1)S(1)} %pad_maximum_fusion.rows_0), channel_id=1, source_target_pairs={{64,0},{128,64},{192,128},{0,192},{65,1},{129,65},{193,129},{1,193... | collective-permute-start | bytes 1769480 | tf_op jit(solution)/shard_map/ppermute | solution.py:35
  78.5 3.8 %collective-permute-done.11.refs_2_ = bf16[128,1024]{1,0:T(8,128)(2,1)S(1)} collective-permute-done((bf16[128,1024]{1,0:T(8,128)(2,1)S(1)}, bf16[128,1024]{1,0:T(8,128)(2,1)S(1)}, u32[]{:S(2)}, u32[]{:S(2)}) %collective-permute-start.11) | collective-permute-done | bytes 262176 | tf_op jit(solution)/shard_map/ppermute | solution.py:39
  83.0 3.0 %collective-permute-start.5 = (bf16[2,128,1152]{2,1,0:T(8,128)(2,1)S(1)}, bf16[2,128,1152]{2,1,0:T(8,128)(2,1)}, u32[]{:S(2)}, u32[]{:S(2)}) collective-permute-start(bf16[2,128,1152]{2,1,0:T(8,128)(2,1)S(1)} %pad_maximum_fusion.rows_0), channel_id=1, source_target_pairs={{128,0},{192,64},{0,128},{64,192},{129,1},{193,65},{1,129},{65,193... | collective-permute-start | bytes 1769480 | tf_op jit(solution)/shard_map/ppermute | solution.py:35
  86.0 1.9 %collective-permute-done.16.refs_7_ = bf16[128,1024]{1,0:T(8,128)(2,1)S(1)} collective-permute-done((bf16[128,1024]{1,0:T(8,128)(2,1)S(1)}, bf16[128,1024]{1,0:T(8,128)(2,1)S(1)}, u32[]{:S(2)}, u32[]{:S(2)}) %collective-permute-start.16) | collective-permute-done | bytes 262176 | tf_op jit(solution)/shard_map/ppermute | solution.py:39
  90.1 4.0 %collective-permute-done.22.refs_13_ = bf16[128,1024]{1,0:T(8,128)(2,1)S(1)} collective-permute-done((bf16[128,1024]{1,0:T(8,128)(2,1)S(1)}, bf16[128,1024]{1,0:T(8,128)(2,1)S(1)}, u32[]{:S(2)}, u32[]{:S(2)}) %collective-permute-start.22) | collective-permute-done | bytes 262176 | tf_op jit(solution)/shard_map/ppermute | solution.py:39
  94.8 1.2 collective-permute-done.15.refs_6_
  97.1 3.3 %collective-permute-done.20.refs_10_ = bf16[128,1024]{1,0:T(8,128)(2,1)} collective-permute-done((bf16[128,1024]{1,0:T(8,128)(2,1)}, bf16[128,1024]{1,0:T(8,128)(2,1)}, u32[]{:S(2)}, u32[]{:S(2)}) %collective-permute-start.20) | collective-permute-done | bytes 262176 | tf_op jit(solution)/shard_map/ppermute | solution.py:39
  100.3 4.3 %collective-permute-done.24.refs_14_ = bf16[128,1024]{1,0:T(8,128)(2,1)} collective-permute-done((bf16[128,1024]{1,0:T(8,128)(2,1)}, bf16[128,1024]{1,0:T(8,128)(2,1)}, u32[]{:S(2)}, u32[]{:S(2)}) %collective-permute-start.24) | collective-permute-done | bytes 262176 | tf_op jit(solution)/shard_map/ppermute | solution.py:39
  104.6 4.5 %collective-permute-done.5.rows_2 = bf16[2,128,1152]{2,1,0:T(8,128)(2,1)} collective-permute-done((bf16[2,128,1152]{2,1,0:T(8,128)(2,1)S(1)}, bf16[2,128,1152]{2,1,0:T(8,128)(2,1)}, u32[]{:S(2)}, u32[]{:S(2)}) %collective-permute-start.5) | collective-permute-done | bytes 589856 | tf_op jit(solution)/shard_map/ppermute | solution.py:35
  109.1 0.9 copy-done.1
  110.0 0.9 copy-done.3
  111.0 0.9 copy-done.5
  112.9 0.9 copy-done.9
  114.8 20.3 %shard_map.17 = (f32[16,64,256]{2,1,0:T(8,128)}, f32[16,64,256]{2,1,0:T(8,128)}) custom-call(s32[5]{0:T(128)S(1)} %stack.32.ix, bf16[2,128,1152]{2,1,0:T(8,128)(2,1)S(1)} %pad_maximum_fusion.rows_0, bf16[2,128,1152]{2,1,0:T(8,128)(2,1)S(1)} %collective-permute-done.3.rows_1, bf16[2,128,1152]{2,1,0:T(8,128)(2,1)S(1)} %collective-permute-done.4.rows_3, ...), custom_call_target="tpu_custom_call" | custom-call | flops 8589934592 | bytes 8388608 | tf_op jit(solution)/shard_map/pallas_call | solution.py:76
  135.0 3.2 %collective-permute-start.25 = (f32[16,64,256]{2,1,0:T(8,128)}, f32[16,64,256]{2,1,0:T(8,128)S(1)}, u32[]{:S(2)}, u32[]{:S(2)}) collective-permute-start(f32[16,64,256]{2,1,0:T(8,128)} %get-tuple-element.8), channel_id=1, source_target_pairs={{0,1},{1,0},{2,3},{3,2},{4,5},{5,4},{6,7},{7,6},{8,9},{9,8},{10,11... | collective-permute-start | bytes 3145736 | tf_op jit(solution)/shard_map/ppermute | solution.py:39
  138.2 2.5 %collective-permute-done.25 = f32[16,64,256]{2,1,0:T(8,128)S(1)} collective-permute-done((f32[16,64,256]{2,1,0:T(8,128)}, f32[16,64,256]{2,1,0:T(8,128)S(1)}, u32[]{:S(2)}, u32[]{:S(2)}) %collective-permute-start.25) | collective-permute-done | bytes 1048608 | tf_op jit(solution)/shard_map/ppermute | solution.py:39
  140.7 2.4 %add_divide_fusion = f32[16,64,256]{2,1,0:T(8,128)} fusion(f32[16,64,256]{2,1,0:T(8,128)} %get-tuple-element.7, f32[16,64,256]{2,1,0:T(8,128)S(1)} %collective-permute-done.25, f32[16]{0:T(128)S(1)} %iota_subtract_fusion), kind=kLoop, calls=%fused_computation | loop fusion | flops 524288 | bytes 3145792 | tf_op jit(solution)/shard_map/div | solution.py:127
  (58 shorter events, 8.3 us)
Async XLA Ops:
  1.0 4.3 %collective-permute-start = (bf16[64,1024]{1,0:T(8,128)(2,1)S(1)}, bf16[64,1024]{1,0:T(8,128)(2,1)S(1)}, u32[]{:S(2)}, u32[]{:S(2)}) collective-permute-start(bf16[64,1024]{1,0:T(8,128)(2,1)S(1)} %get-tuple-element.16), channel_id=1, source_target_pairs={{0,1},{1,0},{2,3},{3,2},{4,5},{5,4},{6,7},{7,6},{8,9},{9,8},{10,11... | collective-permute-start | bytes 393224 | tf_op jit(solution)/shard_map/ppermute | solution.py:39
  5.4 18.6 %collective-permute-start.6 = (bf16[128,256]{1,0:T(8,128)(2,1)S(1)}, bf16[128,256]{1,0:T(8,128)(2,1)S(1)}, u32[]{:S(2)}, u32[]{:S(2)}) collective-permute-start(bf16[128,256]{1,0:T(8,128)(2,1)S(1)} %get-tuple-element.14), channel_id=1, source_target_pairs={{0,0},{1,1},{2,2},{3,3},{4,32},{5,33},{6,34},{7,35},{8,64},{9,65},... | collective-permute-start | bytes 196616 | tf_op jit(solution)/shard_map/ppermute | solution.py:108
  6.1 18.0 %collective-permute-start.7 = (bf16[128,256]{1,0:T(8,128)(2,1)S(1)}, bf16[128,256]{1,0:T(8,128)(2,1)S(1)}, u32[]{:S(2)}, u32[]{:S(2)}) collective-permute-start(bf16[128,256]{1,0:T(8,128)(2,1)S(1)} %get-tuple-element.13), channel_id=1, source_target_pairs={{0,8},{1,9},{2,10},{3,11},{4,40},{5,41},{6,42},{7,43},{8,72},{9,73... | collective-permute-start | bytes 196616 | tf_op jit(solution)/shard_map/ppermute | solution.py:108
  9.0 15.1 %collective-permute-start.8 = (bf16[128,256]{1,0:T(8,128)(2,1)S(1)}, bf16[128,256]{1,0:T(8,128)(2,1)S(1)}, u32[]{:S(2)}, u32[]{:S(2)}) collective-permute-start(bf16[128,256]{1,0:T(8,128)(2,1)S(1)} %get-tuple-element.12), channel_id=1, source_target_pairs={{0,16},{1,17},{2,18},{3,19},{4,48},{5,49},{6,50},{7,51},{8,80},{9,... | collective-permute-start | bytes 196616 | tf_op jit(solution)/shard_map/ppermute | solution.py:108
  18.6 5.5 %collective-permute-start.9 = (bf16[128,256]{1,0:T(8,128)(2,1)S(1)}, bf16[128,256]{1,0:T(8,128)(2,1)S(1)}, u32[]{:S(2)}, u32[]{:S(2)}) collective-permute-start(bf16[128,256]{1,0:T(8,128)(2,1)S(1)} %get-tuple-element.11), channel_id=1, source_target_pairs={{0,24},{1,25},{2,26},{3,27},{4,56},{5,57},{6,58},{7,59},{8,88},{9,... | collective-permute-start | bytes 196616 | tf_op jit(solution)/shard_map/ppermute | solution.py:108
  20.6 13.8 %collective-permute-start.1 = (bf16[128,128]{1,0:T(8,128)(2,1)S(1)}, bf16[128,128]{1,0:T(8,128)(2,1)S(1)}, u32[]{:S(2)}, u32[]{:S(2)}) collective-permute-start(bf16[128,128]{1,0:T(8,128)(2,1)S(1)} %slice.20), channel_id=1, source_target_pairs={{1,0},{32,1},{33,32},{64,33},{65,64},{96,65},{97,96},{128,97},{129... | collective-permute-start | bytes 98312 | tf_op jit(solution)/shard_map/ppermute | solution.py:112
  24.1 18.1 %collective-permute-start.13 = (bf16[128,1024]{1,0:T(8,128)(2,1)S(1)}, bf16[128,1024]{1,0:T(8,128)(2,1)S(1)}, u32[]{:S(2)}, u32[]{:S(2)}) collective-permute-start(bf16[128,1024]{1,0:T(8,128)(2,1)S(1)} %constant_dynamic-update-slice_fusion.refs_0_), channel_id=1, source_target_pairs={{8,0},{16,8},{24,16},{0,24},{9,1},{17,9},{25,17},{1,25},{10,2},{18... | collective-permute-start | bytes 786440 | tf_op jit(solution)/shard_map/ppermute | solution.py:35
  26.3 15.9 %collective-permute-start.17 = (bf16[128,1024]{1,0:T(8,128)(2,1)S(1)}, bf16[128,1024]{1,0:T(8,128)(2,1)S(1)}, u32[]{:S(2)}, u32[]{:S(2)}) collective-permute-start(bf16[128,1024]{1,0:T(8,128)(2,1)S(1)} %constant_dynamic-update-slice_fusion.refs_0_), channel_id=1, source_target_pairs={{24,0},{0,8},{8,16},{16,24},{25,1},{1,9},{9,17},{17,25},{26,2},{2,... | collective-permute-start | bytes 786440 | tf_op jit(solution)/shard_map/ppermute | solution.py:35
  34.5 32.4 %collective-permute-start.2 = (bf16[128,1152]{1,0:T(8,128)(2,1)S(1)}, bf16[128,1152]{1,0:T(8,128)(2,1)S(1)}, u32[]{:S(2)}, u32[]{:S(2)}) collective-permute-start(bf16[128,1152]{1,0:T(8,128)(2,1)S(1)} %get-tuple-element.10), channel_id=1, source_target_pairs={{0,32},{32,0},{1,33},{33,1},{2,34},{34,2},{3,35},{35,3},{4,36},{36... | collective-permute-start | bytes 884744 | tf_op jit(solution)/shard_map/ppermute | solution.py:39
  34.6 29.6 %collective-permute-start.21 = (bf16[128,1024]{1,0:T(8,128)(2,1)S(1)}, bf16[128,1024]{1,0:T(8,128)(2,1)S(1)}, u32[]{:S(2)}, u32[]{:S(2)}) collective-permute-start(bf16[128,1024]{1,0:T(8,128)(2,1)S(1)} %constant_dynamic-update-slice_fusion.refs_0_), channel_id=1, source_target_pairs={{16,0},{24,8},{0,16},{8,24},{17,1},{25,9},{1,17},{9,25},{18,2},{26... | collective-permute-start | bytes 786440 | tf_op jit(solution)/shard_map/ppermute | solution.py:35
  41.8 22.3 %collective-permute-start.10 = (bf16[128,1024]{1,0:T(8,128)(2,1)S(1)}, bf16[128,1024]{1,0:T(8,128)(2,1)S(1)}, u32[]{:S(2)}, u32[]{:S(2)}) collective-permute-start(bf16[128,1024]{1,0:T(8,128)(2,1)S(1)} %constant_dynamic-update-slice_fusion.refs_0_), channel_id=1, source_target_pairs={{0,2},{2,0},{4,6},{6,4},{1,3},{3,1},{5,7},{7,5},{8,10},{10,8},{12,... | collective-permute-start | bytes 786440 | tf_op jit(solution)/shard_map/ppermute | solution.py:39
  42.2 24.6 %collective-permute-start.12 = (bf16[128,1024]{1,0:T(8,128)(2,1)S(1)}, bf16[128,1024]{1,0:T(8,128)(2,1)S(1)}, u32[]{:S(2)}, u32[]{:S(2)}) collective-permute-start(bf16[128,1024]{1,0:T(8,128)(2,1)S(1)} %constant_dynamic-update-slice_fusion.refs_0_), channel_id=1, source_target_pairs={{0,6},{2,4},{4,2},{6,0},{1,7},{3,5},{5,3},{7,1},{8,14},{10,12},{12... | collective-permute-start | bytes 786440 | tf_op jit(solution)/shard_map/ppermute | solution.py:39
  42.2 27.3 %collective-permute-start.14 = (bf16[128,1024]{1,0:T(8,128)(2,1)S(1)}, bf16[128,1024]{1,0:T(8,128)(2,1)S(1)}, u32[]{:S(2)}, u32[]{:S(2)}) collective-permute-start(bf16[128,1024]{1,0:T(8,128)(2,1)S(1)} %collective-permute-done.13.refs_4_), channel_id=1, source_target_pairs={{0,2},{2,0},{4,6},{6,4},{1,3},{3,1},{5,7},{7,5},{8,10},{10,8},{12,... | collective-permute-start | bytes 786440 | tf_op jit(solution)/shard_map/ppermute | solution.py:39
  64.2 7.0 %collective-permute-start.19 = (bf16[128,1024]{1,0:T(8,128)(2,1)S(1)}, bf16[128,1024]{1,0:T(8,128)(2,1)}, u32[]{:S(2)}, u32[]{:S(2)}) collective-permute-start(bf16[128,1024]{1,0:T(8,128)(2,1)S(1)} %collective-permute-done.17.refs_8_), channel_id=1, source_target_pairs={{0,6},{2,4},{4,2},{6,0},{1,7},{3,5},{5,3},{7,1},{8,14},{10,12},{12... | collective-permute-start | bytes 786440 | tf_op jit(solution)/shard_map/ppermute | solution.py:39
  64.2 14.3 %collective-permute-start.23 = (bf16[128,1024]{1,0:T(8,128)(2,1)S(1)}, bf16[128,1024]{1,0:T(8,128)(2,1)}, u32[]{:S(2)}, u32[]{:S(2)}) collective-permute-start(bf16[128,1024]{1,0:T(8,128)(2,1)S(1)} %collective-permute-done.21.refs_12_), channel_id=1, source_target_pairs={{0,6},{2,4},{4,2},{6,0},{1,7},{3,5},{5,3},{7,1},{8,14},{10,12},{12... | collective-permute-start | bytes 786440 | tf_op jit(solution)/shard_map/ppermute | solution.py:39
  66.9 15.4 %collective-permute-start.11 = (bf16[128,1024]{1,0:T(8,128)(2,1)S(1)}, bf16[128,1024]{1,0:T(8,128)(2,1)S(1)}, u32[]{:S(2)}, u32[]{:S(2)}) collective-permute-start(bf16[128,1024]{1,0:T(8,128)(2,1)S(1)} %collective-permute-done.10.refs_1_), channel_id=1, source_target_pairs={{0,6},{2,4},{4,2},{6,0},{1,7},{3,5},{5,3},{7,1},{8,14},{10,12},{12... | collective-permute-start | bytes 786440 | tf_op jit(solution)/shard_map/ppermute | solution.py:39
  67.0 20.9 %collective-permute-start.16 = (bf16[128,1024]{1,0:T(8,128)(2,1)S(1)}, bf16[128,1024]{1,0:T(8,128)(2,1)S(1)}, u32[]{:S(2)}, u32[]{:S(2)}) collective-permute-start(bf16[128,1024]{1,0:T(8,128)(2,1)S(1)} %collective-permute-done.13.refs_4_), channel_id=1, source_target_pairs={{0,6},{2,4},{4,2},{6,0},{1,7},{3,5},{5,3},{7,1},{8,14},{10,12},{12... | collective-permute-start | bytes 786440 | tf_op jit(solution)/shard_map/ppermute | solution.py:39
  69.5 19.0 %copy-start = (bf16[128,1024]{1,0:T(8,128)(2,1)}, bf16[128,1024]{1,0:T(8,128)(2,1)S(1)}, u32[]{:S(2)}) copy-start(bf16[128,1024]{1,0:T(8,128)(2,1)S(1)} %collective-permute-done.14.refs_5_) | copy-start | bytes 786436
  69.5 19.0 %collective-permute-start.18 = (bf16[128,1024]{1,0:T(8,128)(2,1)S(1)}, bf16[128,1024]{1,0:T(8,128)(2,1)S(1)}, u32[]{:S(2)}, u32[]{:S(2)}) collective-permute-start(bf16[128,1024]{1,0:T(8,128)(2,1)S(1)} %collective-permute-done.17.refs_8_), channel_id=1, source_target_pairs={{0,2},{2,0},{4,6},{6,4},{1,3},{3,1},{5,7},{7,5},{8,10},{10,8},{12,... | collective-permute-start | bytes 786440 | tf_op jit(solution)/shard_map/ppermute | solution.py:39
  71.1 33.5 %collective-permute-start.3 = (bf16[2,128,1152]{2,1,0:T(8,128)(2,1)S(1)}, bf16[2,128,1152]{2,1,0:T(8,128)(2,1)S(1)}, u32[]{:S(2)}, u32[]{:S(2)}) collective-permute-start(bf16[2,128,1152]{2,1,0:T(8,128)(2,1)S(1)} %pad_maximum_fusion.rows_0), channel_id=1, source_target_pairs={{64,0},{128,64},{192,128},{0,192},{65,1},{129,65},{193,129},{1,193... | collective-permute-start | bytes 1769480 | tf_op jit(solution)/shard_map/ppermute | solution.py:35
  78.5 26.1 %collective-permute-start.4 = (bf16[2,128,1152]{2,1,0:T(8,128)(2,1)S(1)}, bf16[2,128,1152]{2,1,0:T(8,128)(2,1)S(1)}, u32[]{:S(2)}, u32[]{:S(2)}) collective-permute-start(bf16[2,128,1152]{2,1,0:T(8,128)(2,1)S(1)} %pad_maximum_fusion.rows_0), channel_id=1, source_target_pairs={{192,0},{0,64},{64,128},{128,192},{193,1},{1,65},{65,129},{129,193... | collective-permute-start | bytes 1769480 | tf_op jit(solution)/shard_map/ppermute | solution.py:35
  83.0 26.1 %collective-permute-start.5 = (bf16[2,128,1152]{2,1,0:T(8,128)(2,1)S(1)}, bf16[2,128,1152]{2,1,0:T(8,128)(2,1)}, u32[]{:S(2)}, u32[]{:S(2)}) collective-permute-start(bf16[2,128,1152]{2,1,0:T(8,128)(2,1)S(1)} %pad_maximum_fusion.rows_0), channel_id=1, source_target_pairs={{128,0},{192,64},{0,128},{64,192},{129,1},{193,65},{1,129},{65,193... | collective-permute-start | bytes 1769480 | tf_op jit(solution)/shard_map/ppermute | solution.py:35
  88.6 5.5 %collective-permute-start.22 = (bf16[128,1024]{1,0:T(8,128)(2,1)S(1)}, bf16[128,1024]{1,0:T(8,128)(2,1)S(1)}, u32[]{:S(2)}, u32[]{:S(2)}) collective-permute-start(bf16[128,1024]{1,0:T(8,128)(2,1)S(1)} %collective-permute-done.21.refs_12_), channel_id=1, source_target_pairs={{0,2},{2,0},{4,6},{6,4},{1,3},{3,1},{5,7},{7,5},{8,10},{10,8},{12,... | collective-permute-start | bytes 786440 | tf_op jit(solution)/shard_map/ppermute | solution.py:39
  89.3 6.7 %collective-permute-start.15 = (bf16[128,1024]{1,0:T(8,128)(2,1)S(1)}, bf16[128,1024]{1,0:T(8,128)(2,1)S(1)}, u32[]{:S(2)}, u32[]{:S(2)}) collective-permute-start(bf16[128,1024]{1,0:T(8,128)(2,1)S(1)} %collective-permute-done.14.refs_5_), channel_id=1, source_target_pairs={{0,6},{2,4},{4,2},{6,0},{1,7},{3,5},{5,3},{7,1},{8,14},{10,12},{12... | collective-permute-start | bytes 786440 | tf_op jit(solution)/shard_map/ppermute | solution.py:39
  94.8 5.5 %collective-permute-start.20 = (bf16[128,1024]{1,0:T(8,128)(2,1)}, bf16[128,1024]{1,0:T(8,128)(2,1)}, u32[]{:S(2)}, u32[]{:S(2)}) collective-permute-start(bf16[128,1024]{1,0:T(8,128)(2,1)} %collective-permute-done.19.refs_11_), channel_id=1, source_target_pairs={{0,2},{2,0},{4,6},{6,4},{1,3},{3,1},{5,7},{7,5},{8,10},{10,8},{12,... | collective-permute-start | bytes 786440 | tf_op jit(solution)/shard_map/ppermute | solution.py:39
  96.7 7.9 %collective-permute-start.24 = (bf16[128,1024]{1,0:T(8,128)(2,1)}, bf16[128,1024]{1,0:T(8,128)(2,1)}, u32[]{:S(2)}, u32[]{:S(2)}) collective-permute-start(bf16[128,1024]{1,0:T(8,128)(2,1)} %collective-permute-done.23.refs_15_), channel_id=1, source_target_pairs={{0,2},{2,0},{4,6},{6,4},{1,3},{3,1},{5,7},{7,5},{8,10},{10,8},{12,... | collective-permute-start | bytes 786440 | tf_op jit(solution)/shard_map/ppermute | solution.py:39
  109.1 1.0 copy-start.1
  110.0 0.9 copy-start.3
  111.0 0.9 copy-start.5
  111.9 0.9 copy-start.7
  112.9 0.9 copy-start.9
  135.0 5.7 %collective-permute-start.25 = (f32[16,64,256]{2,1,0:T(8,128)}, f32[16,64,256]{2,1,0:T(8,128)S(1)}, u32[]{:S(2)}, u32[]{:S(2)}) collective-permute-start(f32[16,64,256]{2,1,0:T(8,128)} %get-tuple-element.8), channel_id=1, source_target_pairs={{0,1},{1,0},{2,3},{3,2},{4,5},{5,4},{6,7},{7,6},{8,9},{9,8},{10,11... | collective-permute-start | bytes 3145736 | tf_op jit(solution)/shard_map/ppermute | solution.py:39
  (6 other events, 4.5 us)

commit v2 on v1

v2 whole, which is shorter than its diff:
```python
import jax
import jax.numpy as jnp
from jax import lax
from jax.experimental import pallas as pl
from jax.experimental.pallas import tpu as pltpu
from jax.sharding import Mesh, PartitionSpec as P

LAGS = 16
TOTAL = 16384
AXES = ("x", "zl", "zh", "y", "c")
SIZES = (4, 2, 4, 4, 2)
CH, SPAN, QUARTER, LANES = 128, 1024, 256, 128
OFFSETS = (0, 1, 3, 2)


def device_of(x, zl, zh, y, c):
    return (((x * 2 + zl) * 4 + zh) * 4 + y) * 2 + c


def scatter_pairs(quarter):
    pairs = []
    for x in range(4):
        for zl in range(2):
            for zh in range(4):
                for y in range(4):
                    to_zl = y // 2
                    to_y = y if zl == to_zl else (y + 2) % 4
                    for c in range(2):
                        target = device_of(zh, to_zl, (x + quarter) % 4, to_y, c)
                        pairs.append((device_of(x, zl, zh, y, c), target))
    return pairs


def pull(value, axis, offset, count):
    return lax.ppermute(value, axis, [((i + offset) % count, i) for i in range(count)])


def swap(value, axis, bits, count):
    return lax.ppermute(value, axis, [(i, i ^ bits) for i in range(count)])


def make_kernel(pieces, first, last):
    def kernel(ix, rows, *refs):
        refs = list(refs)
        cols = [refs.pop(0) for _ in range(2 * len(pieces))]
        before = None if first else refs.pop(0)
        outs = [refs.pop(0) for _ in range(2 if last else 1)]
        windows, earlier, later, sems = refs[:4]
        total = refs[4] if last else outs[0]
        zl, zh, y, c = (ix[i] for i in range(1, 5))
        half = lax.rem(y, 2)
        zl_own = lax.select(lax.div(y, 2) == zl, zl, 1 - zl)
        copies = []
        for i, (offset, pair) in enumerate(pieces):
            zl_slab = zl_own if pair == 0 else 1 - zl_own
            mine = []
            for q in range(4):
                slab = lax.rem(zh + offset - q + 8, 4) * 2 + zl_slab
                source = rows.at[slab, :, pl.ds(QUARTER * q, QUARTER + LANES)]
                mine.append(pltpu.make_async_copy(source, windows.at[i, q], sems.at[i, q]))
            for j, place in enumerate((half, 1 - half)):
                target = earlier.at[i, pl.ds(pl.multiple_of(place * CH, CH), CH), :]
                mine.append(pltpu.make_async_copy(cols[2 * i + j], target, sems.at[i, 4 + j]))
            for copy in mine:
                copy.start()
            copies.append(mine)
        for i in range(len(pieces)):
            for copy in copies[i]:
                copy.wait()
            for q in range(4):
                window = windows[i, q]
                for lag in range(LAGS):
                    later[lag * CH : (lag + 1) * CH, QUARTER * q : QUARTER * (q + 1)] = window[:, lag : lag + QUARTER]
            for s in range(4):
                span = slice(512 * s, 512 * (s + 1))
                part = lax.dot_general(
                    later[span, :], earlier[i], (((1,), (1,)), ((), ())), preferred_element_type=jnp.float32
                )
                if i > 0:
                    total[span, :] += part
                elif first:
                    total[span, :] = part
                else:
                    total[span, :] = before[span, :] + part
        if last:
            keep, send = outs
            for lag in range(LAGS):
                scale = jnp.float32(1.0 / (TOTAL - lag))
                keep[lag] = total[pl.ds(pl.multiple_of(lag * CH + c * 64, 64), 64), :] * scale
                send[lag] = total[pl.ds(pl.multiple_of(lag * CH + (1 - c) * 64, 64), 64), :] * scale

    return kernel


def products(ix, rows, pieces, before=None, last=False):
    vmem, anywhere = pl.BlockSpec(memory_space=pltpu.VMEM), pl.BlockSpec(memory_space=pl.ANY)
    n, first = len(pieces), before is None
    sums = jax.ShapeDtypeStruct((LAGS * CH, 256), jnp.float32)
    half = jax.ShapeDtypeStruct((LAGS, 64, 256), jnp.float32)
    scratch = [
        pltpu.VMEM((n, 4, CH, QUARTER + LANES), jnp.bfloat16),
        pltpu.VMEM((n, 256, SPAN), jnp.bfloat16),
        pltpu.VMEM((LAGS * CH, SPAN), jnp.bfloat16),
        pltpu.SemaphoreType.DMA((n, 6)),
    ]
    return pl.pallas_call(
        make_kernel([piece[:2] for piece in pieces], first, last),
        out_shape=(half, half) if last else sums,
        in_specs=[pl.BlockSpec(memory_space=pltpu.SMEM)] + [anywhere] * (1 + 2 * n) + ([] if first else [vmem]),
        out_specs=(vmem, vmem) if last else vmem,
        scratch_shapes=scratch + ([pltpu.VMEM((LAGS * CH, 256), jnp.float32)] if last else []),
        input_output_aliases={} if first or last else {2 + 2 * n: 0},
        compiler_params=pltpu.CompilerParams(vmem_limit_bytes=28 * 2**20),
        cost_estimate=pl.CostEstimate(flops=n * 2 * 2048 * 256 * 1024, bytes_accessed=n * 2**20, transcendentals=0),
    )(ix, rows, *[block for piece in pieces for block in piece[2:]], *([] if first else [before]))


def spread(one, two):
    one_1, two_1 = swap(one, "y", 1, 4), swap(two, "y", 1, 4)
    one_3, two_3 = swap(one, "y", 3, 4), swap(two, "y", 3, 4)
    one_2, two_2 = swap(one_1, "y", 3, 4), swap(two_3, "y", 1, 4)
    return [one, one_1, one_2, one_3], [two, two_1, two_2, two_3]


def on_device(strain):
    c = lax.axis_index("c")
    own = strain.T
    mine = lax.dynamic_slice(own, (0, c * SPAN), (64, SPAN))
    others = lax.dynamic_slice(own, (0, (1 - c) * SPAN), (64, SPAN))
    got = swap(others, "c", 1, 2)
    block = jnp.where(c == 0, jnp.concatenate([mine, got]), jnp.concatenate([got, mine]))

    quarters = [
        lax.ppermute(block[:, QUARTER * q : QUARTER * (q + 1)], AXES, scatter_pairs(q)) for q in range(4)
    ]
    held = jnp.concatenate(quarters, axis=1)

    head = lax.ppermute(block[:, :LANES], ("x", "zl", "c"), [(i, i - 1) for i in range(1, 16)])
    slab = jnp.concatenate([block, head], axis=1)
    rows = lax.all_to_all(
        jnp.broadcast_to(slab[None], (8, CH, SPAN + LANES)), ("x", "zl"), 0, 0, tiled=True
    )

    above, below = pull(held, "zh", 1, 4), pull(held, "zh", 3, 4)
    across = pull(held, "zh", 2, 4)
    cols_1, cols_3 = spread(above, below)
    cols_0, cols_2 = spread(held, across)

    ix = jnp.stack([lax.axis_index(name) for name in AXES]).astype(jnp.int32)
    sums = products(ix, rows, [(0, 0, *cols_0[:2]), (0, 1, *cols_0[2:])])
    sums = products(ix, rows, [(1, 0, *cols_1[:2]), (3, 0, *cols_3[:2])], sums)
    sums = products(ix, rows, [(1, 1, *cols_1[2:]), (3, 1, *cols_3[2:])], sums)
    sums = products(ix, rows, [(2, 0, *cols_2[:2])], sums)
    keep, send = products(ix, rows, [(2, 1, *cols_2[2:])], sums, last=True)
    return keep + swap(send, "c", 1, 2)


def solution(mesh):
    fine = Mesh(mesh.devices.reshape(SIZES), AXES)
    return jax.shard_map(
        on_device,
        mesh=fine,
        in_specs=(P(("x", "zl"), ("zh", "y", "c")),),
        out_specs=P(None, ("zh", "y", "c"), ("x", "zl")),
        check_vma=False,
    )
```

time: 146 us -> 127 us (0.87)
  the two profiles are of different devices: /device:TPU:1 before, /device:TPU:45 now
where the time goes in v2:
time: 127 us
  starting transfers between devices  68.3 us (54%)
  waiting for transfers between devices  27.5 us (22%)
  Pallas kernels  25.5 us (20%)
  local copies, waits for them, and re-layouts  4.5 us (4%)
    ppermute x14, starting transfers between devices, swap(): return lax.ppermute(value, axis, [(i, i ^ bits) for i in range(count)])  28.5 us
    pallas_call x5, Pallas kernels, products(): pl.pallas_call(make_kernel([piece[:2] for piece in pieces], first, last),...  25.5 us
    ppermute x4, starting transfers between devices, on_device(): lax.ppermute(block[:, QUARTER * q:QUARTER * (q + 1)], AXES, scatter_pairs...  16.3 us
    ppermute x4, waiting for transfers between devices, on_device(): lax.ppermute(block[:, QUARTER * q:QUARTER * (q + 1)], AXES, scatter_pairs...  16.1 us
    ppermute x3, starting transfers between devices, pull(): lax.ppermute(value, axis, [((i + offset) % count, i) for i in range(count)])  16 us
    all_to_all x1, starting transfers between devices, on_device(): lax.all_to_all(jnp.broadcast_to(slab[None], (8, CH, SPAN + LANES)), ('x',...  5.14 us
    ppermute x3, waiting for transfers between devices, pull(): lax.ppermute(value, axis, [((i + offset) % count, i) for i in range(count)])  4.32 us
    ppermute x1, waiting for transfers between devices, on_device(): lax.ppermute(block[:, :LANES], ('x', 'zl', 'c'), [(i, i - 1) for i in ran...  3.85 us
  transfers between devices with their start and end apart: 23, of which 6 were waited for; matrix products, arithmetic and copies ran while one was open for 0% of the time, Pallas kernels for 17%

profile of v2, /device:TPU:45, one launch (start us, length us, event | category | flops | bytes accessed | tf_op | source)
XLA Modules:
  0.0 127.2 jit_solution(13153737729843867697)
XLA Ops:
  0.0 1.0 dynamic-slice_bitcast_fusion.1
  1.0 0.8 collective-permute-start
  1.8 1.0 collective-permute-done
  2.8 2.3 %collective-permute-start.1 = (bf16[128,128]{1,0:T(8,128)(2,1)S(1)}, bf16[128,128]{1,0:T(8,128)(2,1)S(1)}, u32[]{:S(2)}, u32[]{:S(2)}) collective-permute-start(bf16[128,128]{1,0:T(8,128)(2,1)S(1)} %slice.20), channel_id=1, source_target_pairs={{1,0},{32,1},{33,32},{64,33},{65,64},{96,65},{97,96},{128,97},{129... | collective-permute-start | bytes 98312 | tf_op jit(solution)/shard_map/ppermute | solution.py:138
  5.1 3.9 %collective-permute-done.1 = bf16[128,128]{1,0:T(8,128)(2,1)S(1)} collective-permute-done((bf16[128,128]{1,0:T(8,128)(2,1)S(1)}, bf16[128,128]{1,0:T(8,128)(2,1)S(1)}, u32[]{:S(2)}, u32[]{:S(2)}) %collective-permute-start.1) | collective-permute-done | bytes 32800 | tf_op jit(solution)/shard_map/ppermute | solution.py:138
  9.0 1.7 %broadcast_in_dim.2 = bf16[8,128,1152]{2,1,0:T(8,128)(2,1)} broadcast(bf16[128,1152]{1,0:T(8,128)(2,1)S(1)} %pad_maximum_fusion), dimensions={1,2} | broadcast | bytes 2654208 | tf_op jit(solution)/shard_map/broadcast_in_dim | solution.py:141
  10.7 5.1 %all-to-all-start = ((bf16[8,128,1152]{2,1,0:T(8,128)(2,1)}), bf16[8,128,1152]{2,1,0:T(8,128)(2,1)S(1)}, u32[]{:S(2)}, u32[]{:S(2)}) async-start(bf16[8,128,1152]{2,1,0:T(8,128)(2,1)} %broadcast_in_dim.2), calls=%async_computation | async-start | bytes 4718592 | tf_op jit(solution)/shard_map/all_to_all | solution.py:140
  15.9 8.5 %collective-permute-start.2 = (bf16[128,256]{1,0:T(8,128)(2,1)S(1)}, bf16[128,256]{1,0:T(8,128)(2,1)S(1)}, u32[]{:S(2)}, u32[]{:S(2)}) collective-permute-start(bf16[128,256]{1,0:T(8,128)(2,1)S(1)} %get-tuple-element.12), channel_id=1, source_target_pairs={{0,0},{1,1},{2,2},{3,3},{4,32},{5,33},{6,34},{7,35},{8,64},{9,65},... | collective-permute-start | bytes 196616 | tf_op jit(solution)/shard_map/ppermute | solution.py:134
  24.3 2.5 %collective-permute-start.3 = (bf16[128,256]{1,0:T(8,128)(2,1)S(1)}, bf16[128,256]{1,0:T(8,128)(2,1)S(1)}, u32[]{:S(2)}, u32[]{:S(2)}) collective-permute-start(bf16[128,256]{1,0:T(8,128)(2,1)S(1)} %get-tuple-element.11), channel_id=1, source_target_pairs={{0,8},{1,9},{2,10},{3,11},{4,40},{5,41},{6,42},{7,43},{8,72},{9,73... | collective-permute-start | bytes 196616 | tf_op jit(solution)/shard_map/ppermute | solution.py:134
  26.9 5.4 %collective-permute-start.5 = (bf16[128,256]{1,0:T(8,128)(2,1)S(1)}, bf16[128,256]{1,0:T(8,128)(2,1)S(1)}, u32[]{:S(2)}, u32[]{:S(2)}) collective-permute-start(bf16[128,256]{1,0:T(8,128)(2,1)S(1)} %get-tuple-element.9), channel_id=1, source_target_pairs={{0,24},{1,25},{2,26},{3,27},{4,56},{5,57},{6,58},{7,59},{8,88},{9,... | collective-permute-start | bytes 196616 | tf_op jit(solution)/shard_map/ppermute | solution.py:134
  32.2 14.8 %collective-permute-done.3 = bf16[128,256]{1,0:T(8,128)(2,1)S(1)} collective-permute-done((bf16[128,256]{1,0:T(8,128)(2,1)S(1)}, bf16[128,256]{1,0:T(8,128)(2,1)S(1)}, u32[]{:S(2)}, u32[]{:S(2)}) %collective-permute-start.3) | collective-permute-done | bytes 65568 | tf_op jit(solution)/shard_map/ppermute | solution.py:134
  47.0 1.3 %collective-permute-done.4 = bf16[128,256]{1,0:T(8,128)(2,1)S(1)} collective-permute-done((bf16[128,256]{1,0:T(8,128)(2,1)S(1)}, bf16[128,256]{1,0:T(8,128)(2,1)S(1)}, u32[]{:S(2)}, u32[]{:S(2)}) %collective-permute-start.4) | collective-permute-done | bytes 65568 | tf_op jit(solution)/shard_map/ppermute | solution.py:134
  48.3 0.3 collective-permute-start.18
  48.6 9.9 %collective-permute-start.10 = (bf16[128,1024]{1,0:T(8,128)(2,1)S(1)}, bf16[128,1024]{1,0:T(8,128)(2,1)S(1)}, u32[]{:S(2)}, u32[]{:S(2)}) collective-permute-start(bf16[128,1024]{1,0:T(8,128)(2,1)S(1)} %constant_dynamic-update-slice_fusion.refs_0_), channel_id=1, source_target_pairs={{8,0},{16,8},{24,16},{0,24},{9,1},{17,9},{25,17},{1,25},{10,2},{18... | collective-permute-start | bytes 786440 | tf_op jit(solution)/shard_map/ppermute | solution.py:35
  58.5 6.1 %collective-permute-start.6 = (bf16[128,1024]{1,0:T(8,128)(2,1)S(1)}, bf16[128,1024]{1,0:T(8,128)(2,1)S(1)}, u32[]{:S(2)}, u32[]{:S(2)}) collective-permute-start(bf16[128,1024]{1,0:T(8,128)(2,1)S(1)} %constant_dynamic-update-slice_fusion.refs_0_), channel_id=1, source_target_pairs={{16,0},{24,8},{0,16},{8,24},{17,1},{25,9},{1,17},{9,25},{18,2},{26... | collective-permute-start | bytes 786440 | tf_op jit(solution)/shard_map/ppermute | solution.py:35
  64.5 1.5 %collective-permute-start.19 = (bf16[128,1024]{1,0:T(8,128)(2,1)}, bf16[128,1024]{1,0:T(8,128)(2,1)}, u32[]{:S(2)}, u32[]{:S(2)}) collective-permute-start(bf16[128,1024]{1,0:T(8,128)(2,1)} %collective-permute-done.18.refs_1_), channel_id=1, source_target_pairs={{0,6},{2,4},{4,2},{6,0},{1,7},{3,5},{5,3},{7,1},{8,14},{10,12},{12... | collective-permute-start | bytes 786440 | tf_op jit(solution)/shard_map/ppermute | solution.py:39
  66.0 4.3 %collective-permute-done.10.refs_0_ = bf16[128,1024]{1,0:T(8,128)(2,1)S(1)} collective-permute-done((bf16[128,1024]{1,0:T(8,128)(2,1)S(1)}, bf16[128,1024]{1,0:T(8,128)(2,1)S(1)}, u32[]{:S(2)}, u32[]{:S(2)}) %collective-permute-start.10) | collective-permute-done | bytes 262176 | tf_op jit(solution)/shard_map/ppermute | solution.py:35
  70.4 0.7 copy-done
  71.1 13.3 %collective-permute-start.17 = (bf16[128,1024]{1,0:T(8,128)(2,1)}, bf16[128,1024]{1,0:T(8,128)(2,1)}, u32[]{:S(2)}, u32[]{:S(2)}) collective-permute-start(bf16[128,1024]{1,0:T(8,128)(2,1)} %collective-permute-done.14.refs_2_), channel_id=1, source_target_pairs={{0,2},{2,0},{4,6},{6,4},{1,3},{3,1},{5,7},{7,5},{8,10},{10,8},{12,... | collective-permute-start | bytes 786440 | tf_op jit(solution)/shard_map/ppermute | solution.py:39
  84.4 2.1 %collective-permute-start.7 = (bf16[128,1024]{1,0:T(8,128)(2,1)S(1)}, bf16[128,1024]{1,0:T(8,128)(2,1)S(1)}, u32[]{:S(2)}, u32[]{:S(2)}) collective-permute-start(bf16[128,1024]{1,0:T(8,128)(2,1)S(1)} %collective-permute-done.6.refs_0_), channel_id=1, source_target_pairs={{0,6},{2,4},{4,2},{6,0},{1,7},{3,5},{5,3},{7,1},{8,14},{10,12},{12... | collective-permute-start | bytes 786440 | tf_op jit(solution)/shard_map/ppermute | solution.py:39
  86.6 1.4 %collective-permute-start.12 = (bf16[128,1024]{1,0:T(8,128)(2,1)}, bf16[128,1024]{1,0:T(8,128)(2,1)}, u32[]{:S(2)}, u32[]{:S(2)}) collective-permute-start(bf16[128,1024]{1,0:T(8,128)(2,1)} %collective-permute-done.11.refs_1_), channel_id=1, source_target_pairs={{0,6},{2,4},{4,2},{6,0},{1,7},{3,5},{5,3},{7,1},{8,14},{10,12},{12... | collective-permute-start | bytes 786440 | tf_op jit(solution)/shard_map/ppermute | solution.py:39
  88.0 4.7 %collective-permute-start.16 = (bf16[128,1024]{1,0:T(8,128)(2,1)}, bf16[128,1024]{1,0:T(8,128)(2,1)}, u32[]{:S(2)}, u32[]{:S(2)}) collective-permute-start(bf16[128,1024]{1,0:T(8,128)(2,1)} %collective-permute-done.15.refs_3_), channel_id=1, source_target_pairs={{0,2},{2,0},{4,6},{6,4},{1,3},{3,1},{5,7},{7,5},{8,10},{10,8},{12,... | collective-permute-start | bytes 786440 | tf_op jit(solution)/shard_map/ppermute | solution.py:39
  92.7 0.9 copy-done.1
  93.6 6.1 %shard_map.17.refs_4_ = f32[2048,256]{1,0:T(8,128)S(1)} custom-call(s32[5]{0:T(128)S(1)} %stack.23.ix, bf16[8,128,1152]{2,1,0:T(8,128)(2,1)S(1)} %all-to-all-done.rows, bf16[128,1024]{1,0:T(8,128)(2,1)S(1)} %constant_dynamic-update-slice_fusion.refs_0_, bf16[128,1024]{1,0:T(8,128)(2,1)} %collective-permute-done.18.refs_1_, ...), custom_call_target="tpu_custom_call" | custom-call | flops 2147483648 | bytes 2097152 | tf_op jit(solution)/shard_map/pallas_call | solution.py:106
  99.9 1.4 %collective-permute-start.8 = (bf16[128,1024]{1,0:T(8,128)(2,1)S(1)}, bf16[128,1024]{1,0:T(8,128)(2,1)S(1)}, u32[]{:S(2)}, u32[]{:S(2)}) collective-permute-start(bf16[128,1024]{1,0:T(8,128)(2,1)S(1)} %collective-permute-done.7.refs_1_), channel_id=1, source_target_pairs={{0,2},{2,0},{4,6},{6,4},{1,3},{3,1},{5,7},{7,5},{8,10},{10,8},{12,... | collective-permute-start | bytes 786440 | tf_op jit(solution)/shard_map/ppermute | solution.py:39
  101.3 6.4 %shard_map.18.refs_4_ = f32[2048,256]{1,0:T(8,128)S(1)} custom-call(s32[5]{0:T(128)S(1)} %stack.23.ix, bf16[8,128,1152]{2,1,0:T(8,128)(2,1)S(1)} %all-to-all-done.rows, bf16[128,1024]{1,0:T(8,128)(2,1)S(1)} %collective-permute-done.10.refs_0_, bf16[128,1024]{1,0:T(8,128)(2,1)} %collective-permute-done.11.refs_1_, ...), custom_call_target="tpu_custom_call", output_to_operand_aliasing={{}: (6, {})} | custom-call | flops 2147483648 | bytes 2097152 | tf_op jit(solution)/shard_map/pallas_call | solution.py:106
  107.8 6.5 %shard_map.19.refs_2_ = f32[2048,256]{1,0:T(8,128)S(1)} custom-call(s32[5]{0:T(128)S(1)} %stack.23.ix, bf16[8,128,1152]{2,1,0:T(8,128)(2,1)S(1)} %all-to-all-done.rows, bf16[128,1024]{1,0:T(8,128)(2,1)} %collective-permute-done.12.refs_0_, bf16[128,1024]{1,0:T(8,128)(2,1)} %collective-permute-done.13.refs_1_, ...), custom_call_target="tpu_custom_call", output_to_operand_aliasing={{}: (6, {})} | custom-call | flops 2147483648 | bytes 2097152 | tf_op jit(solution)/shard_map/pallas_call | solution.py:106
  114.3 3.1 %shard_map.20.refs_2_ = f32[2048,256]{1,0:T(8,128)S(1)} custom-call(s32[5]{0:T(128)S(1)} %stack.23.ix, bf16[8,128,1152]{2,1,0:T(8,128)(2,1)S(1)} %all-to-all-done.rows, bf16[128,1024]{1,0:T(8,128)(2,1)S(1)} %collective-permute-done.6.refs_0_, bf16[128,1024]{1,0:T(8,128)(2,1)S(1)} %collective-permute-done.9.refs_1_, ...), custom_call_target="tpu_custom_call", output_to_operand_aliasing={{}: (4, {})} | custom-call | flops 1073741824 | bytes 1048576 | tf_op jit(solution)/shard_map/pallas_call | solution.py:106
  117.4 3.4 %shard_map.21 = (f32[16,64,256]{2,1,0:T(8,128)S(1)}, f32[16,64,256]{2,1,0:T(8,128)S(1)}) custom-call(s32[5]{0:T(128)S(1)} %stack.23.ix, bf16[8,128,1152]{2,1,0:T(8,128)(2,1)S(1)} %all-to-all-done.rows, bf16[128,1024]{1,0:T(8,128)(2,1)S(1)} %collective-permute-done.8.refs_0_, bf16[128,1024]{1,0:T(8,128)(2,1)S(1)} %collective-permute-done.7.refs_1_, ...), custom_call_target="tpu_custom_call" | custom-call | flops 1073741824 | bytes 1048576 | tf_op jit(solution)/shard_map/pallas_call | solution.py:106
  120.8 3.0 %collective-permute-start.21 = (f32[16,64,256]{2,1,0:T(8,128)S(1)}, f32[16,64,256]{2,1,0:T(8,128)S(1)}, u32[]{:S(2)}, u32[]{:S(2)}) collective-permute-start(f32[16,64,256]{2,1,0:T(8,128)S(1)} %get-tuple-element.8), channel_id=1, source_target_pairs={{0,1},{1,0},{2,3},{3,2},{4,5},{5,4},{6,7},{7,6},{8,9},{9,8},{10,11... | collective-permute-start | bytes 3145736 | tf_op jit(solution)/shard_map/ppermute | solution.py:39
  123.8 2.3 %collective-permute-done.21 = f32[16,64,256]{2,1,0:T(8,128)S(1)} collective-permute-done((f32[16,64,256]{2,1,0:T(8,128)S(1)}, f32[16,64,256]{2,1,0:T(8,128)S(1)}, u32[]{:S(2)}, u32[]{:S(2)}) %collective-permute-start.21) | collective-permute-done | bytes 1048608 | tf_op jit(solution)/shard_map/ppermute | solution.py:39
  126.0 1.1 add.11
  (35 shorter events, 0.4 us)
Async XLA Ops:
  1.0 1.7 %collective-permute-start = (bf16[64,1024]{1,0:T(8,128)(2,1)S(1)}, bf16[64,1024]{1,0:T(8,128)(2,1)S(1)}, u32[]{:S(2)}, u32[]{:S(2)}) collective-permute-start(bf16[64,1024]{1,0:T(8,128)(2,1)S(1)} %get-tuple-element.14), channel_id=1, source_target_pairs={{0,1},{1,0},{2,3},{3,2},{4,5},{5,4},{6,7},{7,6},{8,9},{9,8},{10,11... | collective-permute-start | bytes 393224 | tf_op jit(solution)/shard_map/ppermute | solution.py:39
  2.8 6.1 %collective-permute-start.1 = (bf16[128,128]{1,0:T(8,128)(2,1)S(1)}, bf16[128,128]{1,0:T(8,128)(2,1)S(1)}, u32[]{:S(2)}, u32[]{:S(2)}) collective-permute-start(bf16[128,128]{1,0:T(8,128)(2,1)S(1)} %slice.20), channel_id=1, source_target_pairs={{1,0},{32,1},{33,32},{64,33},{65,64},{96,65},{97,96},{128,97},{129... | collective-permute-start | bytes 98312 | tf_op jit(solution)/shard_map/ppermute | solution.py:138
  10.7 82.0 %all-to-all-start = ((bf16[8,128,1152]{2,1,0:T(8,128)(2,1)}), bf16[8,128,1152]{2,1,0:T(8,128)(2,1)S(1)}, u32[]{:S(2)}, u32[]{:S(2)}) async-start(bf16[8,128,1152]{2,1,0:T(8,128)(2,1)} %broadcast_in_dim.2), calls=%async_computation | async-start | bytes 4718592 | tf_op jit(solution)/shard_map/all_to_all | solution.py:140
  15.9 16.4 %collective-permute-start.2 = (bf16[128,256]{1,0:T(8,128)(2,1)S(1)}, bf16[128,256]{1,0:T(8,128)(2,1)S(1)}, u32[]{:S(2)}, u32[]{:S(2)}) collective-permute-start(bf16[128,256]{1,0:T(8,128)(2,1)S(1)} %get-tuple-element.12), channel_id=1, source_target_pairs={{0,0},{1,1},{2,2},{3,3},{4,32},{5,33},{6,34},{7,35},{8,64},{9,65},... | collective-permute-start | bytes 196616 | tf_op jit(solution)/shard_map/ppermute | solution.py:134
  24.3 22.7 %collective-permute-start.3 = (bf16[128,256]{1,0:T(8,128)(2,1)S(1)}, bf16[128,256]{1,0:T(8,128)(2,1)S(1)}, u32[]{:S(2)}, u32[]{:S(2)}) collective-permute-start(bf16[128,256]{1,0:T(8,128)(2,1)S(1)} %get-tuple-element.11), channel_id=1, source_target_pairs={{0,8},{1,9},{2,10},{3,11},{4,40},{5,41},{6,42},{7,43},{8,72},{9,73... | collective-permute-start | bytes 196616 | tf_op jit(solution)/shard_map/ppermute | solution.py:134
  26.9 21.4 %collective-permute-start.4 = (bf16[128,256]{1,0:T(8,128)(2,1)S(1)}, bf16[128,256]{1,0:T(8,128)(2,1)S(1)}, u32[]{:S(2)}, u32[]{:S(2)}) collective-permute-start(bf16[128,256]{1,0:T(8,128)(2,1)S(1)} %get-tuple-element.10), channel_id=1, source_target_pairs={{0,16},{1,17},{2,18},{3,19},{4,48},{5,49},{6,50},{7,51},{8,80},{9,... | collective-permute-start | bytes 196616 | tf_op jit(solution)/shard_map/ppermute | solution.py:134
  26.9 21.4 %collective-permute-start.5 = (bf16[128,256]{1,0:T(8,128)(2,1)S(1)}, bf16[128,256]{1,0:T(8,128)(2,1)S(1)}, u32[]{:S(2)}, u32[]{:S(2)}) collective-permute-start(bf16[128,256]{1,0:T(8,128)(2,1)S(1)} %get-tuple-element.9), channel_id=1, source_target_pairs={{0,24},{1,25},{2,26},{3,27},{4,56},{5,57},{6,58},{7,59},{8,88},{9,... | collective-permute-start | bytes 196616 | tf_op jit(solution)/shard_map/ppermute | solution.py:134
  48.3 16.2 %collective-permute-start.18 = (bf16[128,1024]{1,0:T(8,128)(2,1)S(1)}, bf16[128,1024]{1,0:T(8,128)(2,1)}, u32[]{:S(2)}, u32[]{:S(2)}) collective-permute-start(bf16[128,1024]{1,0:T(8,128)(2,1)S(1)} %constant_dynamic-update-slice_fusion.refs_0_), channel_id=1, source_target_pairs={{0,2},{2,0},{4,6},{6,4},{1,3},{3,1},{5,7},{7,5},{8,10},{10,8},{12,... | collective-permute-start | bytes 786440 | tf_op jit(solution)/shard_map/ppermute | solution.py:39
  48.6 21.8 %collective-permute-start.10 = (bf16[128,1024]{1,0:T(8,128)(2,1)S(1)}, bf16[128,1024]{1,0:T(8,128)(2,1)S(1)}, u32[]{:S(2)}, u32[]{:S(2)}) collective-permute-start(bf16[128,1024]{1,0:T(8,128)(2,1)S(1)} %constant_dynamic-update-slice_fusion.refs_0_), channel_id=1, source_target_pairs={{8,0},{16,8},{24,16},{0,24},{9,1},{17,9},{25,17},{1,25},{10,2},{18... | collective-permute-start | bytes 786440 | tf_op jit(solution)/shard_map/ppermute | solution.py:35
  58.5 11.9 %collective-permute-start.14 = (bf16[128,1024]{1,0:T(8,128)(2,1)S(1)}, bf16[128,1024]{1,0:T(8,128)(2,1)}, u32[]{:S(2)}, u32[]{:S(2)}) collective-permute-start(bf16[128,1024]{1,0:T(8,128)(2,1)S(1)} %constant_dynamic-update-slice_fusion.refs_0_), channel_id=1, source_target_pairs={{24,0},{0,8},{8,16},{16,24},{25,1},{1,9},{9,17},{17,25},{26,2},{2,... | collective-permute-start | bytes 786440 | tf_op jit(solution)/shard_map/ppermute | solution.py:35
  58.5 11.9 %collective-permute-start.20 = (bf16[128,1024]{1,0:T(8,128)(2,1)S(1)}, bf16[128,1024]{1,0:T(8,128)(2,1)S(1)}, u32[]{:S(2)}, u32[]{:S(2)}) collective-permute-start(bf16[128,1024]{1,0:T(8,128)(2,1)S(1)} %constant_dynamic-update-slice_fusion.refs_0_), channel_id=1, source_target_pairs={{0,6},{2,4},{4,2},{6,0},{1,7},{3,5},{5,3},{7,1},{8,14},{10,12},{12... | collective-permute-start | bytes 786440 | tf_op jit(solution)/shard_map/ppermute | solution.py:39
  58.5 25.9 %collective-permute-start.6 = (bf16[128,1024]{1,0:T(8,128)(2,1)S(1)}, bf16[128,1024]{1,0:T(8,128)(2,1)S(1)}, u32[]{:S(2)}, u32[]{:S(2)}) collective-permute-start(bf16[128,1024]{1,0:T(8,128)(2,1)S(1)} %constant_dynamic-update-slice_fusion.refs_0_), channel_id=1, source_target_pairs={{16,0},{24,8},{0,16},{8,24},{17,1},{25,9},{1,17},{9,25},{18,2},{26... | collective-permute-start | bytes 786440 | tf_op jit(solution)/shard_map/ppermute | solution.py:35
  64.5 22.0 %collective-permute-start.19 = (bf16[128,1024]{1,0:T(8,128)(2,1)}, bf16[128,1024]{1,0:T(8,128)(2,1)}, u32[]{:S(2)}, u32[]{:S(2)}) collective-permute-start(bf16[128,1024]{1,0:T(8,128)(2,1)} %collective-permute-done.18.refs_1_), channel_id=1, source_target_pairs={{0,6},{2,4},{4,2},{6,0},{1,7},{3,5},{5,3},{7,1},{8,14},{10,12},{12... | collective-permute-start | bytes 786440 | tf_op jit(solution)/shard_map/ppermute | solution.py:39
  70.3 16.2 %collective-permute-start.11 = (bf16[128,1024]{1,0:T(8,128)(2,1)S(1)}, bf16[128,1024]{1,0:T(8,128)(2,1)}, u32[]{:S(2)}, u32[]{:S(2)}) collective-permute-start(bf16[128,1024]{1,0:T(8,128)(2,1)S(1)} %collective-permute-done.10.refs_0_), channel_id=1, source_target_pairs={{0,2},{2,0},{4,6},{6,4},{1,3},{3,1},{5,7},{7,5},{8,10},{10,8},{12,... | collective-permute-start | bytes 786440 | tf_op jit(solution)/shard_map/ppermute | solution.py:39
  70.3 17.7 %collective-permute-start.15 = (bf16[128,1024]{1,0:T(8,128)(2,1)}, bf16[128,1024]{1,0:T(8,128)(2,1)}, u32[]{:S(2)}, u32[]{:S(2)}) collective-permute-start(bf16[128,1024]{1,0:T(8,128)(2,1)} %collective-permute-done.14.refs_2_), channel_id=1, source_target_pairs={{0,6},{2,4},{4,2},{6,0},{1,7},{3,5},{5,3},{7,1},{8,14},{10,12},{12... | collective-permute-start | bytes 786440 | tf_op jit(solution)/shard_map/ppermute | solution.py:39
  70.4 0.7 copy-start
  71.1 28.7 %collective-permute-start.17 = (bf16[128,1024]{1,0:T(8,128)(2,1)}, bf16[128,1024]{1,0:T(8,128)(2,1)}, u32[]{:S(2)}, u32[]{:S(2)}) collective-permute-start(bf16[128,1024]{1,0:T(8,128)(2,1)} %collective-permute-done.14.refs_2_), channel_id=1, source_target_pairs={{0,2},{2,0},{4,6},{6,4},{1,3},{3,1},{5,7},{7,5},{8,10},{10,8},{12,... | collective-permute-start | bytes 786440 | tf_op jit(solution)/shard_map/ppermute | solution.py:39
  84.4 15.5 %collective-permute-start.7 = (bf16[128,1024]{1,0:T(8,128)(2,1)S(1)}, bf16[128,1024]{1,0:T(8,128)(2,1)S(1)}, u32[]{:S(2)}, u32[]{:S(2)}) collective-permute-start(bf16[128,1024]{1,0:T(8,128)(2,1)S(1)} %collective-permute-done.6.refs_0_), channel_id=1, source_target_pairs={{0,6},{2,4},{4,2},{6,0},{1,7},{3,5},{5,3},{7,1},{8,14},{10,12},{12... | collective-permute-start | bytes 786440 | tf_op jit(solution)/shard_map/ppermute | solution.py:39
  86.5 21.2 %collective-permute-start.13 = (bf16[128,1024]{1,0:T(8,128)(2,1)S(1)}, bf16[128,1024]{1,0:T(8,128)(2,1)}, u32[]{:S(2)}, u32[]{:S(2)}) collective-permute-start(bf16[128,1024]{1,0:T(8,128)(2,1)S(1)} %collective-permute-done.10.refs_0_), channel_id=1, source_target_pairs={{0,6},{2,4},{4,2},{6,0},{1,7},{3,5},{5,3},{7,1},{8,14},{10,12},{12... | collective-permute-start | bytes 786440 | tf_op jit(solution)/shard_map/ppermute | solution.py:39
  86.6 21.2 %collective-permute-start.12 = (bf16[128,1024]{1,0:T(8,128)(2,1)}, bf16[128,1024]{1,0:T(8,128)(2,1)}, u32[]{:S(2)}, u32[]{:S(2)}) collective-permute-start(bf16[128,1024]{1,0:T(8,128)(2,1)} %collective-permute-done.11.refs_1_), channel_id=1, source_target_pairs={{0,6},{2,4},{4,2},{6,0},{1,7},{3,5},{5,3},{7,1},{8,14},{10,12},{12... | collective-permute-start | bytes 786440 | tf_op jit(solution)/shard_map/ppermute | solution.py:39
  88.0 19.7 %collective-permute-start.16 = (bf16[128,1024]{1,0:T(8,128)(2,1)}, bf16[128,1024]{1,0:T(8,128)(2,1)}, u32[]{:S(2)}, u32[]{:S(2)}) collective-permute-start(bf16[128,1024]{1,0:T(8,128)(2,1)} %collective-permute-done.15.refs_3_), channel_id=1, source_target_pairs={{0,2},{2,0},{4,6},{6,4},{1,3},{3,1},{5,7},{7,5},{8,10},{10,8},{12,... | collective-permute-start | bytes 786440 | tf_op jit(solution)/shard_map/ppermute | solution.py:39
  92.7 1.0 copy-start.1
  99.8 14.5 %collective-permute-start.9 = (bf16[128,1024]{1,0:T(8,128)(2,1)S(1)}, bf16[128,1024]{1,0:T(8,128)(2,1)S(1)}, u32[]{:S(2)}, u32[]{:S(2)}) collective-permute-start(bf16[128,1024]{1,0:T(8,128)(2,1)S(1)} %collective-permute-done.6.refs_0_), channel_id=1, source_target_pairs={{0,2},{2,0},{4,6},{6,4},{1,3},{3,1},{5,7},{7,5},{8,10},{10,8},{12,... | collective-permute-start | bytes 786440 | tf_op jit(solution)/shard_map/ppermute | solution.py:39
  99.9 17.5 %collective-permute-start.8 = (bf16[128,1024]{1,0:T(8,128)(2,1)S(1)}, bf16[128,1024]{1,0:T(8,128)(2,1)S(1)}, u32[]{:S(2)}, u32[]{:S(2)}) collective-permute-start(bf16[128,1024]{1,0:T(8,128)(2,1)S(1)} %collective-permute-done.7.refs_1_), channel_id=1, source_target_pairs={{0,2},{2,0},{4,6},{6,4},{1,3},{3,1},{5,7},{7,5},{8,10},{10,8},{12,... | collective-permute-start | bytes 786440 | tf_op jit(solution)/shard_map/ppermute | solution.py:39
  120.8 5.3 %collective-permute-start.21 = (f32[16,64,256]{2,1,0:T(8,128)S(1)}, f32[16,64,256]{2,1,0:T(8,128)S(1)}, u32[]{:S(2)}, u32[]{:S(2)}) collective-permute-start(f32[16,64,256]{2,1,0:T(8,128)S(1)} %get-tuple-element.8), channel_id=1, source_target_pairs={{0,1},{1,0},{2,3},{3,2},{4,5},{5,4},{6,7},{7,6},{8,9},{9,8},{10,11... | collective-permute-start | bytes 3145736 | tf_op jit(solution)/shard_map/ppermute | solution.py:39

commit v3 on v2

v3 whole, which is shorter than its diff:
```python
import jax
import jax.numpy as jnp
from jax import lax
from jax.experimental import pallas as pl
from jax.experimental.pallas import tpu as pltpu
from jax.sharding import Mesh, PartitionSpec as P

LAGS = 16
TOTAL = 16384
AXES = ("x", "zl", "zh", "y", "c")
SIZES = (4, 2, 4, 4, 2)
CH, SPAN, QUARTER, LANES = 128, 1024, 256, 128
OFFSETS = (0, 1, 3, 2)
ROWS_AT = (0, 1, 3, 2)
VLIM = 28


def device_of(x, zl, zh, y, c):
    return (((x * 2 + zl) * 4 + zh) * 4 + y) * 2 + c


def scatter_pairs(quarter):
    pairs = []
    for x in range(4):
        for zl in range(2):
            for zh in range(4):
                for y in range(4):
                    to_zl = y // 2
                    to_y = y if zl == to_zl else (y + 2) % 4
                    for c in range(2):
                        target = device_of(zh, to_zl, (x + quarter) % 4, to_y, c)
                        pairs.append((device_of(x, zl, zh, y, c), target))
    return pairs


def pull(value, axis, offset, count):
    return lax.ppermute(value, axis, [((i + offset) % count, i) for i in range(count)])


def swap(value, axis, bits, count):
    return lax.ppermute(value, axis, [(i, i ^ bits) for i in range(count)])


def make_kernel(pieces, n_arrays, first, last):
    n = len(pieces)

    def kernel(ix, *refs):
        refs = list(refs)
        rows = [refs.pop(0) for _ in OFFSETS]
        arrays = [refs.pop(0) for _ in range(n_arrays)]
        before = None if first else refs.pop(0)
        outs = [refs.pop(0) for _ in range(2 if last else 1)]
        windows, earlier, sems = refs[:3]
        total = refs[3] if last else outs[0]
        x, zl, zh, y, c = (ix[i] for i in range(5))
        half = lax.rem(y, 2)
        away_zl = lax.select(lax.div(y, 2) == zl, 0, 1)
        copies = []
        for i, (offset, pair, blocks) in enumerate(pieces):
            m = away_zl if pair == 0 else 1 - away_zl
            mine = []
            for q in range(4):
                away = lax.rem(zh + offset - q - x + 8, 4)
                for at, slabs in zip(ROWS_AT, rows):
                    source = slabs.at[m, :, pl.ds(QUARTER * q, QUARTER + LANES)]
                    copy = pltpu.make_async_copy(source, windows.at[i, q], sems.at[i, q])
                    pl.when(away == at)(copy.start)
                mine.append(copy)
            for j, (parts, place) in enumerate(zip(blocks, (half, 1 - half))):
                size = CH // len(parts)
                for s, (number, index) in enumerate(parts):
                    start = pl.multiple_of(place * CH + s * size, size)
                    source = arrays[number] if index is None else arrays[number].at[index]
                    copy = pltpu.make_async_copy(source, earlier.at[i, pl.ds(start, size), :], sems.at[i, 4 + 2 * j + s])
                    copy.start()
                    mine.append(copy)
            copies.append(mine)
        for i in range(n):
            for copy in copies[i]:
                copy.wait()
            wide = [windows[i, q] for q in range(4)]
            for s in range(4):
                span = slice(512 * s, 512 * (s + 1))
                later = jnp.concatenate(
                    [
                        jnp.concatenate([window[:, lag : lag + QUARTER] for window in wide], axis=1)
                        for lag in range(4 * s, 4 * s + 4)
                    ],
                    axis=0,
                )
                part = lax.dot_general(
                    later, earlier[i], (((1,), (1,)), ((), ())), preferred_element_type=jnp.float32
                )
                if i > 0:
                    total[span, :] += part
                elif first:
                    total[span, :] = part
                else:
                    total[span, :] = before[span, :] + part
        if last:
            keep, send = outs
            for lag in range(LAGS):
                scale = jnp.float32(1.0 / (TOTAL - lag))
                keep[lag] = total[pl.ds(pl.multiple_of(lag * CH + c * 64, 64), 64), :] * scale
                send[lag] = total[pl.ds(pl.multiple_of(lag * CH + (1 - c) * 64, 64), 64), :] * scale

    return kernel


def products(ix, rows, pieces, before=None, last=False):
    vmem, anywhere = pl.BlockSpec(memory_space=pltpu.VMEM), pl.BlockSpec(memory_space=pltpu.HBM)
    n, first = len(pieces), before is None
    arrays, plan = [], []
    for offset, pair, *blocks in pieces:
        numbered = []
        for parts in blocks:
            numbers = []
            for array, index in parts:
                known = [i for i, other in enumerate(arrays) if other is array]
                if not known:
                    arrays.append(array)
                numbers.append(((known or [len(arrays) - 1])[0], index))
            numbered.append(numbers)
        plan.append((offset, pair, numbered))
    sums = jax.ShapeDtypeStruct((LAGS * CH, 256), jnp.float32)
    half = jax.ShapeDtypeStruct((LAGS, 64, 256), jnp.float32)
    scratch = [
        pltpu.VMEM((n, 4, CH, QUARTER + LANES), jnp.bfloat16),
        pltpu.VMEM((n, 256, SPAN), jnp.bfloat16),
        pltpu.SemaphoreType.DMA((n, 8)),
    ]
    return pl.pallas_call(
        make_kernel(plan, len(arrays), first, last),
        out_shape=(half, half) if last else sums,
        in_specs=[pl.BlockSpec(memory_space=pltpu.SMEM)] + [anywhere] * (4 + len(arrays)) + ([] if first else [vmem]),
        out_specs=(vmem, vmem) if last else vmem,
        scratch_shapes=scratch + ([pltpu.VMEM((LAGS * CH, 256), jnp.float32)] if last else []),
        input_output_aliases={} if first or last else {5 + len(arrays): 0},
        compiler_params=pltpu.CompilerParams(vmem_limit_bytes=VLIM * 2**20),
        cost_estimate=pl.CostEstimate(flops=n * 2 * 2048 * 256 * 1024, bytes_accessed=n * 2**20, transcendentals=0),
    )(ix, *rows, *arrays, *([] if first else [before]))


def after(values, done):
    return lax.optimization_barrier((values, done))[0]


def on_device(strain):
    c = lax.axis_index("c")
    own = strain.T
    mine = lax.dynamic_slice(own, (0, c * SPAN), (64, SPAN))
    others = lax.dynamic_slice(own, (0, (1 - c) * SPAN), (64, SPAN))
    got = swap(others, "c", 1, 2)
    block = jnp.where(c == 0, jnp.concatenate([mine, got]), jnp.concatenate([got, mine]))

    quarters = [
        lax.ppermute(block[:, QUARTER * q : QUARTER * (q + 1)], AXES, scatter_pairs(q)) for q in range(4)
    ]
    head = lax.ppermute(block[:, :LANES], ("x", "zl", "c"), [(i, i - 1) for i in range(1, 16)])
    slab = jnp.concatenate([block, head], axis=1)
    slabs = jnp.stack([slab, swap(slab, "zl", 1, 2)])
    held = jnp.concatenate(quarters, axis=1)

    above, below = pull(held, "zh", 1, 4), pull(held, "zh", 3, 4)
    own_1, own_3 = swap(held, "y", 1, 4), swap(held, "y", 3, 4)
    rows_2 = pull(after(slabs, held), "x", 2, 4)

    across = pull(after(held, (own_1, own_3)), "zh", 2, 4)
    above, below, own_1, own_3, slabs = lax.optimization_barrier((above, below, own_1, own_3, slabs))
    via_1 = swap(jnp.stack([above, below]), "y", 1, 4)
    via_3 = swap(jnp.stack([above, below, own_1]), "y", 3, 4)
    rows_1 = pull(slabs, "x", 1, 4)
    rows_3 = pull(after(slabs, rows_2), "x", 3, 4)
    rows = [slabs, rows_1, rows_3, rows_2]

    via_1, via_3, across, *rows = lax.optimization_barrier((via_1, via_3, across, *rows))
    late_1 = swap(jnp.stack([across, via_3[1]]), "y", 1, 4)
    late_3 = swap(jnp.stack([across, via_1[0]]), "y", 3, 4)

    ix = jnp.stack([lax.axis_index(name) for name in AXES]).astype(jnp.int32)
    sums = products(
        ix,
        rows,
        [
            (0, 0, [(held, None)], [(own_1, None)]),
            (0, 1, [(via_3, 2)], [(own_3, None)]),
            (1, 0, [(above, None)], [(via_1, 0)]),
            (3, 0, [(below, None)], [(via_1, 1)]),
        ],
    )
    last_1, last_3 = after((late_1, late_3), sums)
    top, bottom = swap(last_1[0, :64], "y", 3, 4), swap(last_3[0, 64:], "y", 1, 4)
    sums = products(
        ix,
        rows,
        [
            (1, 1, [(late_3, 1)], [(via_3, 0)]),
            (3, 1, [(late_1, 1)], [(via_3, 1)]),
            (2, 0, [(across, None)], [(late_1, 0)]),
        ],
        sums,
    )
    keep, send = products(ix, rows, [(2, 1, [(top, None), (bottom, None)], [(late_3, 0)])], sums, last=True)
    return keep + swap(send, "c", 1, 2)


def solution(mesh):
    fine = Mesh(mesh.devices.reshape(SIZES), AXES)
    return jax.shard_map(
        on_device,
        mesh=fine,
        in_specs=(P(("x", "zl"), ("zh", "y", "c")),),
        out_specs=P(None, ("zh", "y", "c"), ("x", "zl")),
        check_vma=False,
    )
```

time: 127 us -> 112 us (0.88)
  the two profiles are of different devices: /device:TPU:45 before, /device:TPU:1 now
where the time goes in v3:
time: 112 us
  starting transfers between devices  46 us (41%)
  waiting for transfers between devices  35.5 us (32%)
  Pallas kernels  18.1 us (16%)
  local copies, waits for them, and re-layouts  9.5 us (8%)
  other arithmetic  2.52 us (2%)
    ppermute x6, waiting for transfers between devices, pull(): lax.ppermute(value, axis, [((i + offset) % count, i) for i in range(count)])  25.4 us
    pallas_call x3, Pallas kernels, products(): pl.pallas_call(make_kernel(plan, len(arrays), first, last), out_shape=(ha...  18.1 us
    ppermute x11, starting transfers between devices, swap(): return lax.ppermute(value, axis, [(i, i ^ bits) for i in range(count)])  18 us
    ppermute x4, starting transfers between devices, on_device(): lax.ppermute(block[:, QUARTER * q:QUARTER * (q + 1)], AXES, scatter_pairs...  15.2 us
    ppermute x6, starting transfers between devices, pull(): lax.ppermute(value, axis, [((i + offset) % count, i) for i in range(count)])  10.5 us
    ppermute x11, waiting for transfers between devices, swap(): return lax.ppermute(value, axis, [(i, i ^ bits) for i in range(count)])  10 us
    unnamed x27, local copies, waits for them, and re-layouts  7.43 us
    ppermute x1, starting transfers between devices, on_device(): lax.ppermute(block[:, :LANES], ('x', 'zl', 'c'), [(i, i - 1) for i in ran...  2.27 us
  transfers between devices with their start and end apart: 22, of which 6 were waited for; matrix products, arithmetic and copies ran while one was open for 0% of the time, Pallas kernels for 13%

profile of v3, /device:TPU:1, one launch (start us, length us, event | category | flops | bytes accessed | tf_op | source)
XLA Modules:
  0.0 111.8 jit_solution(18010165163582309373)
XLA Ops:
  0.0 1.0 dynamic-slice_bitcast_fusion.1
  1.0 3.3 %collective-permute-start = (bf16[64,1024]{1,0:T(8,128)(2,1)S(1)}, bf16[64,1024]{1,0:T(8,128)(2,1)S(1)}, u32[]{:S(2)}, u32[]{:S(2)}) collective-permute-start(bf16[64,1024]{1,0:T(8,128)(2,1)S(1)} %get-tuple-element.52), channel_id=1, source_target_pairs={{0,1},{1,0},{2,3},{3,2},{4,5},{5,4},{6,7},{7,6},{8,9},{9,8},{10,11... | collective-permute-start | bytes 393224 | tf_op jit(solution)/shard_map/ppermute | solution.py:41
  4.3 1.0 collective-permute-done
  5.4 2.3 %collective-permute-start.9 = (bf16[128,128]{1,0:T(8,128)(2,1)S(1)}, bf16[128,128]{1,0:T(8,128)(2,1)S(1)}, u32[]{:S(2)}, u32[]{:S(2)}) collective-permute-start(bf16[128,128]{1,0:T(8,128)(2,1)S(1)} %slice.40), channel_id=1, source_target_pairs={{1,0},{32,1},{33,32},{64,33},{65,64},{96,65},{97,96},{128,97},{129... | collective-permute-start | bytes 98312 | tf_op jit(solution)/shard_map/ppermute | solution.py:159
  8.4 2.9 %collective-permute-start.2 = (bf16[128,256]{1,0:T(8,128)(2,1)S(1)}, bf16[128,256]{1,0:T(8,128)(2,1)S(1)}, u32[]{:S(2)}, u32[]{:S(2)}) collective-permute-start(bf16[128,256]{1,0:T(8,128)(2,1)S(1)} %get-tuple-element.49), channel_id=1, source_target_pairs={{0,8},{1,9},{2,10},{3,11},{4,40},{5,41},{6,42},{7,43},{8,72},{9,73... | collective-permute-start | bytes 196616 | tf_op jit(solution)/shard_map/ppermute | solution.py:157
  11.2 9.6 %collective-permute-start.3 = (bf16[128,256]{1,0:T(8,128)(2,1)S(1)}, bf16[128,256]{1,0:T(8,128)(2,1)S(1)}, u32[]{:S(2)}, u32[]{:S(2)}) collective-permute-start(bf16[128,256]{1,0:T(8,128)(2,1)S(1)} %get-tuple-element.48), channel_id=1, source_target_pairs={{0,16},{1,17},{2,18},{3,19},{4,48},{5,49},{6,50},{7,51},{8,80},{9,... | collective-permute-start | bytes 196616 | tf_op jit(solution)/shard_map/ppermute | solution.py:157
  20.9 2.1 %collective-permute-start.4 = (bf16[128,256]{1,0:T(8,128)(2,1)S(1)}, bf16[128,256]{1,0:T(8,128)(2,1)S(1)}, u32[]{:S(2)}, u32[]{:S(2)}) collective-permute-start(bf16[128,256]{1,0:T(8,128)(2,1)S(1)} %get-tuple-element.47), channel_id=1, source_target_pairs={{0,24},{1,25},{2,26},{3,27},{4,56},{5,57},{6,58},{7,59},{8,88},{9,... | collective-permute-start | bytes 196616 | tf_op jit(solution)/shard_map/ppermute | solution.py:157
  23.0 4.9 %collective-permute-start.10 = (bf16[128,1152]{1,0:T(8,128)(2,1)S(1)}, bf16[128,1152]{1,0:T(8,128)(2,1)S(1)}, u32[]{:S(2)}, u32[]{:S(2)}) collective-permute-start(bf16[128,1152]{1,0:T(8,128)(2,1)S(1)} %get-tuple-element.44), channel_id=1, source_target_pairs={{0,32},{32,0},{1,33},{33,1},{2,34},{34,2},{3,35},{35,3},{4,36},{36... | collective-permute-start | bytes 884744 | tf_op jit(solution)/shard_map/ppermute | solution.py:41
  27.9 6.7 %collective-permute-done.10 = bf16[128,1152]{1,0:T(8,128)(2,1)S(1)} collective-permute-done((bf16[128,1152]{1,0:T(8,128)(2,1)S(1)}, bf16[128,1152]{1,0:T(8,128)(2,1)S(1)}, u32[]{:S(2)}, u32[]{:S(2)}) %collective-permute-start.10) | collective-permute-done | bytes 294944 | tf_op jit(solution)/shard_map/ppermute | solution.py:41
  34.8 5.4 %collective-permute-start.5 = (bf16[128,1024]{1,0:T(8,128)(2,1)S(1)}, bf16[128,1024]{1,0:T(8,128)(2,1)S(1)}, u32[]{:S(2)}, u32[]{:S(2)}) collective-permute-start(bf16[128,1024]{1,0:T(8,128)(2,1)S(1)} %constant_dynamic-update-slice_fusion.refs_4_), channel_id=1, source_target_pairs={{8,0},{16,8},{24,16},{0,24},{9,1},{17,9},{25,17},{1,25},{10,2},{18... | collective-permute-start | bytes 786440 | tf_op jit(solution)/shard_map/ppermute | solution.py:37
  41.0 1.6 %collective-permute-start.8 = (bf16[128,1024]{1,0:T(8,128)(2,1)S(1)}, bf16[128,1024]{1,0:T(8,128)(2,1)S(1)}, u32[]{:S(2)}, u32[]{:S(2)}) collective-permute-start(bf16[128,1024]{1,0:T(8,128)(2,1)S(1)} %constant_dynamic-update-slice_fusion.refs_4_), channel_id=1, source_target_pairs={{0,6},{2,4},{4,2},{6,0},{1,7},{3,5},{5,3},{7,1},{8,14},{10,12},{12... | collective-permute-start | bytes 786440 | tf_op jit(solution)/shard_map/ppermute | solution.py:41
  42.7 8.0 %collective-permute-done.5.refs_8_ = bf16[128,1024]{1,0:T(8,128)(2,1)S(1)} collective-permute-done((bf16[128,1024]{1,0:T(8,128)(2,1)S(1)}, bf16[128,1024]{1,0:T(8,128)(2,1)S(1)}, u32[]{:S(2)}, u32[]{:S(2)}) %collective-permute-start.5) | collective-permute-done | bytes 262176 | tf_op jit(solution)/shard_map/ppermute | solution.py:37
  50.7 3.3 %collective-permute-done.6.refs_10_ = bf16[128,1024]{1,0:T(8,128)(2,1)S(1)} collective-permute-done((bf16[128,1024]{1,0:T(8,128)(2,1)S(1)}, bf16[128,1024]{1,0:T(8,128)(2,1)S(1)}, u32[]{:S(2)}, u32[]{:S(2)}) %collective-permute-start.6) | collective-permute-done | bytes 262176 | tf_op jit(solution)/shard_map/ppermute | solution.py:37
  55.0 1.6 %collective-permute-start.14 = (bf16[2,128,1152]{2,1,0:T(8,128)(2,1)S(1)}, bf16[2,128,1152]{2,1,0:T(8,128)(2,1)S(1)}, u32[]{:S(2)}, u32[]{:S(2)}) collective-permute-start(bf16[2,128,1152]{2,1,0:T(8,128)(2,1)S(1)} %pad_maximum_fusion.3.refs_0_), channel_id=1, source_target_pairs={{64,0},{128,64},{192,128},{0,192},{65,1},{129,65},{193,129},{1,193... | collective-permute-start | bytes 1769480 | tf_op jit(solution)/shard_map/ppermute | solution.py:37
  56.6 2.2 %collective-permute-start.11 = (bf16[2,128,1024]{2,1,0:T(8,128)(2,1)S(1)}, bf16[2,128,1024]{2,1,0:T(8,128)(2,1)S(1)}, u32[]{:S(2)}, u32[]{:S(2)}) collective-permute-start(bf16[2,128,1024]{2,1,0:T(8,128)(2,1)S(1)} %pad_maximum_fusion.4), channel_id=1, source_target_pairs={{0,2},{2,0},{4,6},{6,4},{1,3},{3,1},{5,7},{7,5},{8,10},{10,8},{12,... | collective-permute-start | bytes 1572872 | tf_op jit(solution)/shard_map/ppermute | solution.py:41
  58.8 3.4 %collective-permute-start.13 = (bf16[128,1024]{1,0:T(8,128)(2,1)S(1)}, bf16[128,1024]{1,0:T(8,128)(2,1)S(1)}, u32[]{:S(2)}, u32[]{:S(2)}) collective-permute-start(bf16[128,1024]{1,0:T(8,128)(2,1)S(1)} %constant_dynamic-update-slice_fusion.refs_4_), channel_id=1, source_target_pairs={{16,0},{24,8},{0,16},{8,24},{17,1},{25,9},{1,17},{9,25},{18,2},{26... | collective-permute-start | bytes 786440 | tf_op jit(solution)/shard_map/ppermute | solution.py:37
  62.2 14.1 %collective-permute-done.13.refs_7_ = bf16[128,1024]{1,0:T(8,128)(2,1)S(1)} collective-permute-done((bf16[128,1024]{1,0:T(8,128)(2,1)S(1)}, bf16[128,1024]{1,0:T(8,128)(2,1)S(1)}, u32[]{:S(2)}, u32[]{:S(2)}) %collective-permute-start.13) | collective-permute-done | bytes 262176 | tf_op jit(solution)/shard_map/ppermute | solution.py:37
  78.0 1.1 pad_maximum_fusion.1
  79.3 1.9 %collective-permute-start.18 = (bf16[2,128,1024]{2,1,0:T(8,128)(2,1)}, bf16[2,128,1024]{2,1,0:T(8,128)(2,1)S(1)}, u32[]{:S(2)}, u32[]{:S(2)}) collective-permute-start(bf16[2,128,1024]{2,1,0:T(8,128)(2,1)} %get-tuple-element.45), channel_id=1, source_target_pairs={{0,6},{2,4},{4,2},{6,0},{1,7},{3,5},{5,3},{7,1},{8,14},{10,12},{12... | collective-permute-start | bytes 1572872 | tf_op jit(solution)/shard_map/ppermute | solution.py:41
  81.2 0.9 copy-done.3
  82.2 1.0 copy-done.5
  83.2 1.1 %copy-done.7 = bf16[3,128,1024]{2,1,0:T(8,128)(2,1)S(1)} copy-done((bf16[3,128,1024]{2,1,0:T(8,128)(2,1)S(1)}, bf16[3,128,1024]{2,1,0:T(8,128)(2,1)}, u32[]{:S(2)}) %copy-start.7) | copy-done | bytes 786456
  84.4 0.9 copy-done.9
  85.3 0.9 copy-done.11
  86.3 8.3 %shard_map.17.refs_8_ = f32[2048,256]{1,0:T(8,128)S(1)} custom-call(s32[5]{0:T(128)S(1)} %stack.59.ix, bf16[2,128,1152]{2,1,0:T(8,128)(2,1)S(1)} %pad_maximum_fusion.3.refs_0_, bf16[2,128,1152]{2,1,0:T(8,128)(2,1)S(1)} %collective-permute-done.14.refs_1_, bf16[2,128,1152]{2,1,0:T(8,128)(2,1)S(1)} %collective-permute-done.16.refs_2_, ...), custom_call_target="tpu_custom_call" | custom-call | flops 4294967296 | bytes 4194304 | tf_op jit(solution)/shard_map/pallas_call | solution.py:132
  94.6 0.9 slice_bitcast_fusion.1
  95.5 0.9 collective-permute-start.19
  96.6 6.7 %shard_map.18.refs_7_ = f32[2048,256]{1,0:T(8,128)S(1)} custom-call(s32[5]{0:T(128)S(1)} %stack.59.ix, bf16[2,128,1152]{2,1,0:T(8,128)(2,1)S(1)} %pad_maximum_fusion.3.refs_0_, bf16[2,128,1152]{2,1,0:T(8,128)(2,1)S(1)} %collective-permute-done.14.refs_1_, bf16[2,128,1152]{2,1,0:T(8,128)(2,1)S(1)} %collective-permute-done.16.refs_2_, ...), custom_call_target="tpu_custom_call", output_to_operand_aliasing={{}: (9, {})} | custom-call | flops 3221225472 | bytes 3145728 | tf_op jit(solution)/shard_map/pallas_call | solution.py:132
  103.4 3.1 %shard_map.19 = (f32[16,64,256]{2,1,0:T(8,128)S(1)}, f32[16,64,256]{2,1,0:T(8,128)S(1)}) custom-call(s32[5]{0:T(128)S(1)} %stack.59.ix, bf16[2,128,1152]{2,1,0:T(8,128)(2,1)S(1)} %pad_maximum_fusion.3.refs_0_, bf16[2,128,1152]{2,1,0:T(8,128)(2,1)S(1)} %collective-permute-done.14.refs_1_, bf16[2,128,1152]{2,1,0:T(8,128)(2,1)S(1)} %collective-permute-done.16.refs_2_, ...), custom_call_target="tpu_custom_call" | custom-call | flops 1073741824 | bytes 1048576 | tf_op jit(solution)/shard_map/pallas_call | solution.py:132
  106.4 2.0 %collective-permute-start.21 = (f32[16,64,256]{2,1,0:T(8,128)S(1)}, f32[16,64,256]{2,1,0:T(8,128)S(1)}, u32[]{:S(2)}, u32[]{:S(2)}) collective-permute-start(f32[16,64,256]{2,1,0:T(8,128)S(1)} %get-tuple-element.42), channel_id=1, source_target_pairs={{0,1},{1,0},{2,3},{3,2},{4,5},{5,4},{6,7},{7,6},{8,9},{9,8},{10,11... | collective-permute-start | bytes 3145736 | tf_op jit(solution)/shard_map/ppermute | solution.py:41
  108.4 2.3 %collective-permute-done.21 = f32[16,64,256]{2,1,0:T(8,128)S(1)} collective-permute-done((f32[16,64,256]{2,1,0:T(8,128)S(1)}, f32[16,64,256]{2,1,0:T(8,128)S(1)}, u32[]{:S(2)}, u32[]{:S(2)}) %collective-permute-start.21) | collective-permute-done | bytes 1048608 | tf_op jit(solution)/shard_map/ppermute | solution.py:41
  110.7 1.1 add.11
  (58 shorter events, 4.9 us)
Async XLA Ops:
  1.0 4.3 %collective-permute-start = (bf16[64,1024]{1,0:T(8,128)(2,1)S(1)}, bf16[64,1024]{1,0:T(8,128)(2,1)S(1)}, u32[]{:S(2)}, u32[]{:S(2)}) collective-permute-start(bf16[64,1024]{1,0:T(8,128)(2,1)S(1)} %get-tuple-element.52), channel_id=1, source_target_pairs={{0,1},{1,0},{2,3},{3,2},{4,5},{5,4},{6,7},{7,6},{8,9},{9,8},{10,11... | collective-permute-start | bytes 393224 | tf_op jit(solution)/shard_map/ppermute | solution.py:41
  5.4 17.5 %collective-permute-start.9 = (bf16[128,128]{1,0:T(8,128)(2,1)S(1)}, bf16[128,128]{1,0:T(8,128)(2,1)S(1)}, u32[]{:S(2)}, u32[]{:S(2)}) collective-permute-start(bf16[128,128]{1,0:T(8,128)(2,1)S(1)} %slice.40), channel_id=1, source_target_pairs={{1,0},{32,1},{33,32},{64,33},{65,64},{96,65},{97,96},{128,97},{129... | collective-permute-start | bytes 98312 | tf_op jit(solution)/shard_map/ppermute | solution.py:159
  7.7 20.1 %collective-permute-start.1 = (bf16[128,256]{1,0:T(8,128)(2,1)S(1)}, bf16[128,256]{1,0:T(8,128)(2,1)S(1)}, u32[]{:S(2)}, u32[]{:S(2)}) collective-permute-start(bf16[128,256]{1,0:T(8,128)(2,1)S(1)} %get-tuple-element.50), channel_id=1, source_target_pairs={{0,0},{1,1},{2,2},{3,3},{4,32},{5,33},{6,34},{7,35},{8,64},{9,65},... | collective-permute-start | bytes 196616 | tf_op jit(solution)/shard_map/ppermute | solution.py:157
  8.4 19.5 %collective-permute-start.2 = (bf16[128,256]{1,0:T(8,128)(2,1)S(1)}, bf16[128,256]{1,0:T(8,128)(2,1)S(1)}, u32[]{:S(2)}, u32[]{:S(2)}) collective-permute-start(bf16[128,256]{1,0:T(8,128)(2,1)S(1)} %get-tuple-element.49), channel_id=1, source_target_pairs={{0,8},{1,9},{2,10},{3,11},{4,40},{5,41},{6,42},{7,43},{8,72},{9,73... | collective-permute-start | bytes 196616 | tf_op jit(solution)/shard_map/ppermute | solution.py:157
  11.2 16.6 %collective-permute-start.3 = (bf16[128,256]{1,0:T(8,128)(2,1)S(1)}, bf16[128,256]{1,0:T(8,128)(2,1)S(1)}, u32[]{:S(2)}, u32[]{:S(2)}) collective-permute-start(bf16[128,256]{1,0:T(8,128)(2,1)S(1)} %get-tuple-element.48), channel_id=1, source_target_pairs={{0,16},{1,17},{2,18},{3,19},{4,48},{5,49},{6,50},{7,51},{8,80},{9,... | collective-permute-start | bytes 196616 | tf_op jit(solution)/shard_map/ppermute | solution.py:157
  20.9 7.0 %collective-permute-start.4 = (bf16[128,256]{1,0:T(8,128)(2,1)S(1)}, bf16[128,256]{1,0:T(8,128)(2,1)S(1)}, u32[]{:S(2)}, u32[]{:S(2)}) collective-permute-start(bf16[128,256]{1,0:T(8,128)(2,1)S(1)} %get-tuple-element.47), channel_id=1, source_target_pairs={{0,24},{1,25},{2,26},{3,27},{4,56},{5,57},{6,58},{7,59},{8,88},{9,... | collective-permute-start | bytes 196616 | tf_op jit(solution)/shard_map/ppermute | solution.py:157
  23.0 11.7 %collective-permute-start.10 = (bf16[128,1152]{1,0:T(8,128)(2,1)S(1)}, bf16[128,1152]{1,0:T(8,128)(2,1)S(1)}, u32[]{:S(2)}, u32[]{:S(2)}) collective-permute-start(bf16[128,1152]{1,0:T(8,128)(2,1)S(1)} %get-tuple-element.44), channel_id=1, source_target_pairs={{0,32},{32,0},{1,33},{33,1},{2,34},{34,2},{3,35},{35,3},{4,36},{36... | collective-permute-start | bytes 884744 | tf_op jit(solution)/shard_map/ppermute | solution.py:41
  27.9 48.4 %copy-start.8 = (bf16[128,1024]{1,0:T(8,128)(2,1)}, bf16[128,1024]{1,0:T(8,128)(2,1)S(1)}, u32[]{:S(2)}) copy-start(bf16[128,1024]{1,0:T(8,128)(2,1)S(1)} %constant_dynamic-update-slice_fusion.refs_4_) | copy-start | bytes 786436
  34.7 21.8 %collective-permute-start.15 = (bf16[2,128,1152]{2,1,0:T(8,128)(2,1)S(1)}, bf16[2,128,1152]{2,1,0:T(8,128)(2,1)S(1)}, u32[]{:S(2)}, u32[]{:S(2)}) collective-permute-start(bf16[2,128,1152]{2,1,0:T(8,128)(2,1)S(1)} %pad_maximum_fusion.3.refs_0_), channel_id=1, source_target_pairs={{128,0},{192,64},{0,128},{64,192},{129,1},{193,65},{1,129},{65,193... | collective-permute-start | bytes 1769480 | tf_op jit(solution)/shard_map/ppermute | solution.py:37
  34.8 15.9 %collective-permute-start.5 = (bf16[128,1024]{1,0:T(8,128)(2,1)S(1)}, bf16[128,1024]{1,0:T(8,128)(2,1)S(1)}, u32[]{:S(2)}, u32[]{:S(2)}) collective-permute-start(bf16[128,1024]{1,0:T(8,128)(2,1)S(1)} %constant_dynamic-update-slice_fusion.refs_4_), channel_id=1, source_target_pairs={{8,0},{16,8},{24,16},{0,24},{9,1},{17,9},{25,17},{1,25},{10,2},{18... | collective-permute-start | bytes 786440 | tf_op jit(solution)/shard_map/ppermute | solution.py:37
  40.2 13.8 %collective-permute-start.6 = (bf16[128,1024]{1,0:T(8,128)(2,1)S(1)}, bf16[128,1024]{1,0:T(8,128)(2,1)S(1)}, u32[]{:S(2)}, u32[]{:S(2)}) collective-permute-start(bf16[128,1024]{1,0:T(8,128)(2,1)S(1)} %constant_dynamic-update-slice_fusion.refs_4_), channel_id=1, source_target_pairs={{24,0},{0,8},{8,16},{16,24},{25,1},{1,9},{9,17},{17,25},{26,2},{2,... | collective-permute-start | bytes 786440 | tf_op jit(solution)/shard_map/ppermute | solution.py:37
  40.2 13.8 %collective-permute-start.7 = (bf16[128,1024]{1,0:T(8,128)(2,1)S(1)}, bf16[128,1024]{1,0:T(8,128)(2,1)S(1)}, u32[]{:S(2)}, u32[]{:S(2)}) collective-permute-start(bf16[128,1024]{1,0:T(8,128)(2,1)S(1)} %constant_dynamic-update-slice_fusion.refs_4_), channel_id=1, source_target_pairs={{0,2},{2,0},{4,6},{6,4},{1,3},{3,1},{5,7},{7,5},{8,10},{10,8},{12,... | collective-permute-start | bytes 786440 | tf_op jit(solution)/shard_map/ppermute | solution.py:41
  41.0 13.0 %collective-permute-start.8 = (bf16[128,1024]{1,0:T(8,128)(2,1)S(1)}, bf16[128,1024]{1,0:T(8,128)(2,1)S(1)}, u32[]{:S(2)}, u32[]{:S(2)}) collective-permute-start(bf16[128,1024]{1,0:T(8,128)(2,1)S(1)} %constant_dynamic-update-slice_fusion.refs_4_), channel_id=1, source_target_pairs={{0,6},{2,4},{4,2},{6,0},{1,7},{3,5},{5,3},{7,1},{8,14},{10,12},{12... | collective-permute-start | bytes 786440 | tf_op jit(solution)/shard_map/ppermute | solution.py:41
  54.0 2.6 %copy-start.2 = (bf16[128,1024]{1,0:T(8,128)(2,1)}, bf16[128,1024]{1,0:T(8,128)(2,1)S(1)}, u32[]{:S(2)}) copy-start(bf16[128,1024]{1,0:T(8,128)(2,1)S(1)} %collective-permute-done.7.refs_5_) | copy-start | bytes 786436
  54.9 21.4 %collective-permute-start.12 = (bf16[3,128,1024]{2,1,0:T(8,128)(2,1)S(1)}, bf16[3,128,1024]{2,1,0:T(8,128)(2,1)S(1)}, u32[]{:S(2)}, u32[]{:S(2)}) collective-permute-start(bf16[3,128,1024]{2,1,0:T(8,128)(2,1)S(1)} %pad_maximum_fusion), channel_id=1, source_target_pairs={{0,6},{2,4},{4,2},{6,0},{1,7},{3,5},{5,3},{7,1},{8,14},{10,12},{12... | collective-permute-start | bytes 2359304 | tf_op jit(solution)/shard_map/ppermute | solution.py:41
  55.0 21.3 %collective-permute-start.14 = (bf16[2,128,1152]{2,1,0:T(8,128)(2,1)S(1)}, bf16[2,128,1152]{2,1,0:T(8,128)(2,1)S(1)}, u32[]{:S(2)}, u32[]{:S(2)}) collective-permute-start(bf16[2,128,1152]{2,1,0:T(8,128)(2,1)S(1)} %pad_maximum_fusion.3.refs_0_), channel_id=1, source_target_pairs={{64,0},{128,64},{192,128},{0,192},{65,1},{129,65},{193,129},{1,193... | collective-permute-start | bytes 1769480 | tf_op jit(solution)/shard_map/ppermute | solution.py:37
  56.5 19.8 %collective-permute-start.16 = (bf16[2,128,1152]{2,1,0:T(8,128)(2,1)S(1)}, bf16[2,128,1152]{2,1,0:T(8,128)(2,1)S(1)}, u32[]{:S(2)}, u32[]{:S(2)}) collective-permute-start(bf16[2,128,1152]{2,1,0:T(8,128)(2,1)S(1)} %pad_maximum_fusion.3.refs_0_), channel_id=1, source_target_pairs={{192,0},{0,64},{64,128},{128,192},{193,1},{1,65},{65,129},{129,193... | collective-permute-start | bytes 1769480 | tf_op jit(solution)/shard_map/ppermute | solution.py:37
  56.6 19.7 %collective-permute-start.11 = (bf16[2,128,1024]{2,1,0:T(8,128)(2,1)S(1)}, bf16[2,128,1024]{2,1,0:T(8,128)(2,1)S(1)}, u32[]{:S(2)}, u32[]{:S(2)}) collective-permute-start(bf16[2,128,1024]{2,1,0:T(8,128)(2,1)S(1)} %pad_maximum_fusion.4), channel_id=1, source_target_pairs={{0,2},{2,0},{4,6},{6,4},{1,3},{3,1},{5,7},{7,5},{8,10},{10,8},{12,... | collective-permute-start | bytes 1572872 | tf_op jit(solution)/shard_map/ppermute | solution.py:41
  58.8 17.5 %collective-permute-start.13 = (bf16[128,1024]{1,0:T(8,128)(2,1)S(1)}, bf16[128,1024]{1,0:T(8,128)(2,1)S(1)}, u32[]{:S(2)}, u32[]{:S(2)}) collective-permute-start(bf16[128,1024]{1,0:T(8,128)(2,1)S(1)} %constant_dynamic-update-slice_fusion.refs_4_), channel_id=1, source_target_pairs={{16,0},{24,8},{0,16},{8,24},{17,1},{25,9},{1,17},{9,25},{18,2},{26... | collective-permute-start | bytes 786440 | tf_op jit(solution)/shard_map/ppermute | solution.py:37
  76.3 3.0 %copy-start = (bf16[128,1024]{1,0:T(8,128)(2,1)}, bf16[128,1024]{1,0:T(8,128)(2,1)S(1)}, u32[]{:S(2)}) copy-start(bf16[128,1024]{1,0:T(8,128)(2,1)S(1)} %collective-permute-done.13.refs_7_) | copy-start | bytes 786436
  76.3 0.9 copy-start.6
  79.2 15.4 %collective-permute-start.17 = (bf16[2,128,1024]{2,1,0:T(8,128)(2,1)}, bf16[2,128,1024]{2,1,0:T(8,128)(2,1)}, u32[]{:S(2)}, u32[]{:S(2)}) collective-permute-start(bf16[2,128,1024]{2,1,0:T(8,128)(2,1)} %get-tuple-element.46), channel_id=1, source_target_pairs={{0,2},{2,0},{4,6},{6,4},{1,3},{3,1},{5,7},{7,5},{8,10},{10,8},{12,... | collective-permute-start | bytes 1572872 | tf_op jit(solution)/shard_map/ppermute | solution.py:41
  79.3 15.3 %collective-permute-start.18 = (bf16[2,128,1024]{2,1,0:T(8,128)(2,1)}, bf16[2,128,1024]{2,1,0:T(8,128)(2,1)S(1)}, u32[]{:S(2)}, u32[]{:S(2)}) collective-permute-start(bf16[2,128,1024]{2,1,0:T(8,128)(2,1)} %get-tuple-element.45), channel_id=1, source_target_pairs={{0,6},{2,4},{4,2},{6,0},{1,7},{3,5},{5,3},{7,1},{8,14},{10,12},{12... | collective-permute-start | bytes 1572872 | tf_op jit(solution)/shard_map/ppermute | solution.py:41
  81.2 1.0 copy-start.3
  82.2 1.0 copy-start.5
  83.2 1.1 %copy-start.7 = (bf16[3,128,1024]{2,1,0:T(8,128)(2,1)S(1)}, bf16[3,128,1024]{2,1,0:T(8,128)(2,1)}, u32[]{:S(2)}) copy-start(bf16[3,128,1024]{2,1,0:T(8,128)(2,1)} %copy-done.6) | copy-start | bytes 2359300
  84.4 0.9 copy-start.9
  85.3 0.9 copy-start.11
  86.3 10.4 %copy-start.1 = (bf16[128,1024]{1,0:T(8,128)(2,1)S(1)}, bf16[128,1024]{1,0:T(8,128)(2,1)}, u32[]{:S(2)}) copy-start(bf16[128,1024]{1,0:T(8,128)(2,1)} %copy-done) | copy-start | bytes 786436
  95.5 7.9 %collective-permute-start.19 = (bf16[64,1024]{1,0:T(8,128)(2,1)S(1)}, bf16[64,1024]{1,0:T(8,128)(2,1)S(1)}, u32[]{:S(2)}, u32[]{:S(2)}) collective-permute-start(bf16[64,1024]{1,0:T(8,128)(2,1)S(1)} %slice_bitcast_fusion.1), channel_id=1, source_target_pairs={{0,6},{2,4},{4,2},{6,0},{1,7},{3,5},{5,3},{7,1},{8,14},{10,12},{12... | collective-permute-start | bytes 393224 | tf_op jit(solution)/shard_map/ppermute | solution.py:41
  96.4 7.0 %collective-permute-start.20 = (bf16[64,1024]{1,0:T(8,128)(2,1)S(1)}, bf16[64,1024]{1,0:T(8,128)(2,1)S(1)}, u32[]{:S(2)}, u32[]{:S(2)}) collective-permute-start(bf16[64,1024]{1,0:T(8,128)(2,1)S(1)} %slice_bitcast_fusion), channel_id=1, source_target_pairs={{0,2},{2,0},{4,6},{6,4},{1,3},{3,1},{5,7},{7,5},{8,10},{10,8},{12,... | collective-permute-start | bytes 393224 | tf_op jit(solution)/shard_map/ppermute | solution.py:41
  106.4 4.3 %collective-permute-start.21 = (f32[16,64,256]{2,1,0:T(8,128)S(1)}, f32[16,64,256]{2,1,0:T(8,128)S(1)}, u32[]{:S(2)}, u32[]{:S(2)}) collective-permute-start(f32[16,64,256]{2,1,0:T(8,128)S(1)} %get-tuple-element.42), channel_id=1, source_target_pairs={{0,1},{1,0},{2,3},{3,2},{4,5},{5,4},{6,7},{7,6},{8,9},{9,8},{10,11... | collective-permute-start | bytes 3145736 | tf_op jit(solution)/shard_map/ppermute | solution.py:41
  (2 other events, 1.5 us)

commit v4 on v3

--- a/solution.py
+++ b/solution.py
@@ -12,7 +12,7 @@
 CH, SPAN, QUARTER, LANES = 128, 1024, 256, 128
 OFFSETS = (0, 1, 3, 2)
 ROWS_AT = (0, 1, 3, 2)
-VLIM = 28
+VLIM = 14
 
 
 def device_of(x, zl, zh, y, c):
@@ -41,7 +41,12 @@
     return lax.ppermute(value, axis, [(i, i ^ bits) for i in range(count)])
 
 
-def make_kernel(pieces, n_arrays, first, last):
+def lagged(wide, lags):
+    shifted = [jnp.concatenate([window[:, lag : lag + QUARTER] for window in wide], axis=1) for lag in lags]
+    return jnp.concatenate(shifted, axis=0)
+
+
+def make_kernel(pieces, n_arrays, first, share):
     n = len(pieces)
 
     def kernel(ix, *refs):
@@ -49,9 +54,7 @@
         rows = [refs.pop(0) for _ in OFFSETS]
         arrays = [refs.pop(0) for _ in range(n_arrays)]
         before = None if first else refs.pop(0)
-        outs = [refs.pop(0) for _ in range(2 if last else 1)]
-        windows, earlier, sems = refs[:3]
-        total = refs[3] if last else outs[0]
+        total, windows, earlier, sems = refs
         x, zl, zh, y, c = (ix[i] for i in range(5))
         half = lax.rem(y, 2)
         away_zl = lax.select(lax.div(y, 2) == zl, 0, 1)
@@ -70,24 +73,32 @@
                 size = CH // len(parts)
                 for s, (number, index) in enumerate(parts):
                     start = pl.multiple_of(place * CH + s * size, size)
-                    source = arrays[number] if index is None else arrays[number].at[index]
+                    source = arrays[number].at[pl.ds(index, size), :]
                     copy = pltpu.make_async_copy(source, earlier.at[i, pl.ds(start, size), :], sems.at[i, 4 + 2 * j + s])
                     copy.start()
                     mine.append(copy)
             copies.append(mine)
+        if share:
+            mine = c if share == "keep" else 1 - c
+            for copy in copies[0]:
+                copy.wait()
+            wide = [windows[0, q, pl.ds(pl.multiple_of(mine * 64, 64), 64), :] for q in range(4)]
+            for s in range(2):
+                part = lax.dot_general(
+                    lagged(wide, range(8 * s, 8 * s + 8)), earlier[0], (((1,), (1,)), ((), ())), preferred_element_type=jnp.float32
+                )
+                for lag in range(8 * s, 8 * s + 8):
+                    so_far = before[pl.ds(pl.multiple_of(lag * CH + mine * 64, 64), 64), :]
+                    at = (lag - 8 * s) * 64
+                    total[lag] = (so_far + part[at : at + 64, :]) * jnp.float32(1.0 / (TOTAL - lag))
+            return
         for i in range(n):
             for copy in copies[i]:
                 copy.wait()
             wide = [windows[i, q] for q in range(4)]
             for s in range(4):
                 span = slice(512 * s, 512 * (s + 1))
-                later = jnp.concatenate(
-                    [
-                        jnp.concatenate([window[:, lag : lag + QUARTER] for window in wide], axis=1)
-                        for lag in range(4 * s, 4 * s + 4)
-                    ],
-                    axis=0,
-                )
+                later = lagged(wide, range(4 * s, 4 * s + 4))
                 part = lax.dot_general(
                     later, earlier[i], (((1,), (1,)), ((), ())), preferred_element_type=jnp.float32
                 )
@@ -97,18 +108,12 @@
                     total[span, :] = part
                 else:
                     total[span, :] = before[span, :] + part
-        if last:
-            keep, send = outs
-            for lag in range(LAGS):
-                scale = jnp.float32(1.0 / (TOTAL - lag))
-                keep[lag] = total[pl.ds(pl.multiple_of(lag * CH + c * 64, 64), 64), :] * scale
-                send[lag] = total[pl.ds(pl.multiple_of(lag * CH + (1 - c) * 64, 64), 64), :] * scale
 
     return kernel
 
 
-def products(ix, rows, pieces, before=None, last=False):
-    vmem, anywhere = pl.BlockSpec(memory_space=pltpu.VMEM), pl.BlockSpec(memory_space=pltpu.HBM)
+def products(ix, rows, pieces, before=None, share=None):
+    vmem, anywhere = pl.BlockSpec(memory_space=pltpu.VMEM), pl.BlockSpec(memory_space=pl.ANY)
     n, first = len(pieces), before is None
     arrays, plan = [], []
     for offset, pair, *blocks in pieces:
@@ -130,15 +135,54 @@
         pltpu.SemaphoreType.DMA((n, 8)),
     ]
     return pl.pallas_call(
-        make_kernel(plan, len(arrays), first, last),
-        out_shape=(half, half) if last else sums,
+        make_kernel(plan, len(arrays), first, share),
+        out_shape=half if share else sums,
         in_specs=[pl.BlockSpec(memory_space=pltpu.SMEM)] + [anywhere] * (4 + len(arrays)) + ([] if first else [vmem]),
-        out_specs=(vmem, vmem) if last else vmem,
-        scratch_shapes=scratch + ([pltpu.VMEM((LAGS * CH, 256), jnp.float32)] if last else []),
-        input_output_aliases={} if first or last else {5 + len(arrays): 0},
+        out_specs=vmem,
+        scratch_shapes=scratch,
+        input_output_aliases={} if first or share else {5 + len(arrays): 0},
         compiler_params=pltpu.CompilerParams(vmem_limit_bytes=VLIM * 2**20),
         cost_estimate=pl.CostEstimate(flops=n * 2 * 2048 * 256 * 1024, bytes_accessed=n * 2**20, transcendentals=0),
     )(ix, *rows, *arrays, *([] if first else [before]))
+
+
+def pack(*plans):
+    arrays, numbered = [], []
+    for plan in plans:
+        numbers = []
+        for array, first, count in plan:
+            known = [i for i, other in enumerate(arrays) if other is array]
+            if not known:
+                arrays.append(array)
+            numbers.append(((known or [len(arrays) - 1])[0], first, count))
+        numbered.append(numbers)
+
+    def copy_kernel(*refs):
+        sources, targets, sems = refs[: len(arrays)], refs[len(arrays) : -1], refs[-1]
+        copies = []
+        for target, numbers in zip(targets, numbered):
+            at = 0
+            for number, first, count in numbers:
+                copies.append(
+                    pltpu.make_async_copy(
+                        sources[number].at[pl.ds(first, count), :], target.at[pl.ds(at, count), :], sems.at[len(copies)]
+                    )
+                )
+                copies[-1].start()
+                at += count
+        for copy in copies:
+            copy.wait()
+
+    anywhere = pl.BlockSpec(memory_space=pl.ANY)
+    return pl.pallas_call(
+        copy_kernel,
+        out_shape=[jax.ShapeDtypeStruct((sum(p[2] for p in plan), SPAN), jnp.bfloat16) for plan in plans],
+        in_specs=[anywhere] * len(arrays),
+        out_specs=[anywhere] * len(plans),
+        scratch_shapes=[pltpu.SemaphoreType.DMA((sum(len(plan) for plan in plans),))],
+        compiler_params=pltpu.CompilerParams(vmem_limit_bytes=2**20),
+        cost_estimate=pl.CostEstimate(flops=0, bytes_accessed=2**20, transcendentals=0),
+    )(*arrays)
 
 
 def after(values, done):
@@ -162,46 +206,52 @@
     held = jnp.concatenate(quarters, axis=1)
 
     above, below = pull(held, "zh", 1, 4), pull(held, "zh", 3, 4)
-    own_1, own_3 = swap(held, "y", 1, 4), swap(held, "y", 3, 4)
-    rows_2 = pull(after(slabs, held), "x", 2, 4)
+    held_then, slabs = lax.optimization_barrier((held, slabs))
+    own_1, own_3 = swap(held_then, "y", 1, 4), swap(held_then, "y", 3, 4)
+    rows_2 = pull(slabs, "x", 2, 4)
 
     across = pull(after(held, (own_1, own_3)), "zh", 2, 4)
-    above, below, own_1, own_3, slabs = lax.optimization_barrier((above, below, own_1, own_3, slabs))
-    via_1 = swap(jnp.stack([above, below]), "y", 1, 4)
-    via_3 = swap(jnp.stack([above, below, own_1]), "y", 3, 4)
+    above, below, own_1, own_3, slabs, rows_2 = lax.optimization_barrier(
+        (above, below, own_1, own_3, slabs, rows_2)
+    )
+    to_1, to_3 = pack([(above, 0, CH), (below, 0, CH)], [(above, 0, CH), (below, 0, CH), (own_1, 0, CH)])
+    via_1, via_3 = swap(to_1, "y", 1, 4), swap(to_3, "y", 3, 4)
     rows_1 = pull(slabs, "x", 1, 4)
-    rows_3 = pull(after(slabs, rows_2), "x", 3, 4)
+    rows_3 = pull(slabs, "x", 3, 4)
     rows = [slabs, rows_1, rows_3, rows_2]
 
     via_1, via_3, across, *rows = lax.optimization_barrier((via_1, via_3, across, *rows))
-    late_1 = swap(jnp.stack([across, via_3[1]]), "y", 1, 4)
-    late_3 = swap(jnp.stack([across, via_1[0]]), "y", 3, 4)
+    to_1, to_3 = pack([(across, 0, CH), (via_3, CH, CH)], [(across, 0, CH), (via_1, 0, CH)])
+    late_1, late_3 = swap(to_1, "y", 1, 4), swap(to_3, "y", 3, 4)
 
     ix = jnp.stack([lax.axis_index(name) for name in AXES]).astype(jnp.int32)
     sums = products(
         ix,
         rows,
         [
-            (0, 0, [(held, None)], [(own_1, None)]),
-            (0, 1, [(via_3, 2)], [(own_3, None)]),
-            (1, 0, [(above, None)], [(via_1, 0)]),
-            (3, 0, [(below, None)], [(via_1, 1)]),
+            (0, 0, [(held, 0)], [(own_1, 0)]),
+            (0, 1, [(via_3, 2 * CH)], [(own_3, 0)]),
+            (1, 0, [(above, 0)], [(via_1, 0)]),
+            (3, 0, [(below, 0)], [(via_1, CH)]),
         ],
     )
     last_1, last_3 = after((late_1, late_3), sums)
-    top, bottom = swap(last_1[0, :64], "y", 3, 4), swap(last_3[0, 64:], "y", 1, 4)
+    to_3, to_1 = pack([(last_1, 0, 64)], [(last_3, 64, 64)])
+    top, bottom = swap(to_3, "y", 3, 4), swap(to_1, "y", 1, 4)
     sums = products(
         ix,
         rows,
         [
-            (1, 1, [(late_3, 1)], [(via_3, 0)]),
-            (3, 1, [(late_1, 1)], [(via_3, 1)]),
-            (2, 0, [(across, None)], [(late_1, 0)]),
+            (1, 1, [(late_3, CH)], [(via_3, 0)]),
+            (3, 1, [(late_1, CH)], [(via_3, CH)]),
+            (2, 0, [(across, 0)], [(late_1, 0)]),
         ],
         sums,
     )
-    keep, send = products(ix, rows, [(2, 1, [(top, None), (bottom, None)], [(late_3, 0)])], sums, last=True)
-    return keep + swap(send, "c", 1, 2)
+    final = [(2, 1, [(top, 0), (bottom, 0)], [(late_3, 0)])]
+    send = products(ix, rows, final, sums, share="send")
+    got = swap(send, "c", 1, 2)
+    return products(ix, rows, final, sums, share="keep") + got
 
 
 def solution(mesh):

time: 112 us -> 110 us (0.982)
  Pallas kernels: 18.1 us -> 21.4 us
  local copies, waits for them, and re-layouts: 9.5 us -> 7.78 us
  waiting for transfers between devices: 35.5 us -> 33.9 us
  other arithmetic: 2.52 us -> 1.26 us
    pallas_call x3 -> x7, Pallas kernels: 18.1 us -> 21.4 us  [the longest x4 19.2 us: products(): pl.pallas_call(make_kernel(plan, len(arrays), first, share), out_shape=ha...]
    ppermute x11, waiting for transfers between devices: 10 us -> 7.94 us  [swap(): return lax.ppermute(value, axis, [(i, i ^ bits) for i in range(count)])]
    another operation x3 -> x0, other arithmetic: 1.25 us -> none  [the longest x1 1.12 us: on_device(): late_3 = swap(jnp.stack([across, via_1[0]]), 'y', 3, 4)]
    unnamed x27 -> x33, local copies, waits for them, and re-layouts: 7.43 us -> 6.68 us
  transfers between devices with their start and end apart: 22 -> 22, of which waited for: 6 -> 6; matrix products, arithmetic and copies ran while one was open for 0% -> 0% of each run, Pallas kernels for 13% -> 16%
where the time goes in v4:
time: 110 us
  starting transfers between devices  45.5 us (41%)
  waiting for transfers between devices  33.9 us (31%)
  Pallas kernels  21.4 us (19%)
  local copies, waits for them, and re-layouts  7.78 us (7%)
  other arithmetic  1.26 us (1%)
    ppermute x6, waiting for transfers between devices, pull(): lax.ppermute(value, axis, [((i + offset) % count, i) for i in range(count)])  25.9 us
    pallas_call x4, Pallas kernels, products(): pl.pallas_call(make_kernel(plan, len(arrays), first, share), out_shape=ha...  19.2 us
    ppermute x11, starting transfers between devices, swap(): return lax.ppermute(value, axis, [(i, i ^ bits) for i in range(count)])  17.6 us
    ppermute x4, starting transfers between devices, on_device(): lax.ppermute(block[:, QUARTER * q:QUARTER * (q + 1)], AXES, scatter_pairs...  15.2 us
    ppermute x6, starting transfers between devices, pull(): lax.ppermute(value, axis, [((i + offset) % count, i) for i in range(count)])  10.4 us
    ppermute x11, waiting for transfers between devices, swap(): return lax.ppermute(value, axis, [(i, i ^ bits) for i in range(count)])  7.94 us
    unnamed x33, local copies, waits for them, and re-layouts  6.68 us
    ppermute x1, starting transfers between devices, on_device(): lax.ppermute(block[:, :LANES], ('x', 'zl', 'c'), [(i, i - 1) for i in ran...  2.27 us
  transfers between devices with their start and end apart: 22, of which 6 were waited for; matrix products, arithmetic and copies ran while one was open for 0% of the time, Pallas kernels for 16%

profile of v4, /device:TPU:1, one launch (start us, length us, event | category | flops | bytes accessed | tf_op | source)
XLA Modules:
  0.0 110.0 jit_solution(16845551973175207969)
XLA Ops:
  0.0 1.0 dynamic-slice_bitcast_fusion.1
  1.0 3.3 %collective-permute-start = (bf16[64,1024]{1,0:T(8,128)(2,1)S(1)}, bf16[64,1024]{1,0:T(8,128)(2,1)S(1)}, u32[]{:S(2)}, u32[]{:S(2)}) collective-permute-start(bf16[64,1024]{1,0:T(8,128)(2,1)S(1)} %get-tuple-element.60), channel_id=1, source_target_pairs={{0,1},{1,0},{2,3},{3,2},{4,5},{5,4},{6,7},{7,6},{8,9},{9,8},{10,11... | collective-permute-start | bytes 393224 | tf_op jit(solution)/shard_map/ppermute | solution.py:41
  4.3 1.0 collective-permute-done
  5.4 2.3 %collective-permute-start.7 = (bf16[128,128]{1,0:T(8,128)(2,1)S(1)}, bf16[128,128]{1,0:T(8,128)(2,1)S(1)}, u32[]{:S(2)}, u32[]{:S(2)}) collective-permute-start(bf16[128,128]{1,0:T(8,128)(2,1)S(1)} %slice.24), channel_id=1, source_target_pairs={{1,0},{32,1},{33,32},{64,33},{65,64},{96,65},{97,96},{128,97},{129... | collective-permute-start | bytes 98312 | tf_op jit(solution)/shard_map/ppermute | solution.py:203
  8.4 2.9 %collective-permute-start.2 = (bf16[128,256]{1,0:T(8,128)(2,1)S(1)}, bf16[128,256]{1,0:T(8,128)(2,1)S(1)}, u32[]{:S(2)}, u32[]{:S(2)}) collective-permute-start(bf16[128,256]{1,0:T(8,128)(2,1)S(1)} %get-tuple-element.57), channel_id=1, source_target_pairs={{0,8},{1,9},{2,10},{3,11},{4,40},{5,41},{6,42},{7,43},{8,72},{9,73... | collective-permute-start | bytes 196616 | tf_op jit(solution)/shard_map/ppermute | solution.py:201
  11.2 9.6 %collective-permute-start.3 = (bf16[128,256]{1,0:T(8,128)(2,1)S(1)}, bf16[128,256]{1,0:T(8,128)(2,1)S(1)}, u32[]{:S(2)}, u32[]{:S(2)}) collective-permute-start(bf16[128,256]{1,0:T(8,128)(2,1)S(1)} %get-tuple-element.56), channel_id=1, source_target_pairs={{0,16},{1,17},{2,18},{3,19},{4,48},{5,49},{6,50},{7,51},{8,80},{9,... | collective-permute-start | bytes 196616 | tf_op jit(solution)/shard_map/ppermute | solution.py:201
  20.9 2.1 %collective-permute-start.4 = (bf16[128,256]{1,0:T(8,128)(2,1)S(1)}, bf16[128,256]{1,0:T(8,128)(2,1)S(1)}, u32[]{:S(2)}, u32[]{:S(2)}) collective-permute-start(bf16[128,256]{1,0:T(8,128)(2,1)S(1)} %get-tuple-element.55), channel_id=1, source_target_pairs={{0,24},{1,25},{2,26},{3,27},{4,56},{5,57},{6,58},{7,59},{8,88},{9,... | collective-permute-start | bytes 196616 | tf_op jit(solution)/shard_map/ppermute | solution.py:201
  23.0 4.9 %collective-permute-start.8 = (bf16[128,1152]{1,0:T(8,128)(2,1)S(1)}, bf16[128,1152]{1,0:T(8,128)(2,1)S(1)}, u32[]{:S(2)}, u32[]{:S(2)}) collective-permute-start(bf16[128,1152]{1,0:T(8,128)(2,1)S(1)} %get-tuple-element.54), channel_id=1, source_target_pairs={{0,32},{32,0},{1,33},{33,1},{2,34},{34,2},{3,35},{35,3},{4,36},{36... | collective-permute-start | bytes 884744 | tf_op jit(solution)/shard_map/ppermute | solution.py:41
  27.9 6.7 %collective-permute-done.8 = bf16[128,1152]{1,0:T(8,128)(2,1)S(1)} collective-permute-done((bf16[128,1152]{1,0:T(8,128)(2,1)S(1)}, bf16[128,1152]{1,0:T(8,128)(2,1)S(1)}, u32[]{:S(2)}, u32[]{:S(2)}) %collective-permute-start.8) | collective-permute-done | bytes 294944 | tf_op jit(solution)/shard_map/ppermute | solution.py:41
  34.8 5.4 %collective-permute-start.5 = (bf16[128,1024]{1,0:T(8,128)(2,1)S(1)}, bf16[128,1024]{1,0:T(8,128)(2,1)S(1)}, u32[]{:S(2)}, u32[]{:S(2)}) collective-permute-start(bf16[128,1024]{1,0:T(8,128)(2,1)S(1)} %constant_dynamic-update-slice_fusion.refs_4_), channel_id=1, source_target_pairs={{8,0},{16,8},{24,16},{0,24},{9,1},{17,9},{25,17},{1,25},{10,2},{18... | collective-permute-start | bytes 786440 | tf_op jit(solution)/shard_map/ppermute | solution.py:37
  40.2 2.0 %collective-permute-start.10 = (bf16[128,1024]{1,0:T(8,128)(2,1)S(1)}, bf16[128,1024]{1,0:T(8,128)(2,1)S(1)}, u32[]{:S(2)}, u32[]{:S(2)}) collective-permute-start(bf16[128,1024]{1,0:T(8,128)(2,1)S(1)} %constant_dynamic-update-slice_fusion.refs_4_), channel_id=1, source_target_pairs={{0,6},{2,4},{4,2},{6,0},{1,7},{3,5},{5,3},{7,1},{8,14},{10,12},{12... | collective-permute-start | bytes 786440 | tf_op jit(solution)/shard_map/ppermute | solution.py:41
  42.2 8.5 %collective-permute-done.5.refs_0_.refs_8_ = bf16[128,1024]{1,0:T(8,128)(2,1)S(1)} collective-permute-done((bf16[128,1024]{1,0:T(8,128)(2,1)S(1)}, bf16[128,1024]{1,0:T(8,128)(2,1)S(1)}, u32[]{:S(2)}, u32[]{:S(2)}) %collective-permute-start.5) | collective-permute-done | bytes 262176 | tf_op jit(solution)/shard_map/ppermute | solution.py:37
  50.7 3.3 %collective-permute-done.6.refs_1_.refs_10_ = bf16[128,1024]{1,0:T(8,128)(2,1)S(1)} collective-permute-done((bf16[128,1024]{1,0:T(8,128)(2,1)S(1)}, bf16[128,1024]{1,0:T(8,128)(2,1)S(1)}, u32[]{:S(2)}, u32[]{:S(2)}) %collective-permute-start.6) | collective-permute-done | bytes 262176 | tf_op jit(solution)/shard_map/ppermute | solution.py:37
  54.9 1.0 collective-permute-start.13
  57.4 1.3 %collective-permute-start.12 = (bf16[256,1024]{1,0:T(8,128)(2,1)S(1)}, bf16[256,1024]{1,0:T(8,128)(2,1)S(1)}, u32[]{:S(2)}, u32[]{:S(2)}) collective-permute-start(bf16[256,1024]{1,0:T(8,128)(2,1)S(1)} %get-tuple-element.34), channel_id=1, source_target_pairs={{0,2},{2,0},{4,6},{6,4},{1,3},{3,1},{5,7},{7,5},{8,10},{10,8},{12,... | collective-permute-start | bytes 1572872 | tf_op jit(solution)/shard_map/ppermute | solution.py:41
  58.7 3.4 %collective-permute-start.14 = (bf16[128,1024]{1,0:T(8,128)(2,1)S(1)}, bf16[128,1024]{1,0:T(8,128)(2,1)S(1)}, u32[]{:S(2)}, u32[]{:S(2)}) collective-permute-start(bf16[128,1024]{1,0:T(8,128)(2,1)S(1)} %constant_dynamic-update-slice_fusion.refs_4_), channel_id=1, source_target_pairs={{16,0},{24,8},{0,16},{8,24},{17,1},{25,9},{1,17},{9,25},{18,2},{26... | collective-permute-start | bytes 786440 | tf_op jit(solution)/shard_map/ppermute | solution.py:37
  62.1 14.1 %collective-permute-done.14.refs_0_.refs_7_ = bf16[128,1024]{1,0:T(8,128)(2,1)S(1)} collective-permute-done((bf16[128,1024]{1,0:T(8,128)(2,1)S(1)}, bf16[128,1024]{1,0:T(8,128)(2,1)S(1)}, u32[]{:S(2)}, u32[]{:S(2)}) %collective-permute-start.14) | collective-permute-done | bytes 262176 | tf_op jit(solution)/shard_map/ppermute | solution.py:37
  76.3 1.1 %shard_map.18 = (bf16[256,1024]{1,0:T(8,128)(2,1)}, bf16[256,1024]{1,0:T(8,128)(2,1)}) custom-call(bf16[128,1024]{1,0:T(8,128)(2,1)S(1)} %collective-permute-done.14.refs_0_.refs_7_, bf16[384,1024]{1,0:T(8,128)(2,1)S(1)} %collective-permute-done.13.refs_1_.refs_6_.refs_5_, bf16[256,1024]{1,0:T(8,128)(2,1)S(1)} %collective-permute-done.12.refs_2_.refs_9_), custom_call_target="tpu_custom_call" | custom-call | bytes 1048576 | tf_op jit(solution)/shard_map/pallas_call | solution.py:177
  77.9 1.7 %collective-permute-start.18 = (bf16[256,1024]{1,0:T(8,128)(2,1)}, bf16[256,1024]{1,0:T(8,128)(2,1)S(1)}, u32[]{:S(2)}, u32[]{:S(2)}) collective-permute-start(bf16[256,1024]{1,0:T(8,128)(2,1)} %get-tuple-element.47), channel_id=1, source_target_pairs={{0,6},{2,4},{4,2},{6,0},{1,7},{3,5},{5,3},{7,1},{8,14},{10,12},{12... | collective-permute-start | bytes 1572872 | tf_op jit(solution)/shard_map/ppermute | solution.py:41
  79.7 1.1 %copy-done.1 = bf16[384,1024]{1,0:T(8,128)(2,1)S(1)} copy-done((bf16[384,1024]{1,0:T(8,128)(2,1)S(1)}, bf16[384,1024]{1,0:T(8,128)(2,1)}, u32[]{:S(2)}) %copy-start.1) | copy-done | bytes 786456
  80.8 0.9 copy-done.4
  81.8 0.9 copy-done.6
  82.7 0.9 copy-done.8
  83.7 0.9 copy-done.12
  84.6 0.9 copy-done.14
  85.6 8.3 %shard_map.19.refs_8_ = f32[2048,256]{1,0:T(8,128)S(1)} custom-call(s32[5]{0:T(128)S(1)} %stack.32.ix, bf16[2,128,1152]{2,1,0:T(8,128)(2,1)S(1)} %pad_maximum_fusion.refs_0_, bf16[2,128,1152]{2,1,0:T(8,128)(2,1)S(1)} %collective-permute-done.15.refs_1_, bf16[2,128,1152]{2,1,0:T(8,128)(2,1)S(1)} %collective-permute-done.16.refs_2_, ...), custom_call_target="tpu_custom_call" | custom-call | flops 4294967296 | bytes 4194304 | tf_op jit(solution)/shard_map/pallas_call | solution.py:137
  94.8 1.1 %collective-permute-start.19 = (bf16[64,1024]{1,0:T(8,128)(2,1)S(1)}, bf16[64,1024]{1,0:T(8,128)(2,1)S(1)}, u32[]{:S(2)}, u32[]{:S(2)}) collective-permute-start(bf16[64,1024]{1,0:T(8,128)(2,1)S(1)} %get-tuple-element.51), channel_id=1, source_target_pairs={{0,6},{2,4},{4,2},{6,0},{1,7},{3,5},{5,3},{7,1},{8,14},{10,12},{12... | collective-permute-start | bytes 393224 | tf_op jit(solution)/shard_map/ppermute | solution.py:41
  95.9 6.7 %shard_map.21.refs_7_ = f32[2048,256]{1,0:T(8,128)S(1)} custom-call(s32[5]{0:T(128)S(1)} %stack.32.ix, bf16[2,128,1152]{2,1,0:T(8,128)(2,1)S(1)} %pad_maximum_fusion.refs_0_, bf16[2,128,1152]{2,1,0:T(8,128)(2,1)S(1)} %collective-permute-done.15.refs_1_, bf16[2,128,1152]{2,1,0:T(8,128)(2,1)S(1)} %collective-permute-done.16.refs_2_, ...), custom_call_target="tpu_custom_call", output_to_operand_aliasing={{}: (9, {})} | custom-call | flops 3221225472 | bytes 3145728 | tf_op jit(solution)/shard_map/pallas_call | solution.py:137
  102.7 2.1 %shard_map.23 = f32[16,64,256]{2,1,0:T(8,128)S(1)} custom-call(s32[5]{0:T(128)S(1)} %stack.32.ix, bf16[2,128,1152]{2,1,0:T(8,128)(2,1)S(1)} %pad_maximum_fusion.refs_0_, bf16[2,128,1152]{2,1,0:T(8,128)(2,1)S(1)} %collective-permute-done.15.refs_1_, bf16[2,128,1152]{2,1,0:T(8,128)(2,1)S(1)} %collective-permute-done.16.refs_2_, ...), custom_call_target="tpu_custom_call" | custom-call | flops 1073741824 | bytes 1048576 | tf_op jit(solution)/shard_map/pallas_call | solution.py:137
  104.8 1.9 %collective-permute-start.21 = (f32[16,64,256]{2,1,0:T(8,128)S(1)}, f32[16,64,256]{2,1,0:T(8,128)S(1)}, u32[]{:S(2)}, u32[]{:S(2)}) collective-permute-start(f32[16,64,256]{2,1,0:T(8,128)S(1)} %shard_map.23), channel_id=1, source_target_pairs={{0,1},{1,0},{2,3},{3,2},{4,5},{5,4},{6,7},{7,6},{8,9},{9,8},{10,11... | collective-permute-start | bytes 3145736 | tf_op jit(solution)/shard_map/ppermute | solution.py:41
  106.6 2.1 %shard_map.22 = f32[16,64,256]{2,1,0:T(8,128)S(1)} custom-call(s32[5]{0:T(128)S(1)} %stack.32.ix, bf16[2,128,1152]{2,1,0:T(8,128)(2,1)S(1)} %pad_maximum_fusion.refs_0_, bf16[2,128,1152]{2,1,0:T(8,128)(2,1)S(1)} %collective-permute-done.15.refs_1_, bf16[2,128,1152]{2,1,0:T(8,128)(2,1)S(1)} %collective-permute-done.16.refs_2_, ...), custom_call_target="tpu_custom_call" | custom-call | flops 1073741824 | bytes 1048576 | tf_op jit(solution)/shard_map/pallas_call | solution.py:137
  108.9 1.1 %add.11 = f32[16,64,256]{2,1,0:T(8,128)} add(f32[16,64,256]{2,1,0:T(8,128)S(1)} %shard_map.22, f32[16,64,256]{2,1,0:T(8,128)S(1)} %collective-permute-done.21) | non-fusion elementwise | flops 262144 | bytes 3145728 | tf_op jit(solution)/shard_map/add | solution.py:254
  (61 shorter events, 5.1 us)
Async XLA Ops:
  1.0 4.3 %collective-permute-start = (bf16[64,1024]{1,0:T(8,128)(2,1)S(1)}, bf16[64,1024]{1,0:T(8,128)(2,1)S(1)}, u32[]{:S(2)}, u32[]{:S(2)}) collective-permute-start(bf16[64,1024]{1,0:T(8,128)(2,1)S(1)} %get-tuple-element.60), channel_id=1, source_target_pairs={{0,1},{1,0},{2,3},{3,2},{4,5},{5,4},{6,7},{7,6},{8,9},{9,8},{10,11... | collective-permute-start | bytes 393224 | tf_op jit(solution)/shard_map/ppermute | solution.py:41
  5.4 17.5 %collective-permute-start.7 = (bf16[128,128]{1,0:T(8,128)(2,1)S(1)}, bf16[128,128]{1,0:T(8,128)(2,1)S(1)}, u32[]{:S(2)}, u32[]{:S(2)}) collective-permute-start(bf16[128,128]{1,0:T(8,128)(2,1)S(1)} %slice.24), channel_id=1, source_target_pairs={{1,0},{32,1},{33,32},{64,33},{65,64},{96,65},{97,96},{128,97},{129... | collective-permute-start | bytes 98312 | tf_op jit(solution)/shard_map/ppermute | solution.py:203
  7.7 20.1 %collective-permute-start.1 = (bf16[128,256]{1,0:T(8,128)(2,1)S(1)}, bf16[128,256]{1,0:T(8,128)(2,1)S(1)}, u32[]{:S(2)}, u32[]{:S(2)}) collective-permute-start(bf16[128,256]{1,0:T(8,128)(2,1)S(1)} %get-tuple-element.58), channel_id=1, source_target_pairs={{0,0},{1,1},{2,2},{3,3},{4,32},{5,33},{6,34},{7,35},{8,64},{9,65},... | collective-permute-start | bytes 196616 | tf_op jit(solution)/shard_map/ppermute | solution.py:201
  8.4 19.5 %collective-permute-start.2 = (bf16[128,256]{1,0:T(8,128)(2,1)S(1)}, bf16[128,256]{1,0:T(8,128)(2,1)S(1)}, u32[]{:S(2)}, u32[]{:S(2)}) collective-permute-start(bf16[128,256]{1,0:T(8,128)(2,1)S(1)} %get-tuple-element.57), channel_id=1, source_target_pairs={{0,8},{1,9},{2,10},{3,11},{4,40},{5,41},{6,42},{7,43},{8,72},{9,73... | collective-permute-start | bytes 196616 | tf_op jit(solution)/shard_map/ppermute | solution.py:201
  11.2 16.6 %collective-permute-start.3 = (bf16[128,256]{1,0:T(8,128)(2,1)S(1)}, bf16[128,256]{1,0:T(8,128)(2,1)S(1)}, u32[]{:S(2)}, u32[]{:S(2)}) collective-permute-start(bf16[128,256]{1,0:T(8,128)(2,1)S(1)} %get-tuple-element.56), channel_id=1, source_target_pairs={{0,16},{1,17},{2,18},{3,19},{4,48},{5,49},{6,50},{7,51},{8,80},{9,... | collective-permute-start | bytes 196616 | tf_op jit(solution)/shard_map/ppermute | solution.py:201
  20.9 7.0 %collective-permute-start.4 = (bf16[128,256]{1,0:T(8,128)(2,1)S(1)}, bf16[128,256]{1,0:T(8,128)(2,1)S(1)}, u32[]{:S(2)}, u32[]{:S(2)}) collective-permute-start(bf16[128,256]{1,0:T(8,128)(2,1)S(1)} %get-tuple-element.55), channel_id=1, source_target_pairs={{0,24},{1,25},{2,26},{3,27},{4,56},{5,57},{6,58},{7,59},{8,88},{9,... | collective-permute-start | bytes 196616 | tf_op jit(solution)/shard_map/ppermute | solution.py:201
  23.0 11.7 %collective-permute-start.8 = (bf16[128,1152]{1,0:T(8,128)(2,1)S(1)}, bf16[128,1152]{1,0:T(8,128)(2,1)S(1)}, u32[]{:S(2)}, u32[]{:S(2)}) collective-permute-start(bf16[128,1152]{1,0:T(8,128)(2,1)S(1)} %get-tuple-element.54), channel_id=1, source_target_pairs={{0,32},{32,0},{1,33},{33,1},{2,34},{34,2},{3,35},{35,3},{4,36},{36... | collective-permute-start | bytes 884744 | tf_op jit(solution)/shard_map/ppermute | solution.py:41
  27.9 49.9 %copy-start.11 = (bf16[128,1024]{1,0:T(8,128)(2,1)}, bf16[128,1024]{1,0:T(8,128)(2,1)S(1)}, u32[]{:S(2)}) copy-start(bf16[128,1024]{1,0:T(8,128)(2,1)S(1)} %constant_dynamic-update-slice_fusion.refs_4_) | copy-start | bytes 786436
  34.7 20.0 %collective-permute-start.11 = (bf16[2,128,1152]{2,1,0:T(8,128)(2,1)S(1)}, bf16[2,128,1152]{2,1,0:T(8,128)(2,1)S(1)}, u32[]{:S(2)}, u32[]{:S(2)}) collective-permute-start(bf16[2,128,1152]{2,1,0:T(8,128)(2,1)S(1)} %pad_maximum_fusion.refs_0_), channel_id=1, source_target_pairs={{128,0},{192,64},{0,128},{64,192},{129,1},{193,65},{1,129},{65,193... | collective-permute-start | bytes 1769480 | tf_op jit(solution)/shard_map/ppermute | solution.py:37
  34.8 15.9 %collective-permute-start.5 = (bf16[128,1024]{1,0:T(8,128)(2,1)S(1)}, bf16[128,1024]{1,0:T(8,128)(2,1)S(1)}, u32[]{:S(2)}, u32[]{:S(2)}) collective-permute-start(bf16[128,1024]{1,0:T(8,128)(2,1)S(1)} %constant_dynamic-update-slice_fusion.refs_4_), channel_id=1, source_target_pairs={{8,0},{16,8},{24,16},{0,24},{9,1},{17,9},{25,17},{1,25},{10,2},{18... | collective-permute-start | bytes 786440 | tf_op jit(solution)/shard_map/ppermute | solution.py:37
  40.2 13.8 %collective-permute-start.6 = (bf16[128,1024]{1,0:T(8,128)(2,1)S(1)}, bf16[128,1024]{1,0:T(8,128)(2,1)S(1)}, u32[]{:S(2)}, u32[]{:S(2)}) collective-permute-start(bf16[128,1024]{1,0:T(8,128)(2,1)S(1)} %constant_dynamic-update-slice_fusion.refs_4_), channel_id=1, source_target_pairs={{24,0},{0,8},{8,16},{16,24},{25,1},{1,9},{9,17},{17,25},{26,2},{2,... | collective-permute-start | bytes 786440 | tf_op jit(solution)/shard_map/ppermute | solution.py:37
  40.2 13.8 %collective-permute-start.10 = (bf16[128,1024]{1,0:T(8,128)(2,1)S(1)}, bf16[128,1024]{1,0:T(8,128)(2,1)S(1)}, u32[]{:S(2)}, u32[]{:S(2)}) collective-permute-start(bf16[128,1024]{1,0:T(8,128)(2,1)S(1)} %constant_dynamic-update-slice_fusion.refs_4_), channel_id=1, source_target_pairs={{0,6},{2,4},{4,2},{6,0},{1,7},{3,5},{5,3},{7,1},{8,14},{10,12},{12... | collective-permute-start | bytes 786440 | tf_op jit(solution)/shard_map/ppermute | solution.py:41
  42.2 12.5 %collective-permute-start.9 = (bf16[128,1024]{1,0:T(8,128)(2,1)S(1)}, bf16[128,1024]{1,0:T(8,128)(2,1)S(1)}, u32[]{:S(2)}, u32[]{:S(2)}) collective-permute-start(bf16[128,1024]{1,0:T(8,128)(2,1)S(1)} %constant_dynamic-update-slice_fusion.refs_4_), channel_id=1, source_target_pairs={{0,2},{2,0},{4,6},{6,4},{1,3},{3,1},{5,7},{7,5},{8,10},{10,8},{12,... | collective-permute-start | bytes 786440 | tf_op jit(solution)/shard_map/ppermute | solution.py:41
  50.7 27.1 %copy-start.3 = (bf16[128,1024]{1,0:T(8,128)(2,1)}, bf16[128,1024]{1,0:T(8,128)(2,1)S(1)}, u32[]{:S(2)}) copy-start(bf16[128,1024]{1,0:T(8,128)(2,1)S(1)} %collective-permute-done.5.refs_0_.refs_8_) | copy-start | bytes 786436
  54.0 23.8 %copy-start.5 = (bf16[128,1024]{1,0:T(8,128)(2,1)}, bf16[128,1024]{1,0:T(8,128)(2,1)S(1)}, u32[]{:S(2)}) copy-start(bf16[128,1024]{1,0:T(8,128)(2,1)S(1)} %collective-permute-done.6.refs_1_.refs_10_) | copy-start | bytes 786436
  54.8 21.5 %copy-start.7 = (bf16[128,1024]{1,0:T(8,128)(2,1)}, bf16[128,1024]{1,0:T(8,128)(2,1)S(1)}, u32[]{:S(2)}) copy-start(bf16[128,1024]{1,0:T(8,128)(2,1)S(1)} %collective-permute-done.9.refs_2_.refs_5_) | copy-start | bytes 786436
  54.9 21.3 %collective-permute-start.13 = (bf16[384,1024]{1,0:T(8,128)(2,1)S(1)}, bf16[384,1024]{1,0:T(8,128)(2,1)S(1)}, u32[]{:S(2)}, u32[]{:S(2)}) collective-permute-start(bf16[384,1024]{1,0:T(8,128)(2,1)S(1)} %get-tuple-element.35), channel_id=1, source_target_pairs={{0,6},{2,4},{4,2},{6,0},{1,7},{3,5},{5,3},{7,1},{8,14},{10,12},{12... | collective-permute-start | bytes 2359304 | tf_op jit(solution)/shard_map/ppermute | solution.py:41
  55.9 20.3 %collective-permute-start.15 = (bf16[2,128,1152]{2,1,0:T(8,128)(2,1)S(1)}, bf16[2,128,1152]{2,1,0:T(8,128)(2,1)S(1)}, u32[]{:S(2)}, u32[]{:S(2)}) collective-permute-start(bf16[2,128,1152]{2,1,0:T(8,128)(2,1)S(1)} %pad_maximum_fusion.refs_0_), channel_id=1, source_target_pairs={{64,0},{128,64},{192,128},{0,192},{65,1},{129,65},{193,129},{1,193... | collective-permute-start | bytes 1769480 | tf_op jit(solution)/shard_map/ppermute | solution.py:37
  56.6 19.6 %collective-permute-start.16 = (bf16[2,128,1152]{2,1,0:T(8,128)(2,1)S(1)}, bf16[2,128,1152]{2,1,0:T(8,128)(2,1)S(1)}, u32[]{:S(2)}, u32[]{:S(2)}) collective-permute-start(bf16[2,128,1152]{2,1,0:T(8,128)(2,1)S(1)} %pad_maximum_fusion.refs_0_), channel_id=1, source_target_pairs={{192,0},{0,64},{64,128},{128,192},{193,1},{1,65},{65,129},{129,193... | collective-permute-start | bytes 1769480 | tf_op jit(solution)/shard_map/ppermute | solution.py:37
  57.4 18.8 %collective-permute-start.12 = (bf16[256,1024]{1,0:T(8,128)(2,1)S(1)}, bf16[256,1024]{1,0:T(8,128)(2,1)S(1)}, u32[]{:S(2)}, u32[]{:S(2)}) collective-permute-start(bf16[256,1024]{1,0:T(8,128)(2,1)S(1)} %get-tuple-element.34), channel_id=1, source_target_pairs={{0,2},{2,0},{4,6},{6,4},{1,3},{3,1},{5,7},{7,5},{8,10},{10,8},{12,... | collective-permute-start | bytes 1572872 | tf_op jit(solution)/shard_map/ppermute | solution.py:41
  58.7 17.5 %collective-permute-start.14 = (bf16[128,1024]{1,0:T(8,128)(2,1)S(1)}, bf16[128,1024]{1,0:T(8,128)(2,1)S(1)}, u32[]{:S(2)}, u32[]{:S(2)}) collective-permute-start(bf16[128,1024]{1,0:T(8,128)(2,1)S(1)} %constant_dynamic-update-slice_fusion.refs_4_), channel_id=1, source_target_pairs={{16,0},{24,8},{0,16},{8,24},{17,1},{25,9},{1,17},{9,25},{18,2},{26... | collective-permute-start | bytes 786440 | tf_op jit(solution)/shard_map/ppermute | solution.py:37
  76.2 1.7 %copy-start.9 = (bf16[128,1024]{1,0:T(8,128)(2,1)}, bf16[128,1024]{1,0:T(8,128)(2,1)S(1)}, u32[]{:S(2)}) copy-start(bf16[128,1024]{1,0:T(8,128)(2,1)S(1)} %collective-permute-done.14.refs_0_.refs_7_) | copy-start | bytes 786436
  76.2 1.6 %copy-start = (bf16[384,1024]{1,0:T(8,128)(2,1)}, bf16[384,1024]{1,0:T(8,128)(2,1)S(1)}, u32[]{:S(2)}) copy-start(bf16[384,1024]{1,0:T(8,128)(2,1)S(1)} %collective-permute-done.13.refs_1_.refs_6_.refs_5_) | copy-start | bytes 2359300
  77.4 16.5 %collective-permute-start.17 = (bf16[256,1024]{1,0:T(8,128)(2,1)}, bf16[256,1024]{1,0:T(8,128)(2,1)}, u32[]{:S(2)}, u32[]{:S(2)}) collective-permute-start(bf16[256,1024]{1,0:T(8,128)(2,1)} %get-tuple-element.46), channel_id=1, source_target_pairs={{0,2},{2,0},{4,6},{6,4},{1,3},{3,1},{5,7},{7,5},{8,10},{10,8},{12,... | collective-permute-start | bytes 1572872 | tf_op jit(solution)/shard_map/ppermute | solution.py:41
  77.9 16.0 %collective-permute-start.18 = (bf16[256,1024]{1,0:T(8,128)(2,1)}, bf16[256,1024]{1,0:T(8,128)(2,1)S(1)}, u32[]{:S(2)}, u32[]{:S(2)}) collective-permute-start(bf16[256,1024]{1,0:T(8,128)(2,1)} %get-tuple-element.47), channel_id=1, source_target_pairs={{0,6},{2,4},{4,2},{6,0},{1,7},{3,5},{5,3},{7,1},{8,14},{10,12},{12... | collective-permute-start | bytes 1572872 | tf_op jit(solution)/shard_map/ppermute | solution.py:41
  79.7 1.1 %copy-start.1 = (bf16[384,1024]{1,0:T(8,128)(2,1)S(1)}, bf16[384,1024]{1,0:T(8,128)(2,1)}, u32[]{:S(2)}) copy-start(bf16[384,1024]{1,0:T(8,128)(2,1)} %copy-done) | copy-start | bytes 2359300
  80.8 0.9 copy-start.4
  85.6 10.3 %copy-start.2 = (bf16[384,1024]{1,0:T(8,128)(2,1)S(1)}, bf16[384,1024]{1,0:T(8,128)(2,1)}, u32[]{:S(2)}) copy-start(bf16[384,1024]{1,0:T(8,128)(2,1)} %copy-done) | copy-start | bytes 2359300
  85.6 10.3 %copy-start.10 = (bf16[128,1024]{1,0:T(8,128)(2,1)S(1)}, bf16[128,1024]{1,0:T(8,128)(2,1)}, u32[]{:S(2)}) copy-start(bf16[128,1024]{1,0:T(8,128)(2,1)} %copy-done.9) | copy-start | bytes 786436
  94.8 7.9 %collective-permute-start.19 = (bf16[64,1024]{1,0:T(8,128)(2,1)S(1)}, bf16[64,1024]{1,0:T(8,128)(2,1)S(1)}, u32[]{:S(2)}, u32[]{:S(2)}) collective-permute-start(bf16[64,1024]{1,0:T(8,128)(2,1)S(1)} %get-tuple-element.51), channel_id=1, source_target_pairs={{0,6},{2,4},{4,2},{6,0},{1,7},{3,5},{5,3},{7,1},{8,14},{10,12},{12... | collective-permute-start | bytes 393224 | tf_op jit(solution)/shard_map/ppermute | solution.py:41
  95.9 6.8 %collective-permute-start.20 = (bf16[64,1024]{1,0:T(8,128)(2,1)S(1)}, bf16[64,1024]{1,0:T(8,128)(2,1)S(1)}, u32[]{:S(2)}, u32[]{:S(2)}) collective-permute-start(bf16[64,1024]{1,0:T(8,128)(2,1)S(1)} %get-tuple-element.52), channel_id=1, source_target_pairs={{0,2},{2,0},{4,6},{6,4},{1,3},{3,1},{5,7},{7,5},{8,10},{10,8},{12,... | collective-permute-start | bytes 393224 | tf_op jit(solution)/shard_map/ppermute | solution.py:41
  104.8 4.1 %collective-permute-start.21 = (f32[16,64,256]{2,1,0:T(8,128)S(1)}, f32[16,64,256]{2,1,0:T(8,128)S(1)}, u32[]{:S(2)}, u32[]{:S(2)}) collective-permute-start(f32[16,64,256]{2,1,0:T(8,128)S(1)} %shard_map.23), channel_id=1, source_target_pairs={{0,1},{1,0},{2,3},{3,2},{4,5},{5,4},{6,7},{7,6},{8,9},{9,8},{10,11... | collective-permute-start | bytes 3145736 | tf_op jit(solution)/shard_map/ppermute | solution.py:41
  (5 other events, 4.5 us)

commit v5 on v4

--- a/solution.py
+++ b/solution.py
@@ -41,6 +41,35 @@
     return lax.ppermute(value, axis, [(i, i ^ bits) for i in range(count)])
 
 
+def clear(ref):
+    ref[...] = jnp.zeros(ref.shape, ref.dtype)
+
+
+def heads_of(rows):
+    def head_kernel(*refs):
+        sources, target, sems = refs[:4], refs[4], refs[5]
+        copies = [
+            pltpu.make_async_copy(slabs.at[m, :, pl.ds(0, LANES)], target.at[2 * at + m], sems.at[2 * at + m])
+            for at, slabs in zip(ROWS_AT, sources)
+            for m in range(2)
+        ]
+        for copy in copies:
+            copy.start()
+        for copy in copies:
+            copy.wait()
+
+    anywhere = pl.BlockSpec(memory_space=pl.ANY)
+    return pl.pallas_call(
+        head_kernel,
+        out_shape=jax.ShapeDtypeStruct((8, CH, LANES), jnp.bfloat16),
+        in_specs=[anywhere] * 4,
+        out_specs=anywhere,
+        scratch_shapes=[pltpu.SemaphoreType.DMA((8,))],
+        compiler_params=pltpu.CompilerParams(vmem_limit_bytes=2**20),
+        cost_estimate=pl.CostEstimate(flops=0, bytes_accessed=2**19, transcendentals=0),
+    )(*rows)
+
+
 def lagged(wide, lags):
     shifted = [jnp.concatenate([window[:, lag : lag + QUARTER] for window in wide], axis=1) for lag in lags]
     return jnp.concatenate(shifted, axis=0)
@@ -51,24 +80,32 @@
 
     def kernel(ix, *refs):
         refs = list(refs)
-        rows = [refs.pop(0) for _ in OFFSETS]
+        rows, heads = [refs.pop(0) for _ in OFFSETS], refs.pop(0)
         arrays = [refs.pop(0) for _ in range(n_arrays)]
         before = None if first else refs.pop(0)
         total, windows, earlier, sems = refs
         x, zl, zh, y, c = (ix[i] for i in range(5))
         half = lax.rem(y, 2)
         away_zl = lax.select(lax.div(y, 2) == zl, 0, 1)
-        copies = []
+        copies, ends = [], []
         for i, (offset, pair, blocks) in enumerate(pieces):
             m = away_zl if pair == 0 else 1 - away_zl
             mine = []
             for q in range(4):
                 away = lax.rem(zh + offset - q - x + 8, 4)
+                width = QUARTER + LANES if q < 3 else QUARTER
                 for at, slabs in zip(ROWS_AT, rows):
-                    source = slabs.at[m, :, pl.ds(QUARTER * q, QUARTER + LANES)]
-                    copy = pltpu.make_async_copy(source, windows.at[i, q], sems.at[i, q])
+                    source = slabs.at[m, :, pl.ds(QUARTER * q, width)]
+                    copy = pltpu.make_async_copy(source, windows.at[i, q, :, pl.ds(0, width)], sems.at[i, q])
                     pl.when(away == at)(copy.start)
                 mine.append(copy)
+            zl_slab = lax.rem(zl + m, 2)
+            onward = c * zl_slab
+            head = 2 * lax.rem(away + onward, 4) + lax.select(c == 0, m, 1 - m)
+            copy = pltpu.make_async_copy(heads.at[head], windows.at[i, 3, :, pl.ds(QUARTER, LANES)], sems.at[i, 8])
+            copy.start()
+            mine.append(copy)
+            ends.append((onward == 1) & (lax.rem(zh + offset - 3 + 8, 4) == 3))
             for j, (parts, place) in enumerate(zip(blocks, (half, 1 - half))):
                 size = CH // len(parts)
                 for s, (number, index) in enumerate(parts):
@@ -82,6 +119,7 @@
             mine = c if share == "keep" else 1 - c
             for copy in copies[0]:
                 copy.wait()
+            pl.when(ends[0])(lambda: clear(windows.at[0, 3, :, pl.ds(QUARTER, LANES)]))
             wide = [windows[0, q, pl.ds(pl.multiple_of(mine * 64, 64), 64), :] for q in range(4)]
             for s in range(2):
                 part = lax.dot_general(
@@ -95,6 +133,7 @@
         for i in range(n):
             for copy in copies[i]:
                 copy.wait()
+            pl.when(ends[i])(lambda i=i: clear(windows.at[i, 3, :, pl.ds(QUARTER, LANES)]))
             wide = [windows[i, q] for q in range(4)]
             for s in range(4):
                 span = slice(512 * s, 512 * (s + 1))
@@ -132,15 +171,15 @@
     scratch = [
         pltpu.VMEM((n, 4, CH, QUARTER + LANES), jnp.bfloat16),
         pltpu.VMEM((n, 256, SPAN), jnp.bfloat16),
-        pltpu.SemaphoreType.DMA((n, 8)),
+        pltpu.SemaphoreType.DMA((n, 9)),
     ]
     return pl.pallas_call(
         make_kernel(plan, len(arrays), first, share),
         out_shape=half if share else sums,
-        in_specs=[pl.BlockSpec(memory_space=pltpu.SMEM)] + [anywhere] * (4 + len(arrays)) + ([] if first else [vmem]),
+        in_specs=[pl.BlockSpec(memory_space=pltpu.SMEM)] + [anywhere] * (5 + len(arrays)) + ([] if first else [vmem]),
         out_specs=vmem,
         scratch_shapes=scratch,
-        input_output_aliases={} if first or share else {5 + len(arrays): 0},
+        input_output_aliases={} if first or share else {6 + len(arrays): 0},
         compiler_params=pltpu.CompilerParams(vmem_limit_bytes=VLIM * 2**20),
         cost_estimate=pl.CostEstimate(flops=n * 2 * 2048 * 256 * 1024, bytes_accessed=n * 2**20, transcendentals=0),
     )(ix, *rows, *arrays, *([] if first else [before]))
@@ -200,9 +239,7 @@
     quarters = [
         lax.ppermute(block[:, QUARTER * q : QUARTER * (q + 1)], AXES, scatter_pairs(q)) for q in range(4)
     ]
-    head = lax.ppermute(block[:, :LANES], ("x", "zl", "c"), [(i, i - 1) for i in range(1, 16)])
-    slab = jnp.concatenate([block, head], axis=1)
-    slabs = jnp.stack([slab, swap(slab, "zl", 1, 2)])
+    slabs = jnp.stack([block, swap(block, "zl", 1, 2)])
     held = jnp.concatenate(quarters, axis=1)
 
     above, below = pull(held, "zh", 1, 4), pull(held, "zh", 3, 4)
@@ -221,6 +258,7 @@
     rows = [slabs, rows_1, rows_3, rows_2]
 
     via_1, via_3, across, *rows = lax.optimization_barrier((via_1, via_3, across, *rows))
+    rows = [*rows, swap(heads_of(rows), "c", 1, 2)]
     to_1, to_3 = pack([(across, 0, CH), (via_3, CH, CH)], [(across, 0, CH), (via_1, 0, CH)])
     late_1, late_3 = swap(to_1, "y", 1, 4), swap(to_3, "y", 3, 4)
 

time: 110 us -> 109 us (level)
  the two profiles are of different devices: /device:TPU:1 before, /device:TPU:15 now
where the time goes in v5:
time: 109 us
  starting transfers between devices  61 us (56%)
  Pallas kernels  22.5 us (21%)
  waiting for transfers between devices  15.8 us (14%)
  local copies, waits for them, and re-layouts  7.75 us (7%)
  other arithmetic  1.26 us (1%)
    ppermute x12, starting transfers between devices, swap(): return lax.ppermute(value, axis, [(i, i ^ bits) for i in range(count)])  34.2 us
    pallas_call x4, Pallas kernels, products(): pl.pallas_call(make_kernel(plan, len(arrays), first, share), out_shape=ha...  19.5 us
    ppermute x4, starting transfers between devices, on_device(): lax.ppermute(block[:, QUARTER * q:QUARTER * (q + 1)], AXES, scatter_pairs...  13.9 us
    ppermute x6, starting transfers between devices, pull(): lax.ppermute(value, axis, [((i + offset) % count, i) for i in range(count)])  12.9 us
    ppermute x6, waiting for transfers between devices, pull(): lax.ppermute(value, axis, [((i + offset) % count, i) for i in range(count)])  7.99 us
    unnamed x33, local copies, waits for them, and re-layouts  6.64 us
    ppermute x12, waiting for transfers between devices, swap(): return lax.ppermute(value, axis, [(i, i ^ bits) for i in range(count)])  5.18 us
    ppermute x4, waiting for transfers between devices, on_device(): lax.ppermute(block[:, QUARTER * q:QUARTER * (q + 1)], AXES, scatter_pairs...  2.64 us
  transfers between devices with their start and end apart: 22, of which 6 were waited for; matrix products, arithmetic and copies ran while one was open for 0% of the time, Pallas kernels for 17%

profile of v5, /device:TPU:15, one launch (start us, length us, event | category | flops | bytes accessed | tf_op | source)
XLA Modules:
  0.0 108.6 jit_solution(1840964832492150943)
XLA Ops:
  0.0 1.0 dynamic-slice_bitcast_fusion.1
  1.8 1.0 collective-permute-done
  2.8 1.7 %collective-permute-start.7 = (bf16[128,1024]{1,0:T(8,128)(2,1)S(1)}, bf16[128,1024]{1,0:T(8,128)(2,1)S(1)}, u32[]{:S(2)}, u32[]{:S(2)}) collective-permute-start(bf16[128,1024]{1,0:T(8,128)(2,1)S(1)} %maximum_select_fusion), channel_id=1, source_target_pairs={{0,32},{32,0},{1,33},{33,1},{2,34},{34,2},{3,35},{35,3},{4,36},{36... | collective-permute-start | bytes 786440 | tf_op jit(solution)/shard_map/ppermute | solution.py:41
  4.6 6.9 %collective-permute-start.1 = (bf16[128,256]{1,0:T(8,128)(2,1)S(1)}, bf16[128,256]{1,0:T(8,128)(2,1)S(1)}, u32[]{:S(2)}, u32[]{:S(2)}) collective-permute-start(bf16[128,256]{1,0:T(8,128)(2,1)S(1)} %get-tuple-element.59), channel_id=1, source_target_pairs={{0,0},{1,1},{2,2},{3,3},{4,32},{5,33},{6,34},{7,35},{8,64},{9,65},... | collective-permute-start | bytes 196616 | tf_op jit(solution)/shard_map/ppermute | solution.py:240
  11.7 6.8 %collective-permute-start.4 = (bf16[128,256]{1,0:T(8,128)(2,1)S(1)}, bf16[128,256]{1,0:T(8,128)(2,1)S(1)}, u32[]{:S(2)}, u32[]{:S(2)}) collective-permute-start(bf16[128,256]{1,0:T(8,128)(2,1)S(1)} %get-tuple-element.56), channel_id=1, source_target_pairs={{0,24},{1,25},{2,26},{3,27},{4,56},{5,57},{6,58},{7,59},{8,88},{9,... | collective-permute-start | bytes 196616 | tf_op jit(solution)/shard_map/ppermute | solution.py:240
  18.5 1.3 %collective-permute-done.1 = bf16[128,256]{1,0:T(8,128)(2,1)S(1)} collective-permute-done((bf16[128,256]{1,0:T(8,128)(2,1)S(1)}, bf16[128,256]{1,0:T(8,128)(2,1)S(1)}, u32[]{:S(2)}, u32[]{:S(2)}) %collective-permute-start.1) | collective-permute-done | bytes 65568 | tf_op jit(solution)/shard_map/ppermute | solution.py:240
  19.9 1.3 %collective-permute-done.4 = bf16[128,256]{1,0:T(8,128)(2,1)S(1)} collective-permute-done((bf16[128,256]{1,0:T(8,128)(2,1)S(1)}, bf16[128,256]{1,0:T(8,128)(2,1)S(1)}, u32[]{:S(2)}, u32[]{:S(2)}) %collective-permute-start.4) | collective-permute-done | bytes 65568 | tf_op jit(solution)/shard_map/ppermute | solution.py:240
  21.3 4.1 %collective-permute-start.10 = (bf16[2,128,1024]{2,1,0:T(8,128)(2,1)S(1)}, bf16[2,128,1024]{2,1,0:T(8,128)(2,1)S(1)}, u32[]{:S(2)}, u32[]{:S(2)}) collective-permute-start(bf16[2,128,1024]{2,1,0:T(8,128)(2,1)S(1)} %pad_maximum_fusion.refs_0_), channel_id=1, source_target_pairs={{128,0},{192,64},{0,128},{64,192},{129,1},{193,65},{1,129},{65,193... | collective-permute-start | bytes 1572872 | tf_op jit(solution)/shard_map/ppermute | solution.py:37
  25.4 1.0 collective-permute-start.5
  26.3 1.4 %collective-permute-start.6 = (bf16[128,1024]{1,0:T(8,128)(2,1)S(1)}, bf16[128,1024]{1,0:T(8,128)(2,1)S(1)}, u32[]{:S(2)}, u32[]{:S(2)}) collective-permute-start(bf16[128,1024]{1,0:T(8,128)(2,1)S(1)} %constant_dynamic-update-slice_fusion.refs_5_), channel_id=1, source_target_pairs={{24,0},{0,8},{8,16},{16,24},{25,1},{1,9},{9,17},{17,25},{26,2},{2,... | collective-permute-start | bytes 786440 | tf_op jit(solution)/shard_map/ppermute | solution.py:37
  27.9 7.4 %collective-permute-start.9 = (bf16[128,1024]{1,0:T(8,128)(2,1)S(1)}, bf16[128,1024]{1,0:T(8,128)(2,1)S(1)}, u32[]{:S(2)}, u32[]{:S(2)}) collective-permute-start(bf16[128,1024]{1,0:T(8,128)(2,1)S(1)} %constant_dynamic-update-slice_fusion.refs_5_), channel_id=1, source_target_pairs={{0,6},{2,4},{4,2},{6,0},{1,7},{3,5},{5,3},{7,1},{8,14},{10,12},{12... | collective-permute-start | bytes 786440 | tf_op jit(solution)/shard_map/ppermute | solution.py:41
  35.4 4.0 %collective-permute-done.9.refs_8_ = bf16[128,1024]{1,0:T(8,128)(2,1)S(1)} collective-permute-done((bf16[128,1024]{1,0:T(8,128)(2,1)S(1)}, bf16[128,1024]{1,0:T(8,128)(2,1)S(1)}, u32[]{:S(2)}, u32[]{:S(2)}) %collective-permute-start.9) | collective-permute-done | bytes 262176 | tf_op jit(solution)/shard_map/ppermute | solution.py:41
  40.2 1.6 %collective-permute-start.12 = (bf16[384,1024]{1,0:T(8,128)(2,1)S(1)}, bf16[384,1024]{1,0:T(8,128)(2,1)S(1)}, u32[]{:S(2)}, u32[]{:S(2)}) collective-permute-start(bf16[384,1024]{1,0:T(8,128)(2,1)S(1)} %get-tuple-element.35), channel_id=1, source_target_pairs={{0,6},{2,4},{4,2},{6,0},{1,7},{3,5},{5,3},{7,1},{8,14},{10,12},{12... | collective-permute-start | bytes 2359304 | tf_op jit(solution)/shard_map/ppermute | solution.py:41
  41.8 1.5 %collective-permute-start.11 = (bf16[256,1024]{1,0:T(8,128)(2,1)S(1)}, bf16[256,1024]{1,0:T(8,128)(2,1)S(1)}, u32[]{:S(2)}, u32[]{:S(2)}) collective-permute-start(bf16[256,1024]{1,0:T(8,128)(2,1)S(1)} %get-tuple-element.34), channel_id=1, source_target_pairs={{0,2},{2,0},{4,6},{6,4},{1,3},{3,1},{5,7},{7,5},{8,10},{10,8},{12,... | collective-permute-start | bytes 1572872 | tf_op jit(solution)/shard_map/ppermute | solution.py:41
  43.3 1.2 %collective-permute-start.14 = (bf16[2,128,1024]{2,1,0:T(8,128)(2,1)S(1)}, bf16[2,128,1024]{2,1,0:T(8,128)(2,1)S(1)}, u32[]{:S(2)}, u32[]{:S(2)}) collective-permute-start(bf16[2,128,1024]{2,1,0:T(8,128)(2,1)S(1)} %pad_maximum_fusion.refs_0_), channel_id=1, source_target_pairs={{64,0},{128,64},{192,128},{0,192},{65,1},{129,65},{193,129},{1,193... | collective-permute-start | bytes 1572872 | tf_op jit(solution)/shard_map/ppermute | solution.py:37
  44.5 1.5 %collective-permute-start.15 = (bf16[2,128,1024]{2,1,0:T(8,128)(2,1)S(1)}, bf16[2,128,1024]{2,1,0:T(8,128)(2,1)S(1)}, u32[]{:S(2)}, u32[]{:S(2)}) collective-permute-start(bf16[2,128,1024]{2,1,0:T(8,128)(2,1)S(1)} %pad_maximum_fusion.refs_0_), channel_id=1, source_target_pairs={{192,0},{0,64},{64,128},{128,192},{193,1},{1,65},{65,129},{129,193... | collective-permute-start | bytes 1572872 | tf_op jit(solution)/shard_map/ppermute | solution.py:37
  46.0 3.8 %collective-permute-start.13 = (bf16[128,1024]{1,0:T(8,128)(2,1)S(1)}, bf16[128,1024]{1,0:T(8,128)(2,1)S(1)}, u32[]{:S(2)}, u32[]{:S(2)}) collective-permute-start(bf16[128,1024]{1,0:T(8,128)(2,1)S(1)} %constant_dynamic-update-slice_fusion.refs_5_), channel_id=1, source_target_pairs={{16,0},{24,8},{0,16},{8,24},{17,1},{25,9},{1,17},{9,25},{18,2},{26... | collective-permute-start | bytes 786440 | tf_op jit(solution)/shard_map/ppermute | solution.py:37
  49.7 8.0 %collective-permute-done.13.refs_0_.refs_8_ = bf16[128,1024]{1,0:T(8,128)(2,1)S(1)} collective-permute-done((bf16[128,1024]{1,0:T(8,128)(2,1)S(1)}, bf16[128,1024]{1,0:T(8,128)(2,1)S(1)}, u32[]{:S(2)}, u32[]{:S(2)}) %collective-permute-start.13) | collective-permute-done | bytes 262176 | tf_op jit(solution)/shard_map/ppermute | solution.py:37
  58.6 15.6 %collective-permute-start.16 = (bf16[8,128,128]{2,1,0:T(8,128)(2,1)}, bf16[8,128,128]{2,1,0:T(8,128)(2,1)S(1)}, u32[]{:S(2)}, u32[]{:S(2)}) collective-permute-start(bf16[8,128,128]{2,1,0:T(8,128)(2,1)} %shard_map.18), channel_id=1, source_target_pairs={{0,1},{1,0},{2,3},{3,2},{4,5},{5,4},{6,7},{7,6},{8,9},{9,8},{10,11... | collective-permute-start | bytes 786440 | tf_op jit(solution)/shard_map/ppermute | solution.py:41
  74.2 1.1 shard_map.19
  75.6 1.1 %copy-done.1 = bf16[384,1024]{1,0:T(8,128)(2,1)S(1)} copy-done((bf16[384,1024]{1,0:T(8,128)(2,1)S(1)}, bf16[384,1024]{1,0:T(8,128)(2,1)}, u32[]{:S(2)}) %copy-start.1) | copy-done | bytes 786456
  76.7 0.9 copy-done.4
  77.7 0.9 copy-done.6
  79.6 0.9 copy-done.12
  81.5 8.4 %shard_map.20.refs_9_ = f32[2048,256]{1,0:T(8,128)S(1)} custom-call(s32[5]{0:T(128)S(1)} %stack.30.ix, bf16[2,128,1024]{2,1,0:T(8,128)(2,1)S(1)} %pad_maximum_fusion.refs_0_, bf16[2,128,1024]{2,1,0:T(8,128)(2,1)S(1)} %collective-permute-done.14.refs_1_, bf16[2,128,1024]{2,1,0:T(8,128)(2,1)S(1)} %collective-permute-done.15.refs_2_, ...), custom_call_target="tpu_custom_call" | custom-call | flops 4294967296 | bytes 4194304 | tf_op jit(solution)/shard_map/pallas_call | solution.py:176
  90.9 1.6 %collective-permute-start.19 = (bf16[64,1024]{1,0:T(8,128)(2,1)S(1)}, bf16[64,1024]{1,0:T(8,128)(2,1)S(1)}, u32[]{:S(2)}, u32[]{:S(2)}) collective-permute-start(bf16[64,1024]{1,0:T(8,128)(2,1)S(1)} %get-tuple-element.51), channel_id=1, source_target_pairs={{0,6},{2,4},{4,2},{6,0},{1,7},{3,5},{5,3},{7,1},{8,14},{10,12},{12... | collective-permute-start | bytes 393224 | tf_op jit(solution)/shard_map/ppermute | solution.py:41
  92.4 2.5 %collective-permute-start.20 = (bf16[64,1024]{1,0:T(8,128)(2,1)S(1)}, bf16[64,1024]{1,0:T(8,128)(2,1)S(1)}, u32[]{:S(2)}, u32[]{:S(2)}) collective-permute-start(bf16[64,1024]{1,0:T(8,128)(2,1)S(1)} %get-tuple-element.52), channel_id=1, source_target_pairs={{0,2},{2,0},{4,6},{6,4},{1,3},{3,1},{5,7},{7,5},{8,10},{10,8},{12,... | collective-permute-start | bytes 393224 | tf_op jit(solution)/shard_map/ppermute | solution.py:41
  95.0 6.9 %shard_map.22.refs_8_ = f32[2048,256]{1,0:T(8,128)S(1)} custom-call(s32[5]{0:T(128)S(1)} %stack.30.ix, bf16[2,128,1024]{2,1,0:T(8,128)(2,1)S(1)} %pad_maximum_fusion.refs_0_, bf16[2,128,1024]{2,1,0:T(8,128)(2,1)S(1)} %collective-permute-done.14.refs_1_, bf16[2,128,1024]{2,1,0:T(8,128)(2,1)S(1)} %collective-permute-done.15.refs_2_, ...), custom_call_target="tpu_custom_call", output_to_operand_aliasing={{}: (10, {})} | custom-call | flops 3221225472 | bytes 3145728 | tf_op jit(solution)/shard_map/pallas_call | solution.py:176
  101.8 2.1 %shard_map.24 = f32[16,64,256]{2,1,0:T(8,128)S(1)} custom-call(s32[5]{0:T(128)S(1)} %stack.30.ix, bf16[2,128,1024]{2,1,0:T(8,128)(2,1)S(1)} %pad_maximum_fusion.refs_0_, bf16[2,128,1024]{2,1,0:T(8,128)(2,1)S(1)} %collective-permute-done.14.refs_1_, bf16[2,128,1024]{2,1,0:T(8,128)(2,1)S(1)} %collective-permute-done.15.refs_2_, ...), custom_call_target="tpu_custom_call" | custom-call | flops 1073741824 | bytes 1048576 | tf_op jit(solution)/shard_map/pallas_call | solution.py:176
  104.0 1.2 %collective-permute-start.21 = (f32[16,64,256]{2,1,0:T(8,128)S(1)}, f32[16,64,256]{2,1,0:T(8,128)S(1)}, u32[]{:S(2)}, u32[]{:S(2)}) collective-permute-start(f32[16,64,256]{2,1,0:T(8,128)S(1)} %shard_map.24), channel_id=1, source_target_pairs={{0,1},{1,0},{2,3},{3,2},{4,5},{5,4},{6,7},{7,6},{8,9},{9,8},{10,11... | collective-permute-start | bytes 3145736 | tf_op jit(solution)/shard_map/ppermute | solution.py:41
  105.2 2.1 %shard_map.23 = f32[16,64,256]{2,1,0:T(8,128)S(1)} custom-call(s32[5]{0:T(128)S(1)} %stack.30.ix, bf16[2,128,1024]{2,1,0:T(8,128)(2,1)S(1)} %pad_maximum_fusion.refs_0_, bf16[2,128,1024]{2,1,0:T(8,128)(2,1)S(1)} %collective-permute-done.14.refs_1_, bf16[2,128,1024]{2,1,0:T(8,128)(2,1)S(1)} %collective-permute-done.15.refs_2_, ...), custom_call_target="tpu_custom_call" | custom-call | flops 1073741824 | bytes 1048576 | tf_op jit(solution)/shard_map/pallas_call | solution.py:176
  107.5 1.1 %add.11 = f32[16,64,256]{2,1,0:T(8,128)} add(f32[16,64,256]{2,1,0:T(8,128)S(1)} %shard_map.23, f32[16,64,256]{2,1,0:T(8,128)S(1)} %collective-permute-done.21) | non-fusion elementwise | flops 262144 | bytes 3145728 | tf_op jit(solution)/shard_map/add | solution.py:292
  (61 shorter events, 6.3 us)
Async XLA Ops:
  1.0 1.7 %collective-permute-start = (bf16[64,1024]{1,0:T(8,128)(2,1)S(1)}, bf16[64,1024]{1,0:T(8,128)(2,1)S(1)}, u32[]{:S(2)}, u32[]{:S(2)}) collective-permute-start(bf16[64,1024]{1,0:T(8,128)(2,1)S(1)} %get-tuple-element.54), channel_id=1, source_target_pairs={{0,1},{1,0},{2,3},{3,2},{4,5},{5,4},{6,7},{7,6},{8,9},{9,8},{10,11... | collective-permute-start | bytes 393224 | tf_op jit(solution)/shard_map/ppermute | solution.py:41
  2.8 18.4 %collective-permute-start.7 = (bf16[128,1024]{1,0:T(8,128)(2,1)S(1)}, bf16[128,1024]{1,0:T(8,128)(2,1)S(1)}, u32[]{:S(2)}, u32[]{:S(2)}) collective-permute-start(bf16[128,1024]{1,0:T(8,128)(2,1)S(1)} %maximum_select_fusion), channel_id=1, source_target_pairs={{0,32},{32,0},{1,33},{33,1},{2,34},{34,2},{3,35},{35,3},{4,36},{36... | collective-permute-start | bytes 786440 | tf_op jit(solution)/shard_map/ppermute | solution.py:41
  4.6 15.3 %collective-permute-start.1 = (bf16[128,256]{1,0:T(8,128)(2,1)S(1)}, bf16[128,256]{1,0:T(8,128)(2,1)S(1)}, u32[]{:S(2)}, u32[]{:S(2)}) collective-permute-start(bf16[128,256]{1,0:T(8,128)(2,1)S(1)} %get-tuple-element.59), channel_id=1, source_target_pairs={{0,0},{1,1},{2,2},{3,3},{4,32},{5,33},{6,34},{7,35},{8,64},{9,65},... | collective-permute-start | bytes 196616 | tf_op jit(solution)/shard_map/ppermute | solution.py:240
  11.5 8.3 %collective-permute-start.2 = (bf16[128,256]{1,0:T(8,128)(2,1)S(1)}, bf16[128,256]{1,0:T(8,128)(2,1)S(1)}, u32[]{:S(2)}, u32[]{:S(2)}) collective-permute-start(bf16[128,256]{1,0:T(8,128)(2,1)S(1)} %get-tuple-element.58), channel_id=1, source_target_pairs={{0,8},{1,9},{2,10},{3,11},{4,40},{5,41},{6,42},{7,43},{8,72},{9,73... | collective-permute-start | bytes 196616 | tf_op jit(solution)/shard_map/ppermute | solution.py:240
  11.6 8.3 %collective-permute-start.3 = (bf16[128,256]{1,0:T(8,128)(2,1)S(1)}, bf16[128,256]{1,0:T(8,128)(2,1)S(1)}, u32[]{:S(2)}, u32[]{:S(2)}) collective-permute-start(bf16[128,256]{1,0:T(8,128)(2,1)S(1)} %get-tuple-element.57), channel_id=1, source_target_pairs={{0,16},{1,17},{2,18},{3,19},{4,48},{5,49},{6,50},{7,51},{8,80},{9,... | collective-permute-start | bytes 196616 | tf_op jit(solution)/shard_map/ppermute | solution.py:240
  11.7 9.5 %collective-permute-start.4 = (bf16[128,256]{1,0:T(8,128)(2,1)S(1)}, bf16[128,256]{1,0:T(8,128)(2,1)S(1)}, u32[]{:S(2)}, u32[]{:S(2)}) collective-permute-start(bf16[128,256]{1,0:T(8,128)(2,1)S(1)} %get-tuple-element.56), channel_id=1, source_target_pairs={{0,24},{1,25},{2,26},{3,27},{4,56},{5,57},{6,58},{7,59},{8,88},{9,... | collective-permute-start | bytes 196616 | tf_op jit(solution)/shard_map/ppermute | solution.py:240
  21.2 36.5 %copy-start.11 = (bf16[128,1024]{1,0:T(8,128)(2,1)}, bf16[128,1024]{1,0:T(8,128)(2,1)S(1)}, u32[]{:S(2)}) copy-start(bf16[128,1024]{1,0:T(8,128)(2,1)S(1)} %constant_dynamic-update-slice_fusion.refs_5_) | copy-start | bytes 786436
  21.3 18.8 %collective-permute-start.10 = (bf16[2,128,1024]{2,1,0:T(8,128)(2,1)S(1)}, bf16[2,128,1024]{2,1,0:T(8,128)(2,1)S(1)}, u32[]{:S(2)}, u32[]{:S(2)}) collective-permute-start(bf16[2,128,1024]{2,1,0:T(8,128)(2,1)S(1)} %pad_maximum_fusion.refs_0_), channel_id=1, source_target_pairs={{128,0},{192,64},{0,128},{64,192},{129,1},{193,65},{1,129},{65,193... | collective-permute-start | bytes 1572872 | tf_op jit(solution)/shard_map/ppermute | solution.py:37
  25.4 10.0 %collective-permute-start.5 = (bf16[128,1024]{1,0:T(8,128)(2,1)S(1)}, bf16[128,1024]{1,0:T(8,128)(2,1)S(1)}, u32[]{:S(2)}, u32[]{:S(2)}) collective-permute-start(bf16[128,1024]{1,0:T(8,128)(2,1)S(1)} %constant_dynamic-update-slice_fusion.refs_5_), channel_id=1, source_target_pairs={{8,0},{16,8},{24,16},{0,24},{9,1},{17,9},{25,17},{1,25},{10,2},{18... | collective-permute-start | bytes 786440 | tf_op jit(solution)/shard_map/ppermute | solution.py:37
  26.3 9.0 %collective-permute-start.6 = (bf16[128,1024]{1,0:T(8,128)(2,1)S(1)}, bf16[128,1024]{1,0:T(8,128)(2,1)S(1)}, u32[]{:S(2)}, u32[]{:S(2)}) collective-permute-start(bf16[128,1024]{1,0:T(8,128)(2,1)S(1)} %constant_dynamic-update-slice_fusion.refs_5_), channel_id=1, source_target_pairs={{24,0},{0,8},{8,16},{16,24},{25,1},{1,9},{9,17},{17,25},{26,2},{2,... | collective-permute-start | bytes 786440 | tf_op jit(solution)/shard_map/ppermute | solution.py:37
  27.7 7.6 %collective-permute-start.8 = (bf16[128,1024]{1,0:T(8,128)(2,1)S(1)}, bf16[128,1024]{1,0:T(8,128)(2,1)S(1)}, u32[]{:S(2)}, u32[]{:S(2)}) collective-permute-start(bf16[128,1024]{1,0:T(8,128)(2,1)S(1)} %constant_dynamic-update-slice_fusion.refs_5_), channel_id=1, source_target_pairs={{0,2},{2,0},{4,6},{6,4},{1,3},{3,1},{5,7},{7,5},{8,10},{10,8},{12,... | collective-permute-start | bytes 786440 | tf_op jit(solution)/shard_map/ppermute | solution.py:41
  27.9 11.5 %collective-permute-start.9 = (bf16[128,1024]{1,0:T(8,128)(2,1)S(1)}, bf16[128,1024]{1,0:T(8,128)(2,1)S(1)}, u32[]{:S(2)}, u32[]{:S(2)}) collective-permute-start(bf16[128,1024]{1,0:T(8,128)(2,1)S(1)} %constant_dynamic-update-slice_fusion.refs_5_), channel_id=1, source_target_pairs={{0,6},{2,4},{4,2},{6,0},{1,7},{3,5},{5,3},{7,1},{8,14},{10,12},{12... | collective-permute-start | bytes 786440 | tf_op jit(solution)/shard_map/ppermute | solution.py:41
  35.3 39.9 %copy-start.3 = (bf16[128,1024]{1,0:T(8,128)(2,1)}, bf16[128,1024]{1,0:T(8,128)(2,1)S(1)}, u32[]{:S(2)}) copy-start(bf16[128,1024]{1,0:T(8,128)(2,1)S(1)} %collective-permute-done.5.refs_0_.refs_9_) | copy-start | bytes 786436
  35.3 39.9 %copy-start.5 = (bf16[128,1024]{1,0:T(8,128)(2,1)}, bf16[128,1024]{1,0:T(8,128)(2,1)S(1)}, u32[]{:S(2)}) copy-start(bf16[128,1024]{1,0:T(8,128)(2,1)S(1)} %collective-permute-done.6.refs_1_.refs_11_) | copy-start | bytes 786436
  35.3 22.4 %copy-start.7 = (bf16[128,1024]{1,0:T(8,128)(2,1)}, bf16[128,1024]{1,0:T(8,128)(2,1)S(1)}, u32[]{:S(2)}) copy-start(bf16[128,1024]{1,0:T(8,128)(2,1)S(1)} %collective-permute-done.8.refs_2_.refs_6_) | copy-start | bytes 786436
  40.2 17.5 %collective-permute-start.12 = (bf16[384,1024]{1,0:T(8,128)(2,1)S(1)}, bf16[384,1024]{1,0:T(8,128)(2,1)S(1)}, u32[]{:S(2)}, u32[]{:S(2)}) collective-permute-start(bf16[384,1024]{1,0:T(8,128)(2,1)S(1)} %get-tuple-element.35), channel_id=1, source_target_pairs={{0,6},{2,4},{4,2},{6,0},{1,7},{3,5},{5,3},{7,1},{8,14},{10,12},{12... | collective-permute-start | bytes 2359304 | tf_op jit(solution)/shard_map/ppermute | solution.py:41
  41.8 15.9 %collective-permute-start.11 = (bf16[256,1024]{1,0:T(8,128)(2,1)S(1)}, bf16[256,1024]{1,0:T(8,128)(2,1)S(1)}, u32[]{:S(2)}, u32[]{:S(2)}) collective-permute-start(bf16[256,1024]{1,0:T(8,128)(2,1)S(1)} %get-tuple-element.34), channel_id=1, source_target_pairs={{0,2},{2,0},{4,6},{6,4},{1,3},{3,1},{5,7},{7,5},{8,10},{10,8},{12,... | collective-permute-start | bytes 1572872 | tf_op jit(solution)/shard_map/ppermute | solution.py:41
  43.3 14.4 %collective-permute-start.14 = (bf16[2,128,1024]{2,1,0:T(8,128)(2,1)S(1)}, bf16[2,128,1024]{2,1,0:T(8,128)(2,1)S(1)}, u32[]{:S(2)}, u32[]{:S(2)}) collective-permute-start(bf16[2,128,1024]{2,1,0:T(8,128)(2,1)S(1)} %pad_maximum_fusion.refs_0_), channel_id=1, source_target_pairs={{64,0},{128,64},{192,128},{0,192},{65,1},{129,65},{193,129},{1,193... | collective-permute-start | bytes 1572872 | tf_op jit(solution)/shard_map/ppermute | solution.py:37
  44.5 13.2 %collective-permute-start.15 = (bf16[2,128,1024]{2,1,0:T(8,128)(2,1)S(1)}, bf16[2,128,1024]{2,1,0:T(8,128)(2,1)S(1)}, u32[]{:S(2)}, u32[]{:S(2)}) collective-permute-start(bf16[2,128,1024]{2,1,0:T(8,128)(2,1)S(1)} %pad_maximum_fusion.refs_0_), channel_id=1, source_target_pairs={{192,0},{0,64},{64,128},{128,192},{193,1},{1,65},{65,129},{129,193... | collective-permute-start | bytes 1572872 | tf_op jit(solution)/shard_map/ppermute | solution.py:37
  46.0 11.7 %collective-permute-start.13 = (bf16[128,1024]{1,0:T(8,128)(2,1)S(1)}, bf16[128,1024]{1,0:T(8,128)(2,1)S(1)}, u32[]{:S(2)}, u32[]{:S(2)}) collective-permute-start(bf16[128,1024]{1,0:T(8,128)(2,1)S(1)} %constant_dynamic-update-slice_fusion.refs_5_), channel_id=1, source_target_pairs={{16,0},{24,8},{0,16},{8,24},{17,1},{25,9},{1,17},{9,25},{18,2},{26... | collective-permute-start | bytes 786440 | tf_op jit(solution)/shard_map/ppermute | solution.py:37
  57.7 17.7 %copy-start.9 = (bf16[128,1024]{1,0:T(8,128)(2,1)}, bf16[128,1024]{1,0:T(8,128)(2,1)S(1)}, u32[]{:S(2)}) copy-start(bf16[128,1024]{1,0:T(8,128)(2,1)S(1)} %collective-permute-done.13.refs_0_.refs_8_) | copy-start | bytes 786436
  57.8 17.6 %copy-start = (bf16[384,1024]{1,0:T(8,128)(2,1)}, bf16[384,1024]{1,0:T(8,128)(2,1)S(1)}, u32[]{:S(2)}) copy-start(bf16[384,1024]{1,0:T(8,128)(2,1)S(1)} %collective-permute-done.12.refs_1_.refs_7_.refs_6_) | copy-start | bytes 2359300
  58.6 17.0 %collective-permute-start.16 = (bf16[8,128,128]{2,1,0:T(8,128)(2,1)}, bf16[8,128,128]{2,1,0:T(8,128)(2,1)S(1)}, u32[]{:S(2)}, u32[]{:S(2)}) collective-permute-start(bf16[8,128,128]{2,1,0:T(8,128)(2,1)} %shard_map.18), channel_id=1, source_target_pairs={{0,1},{1,0},{2,3},{3,2},{4,5},{5,4},{6,7},{7,6},{8,9},{9,8},{10,11... | collective-permute-start | bytes 786440 | tf_op jit(solution)/shard_map/ppermute | solution.py:41
  75.3 14.6 %collective-permute-start.17 = (bf16[256,1024]{1,0:T(8,128)(2,1)}, bf16[256,1024]{1,0:T(8,128)(2,1)}, u32[]{:S(2)}, u32[]{:S(2)}) collective-permute-start(bf16[256,1024]{1,0:T(8,128)(2,1)} %get-tuple-element.46), channel_id=1, source_target_pairs={{0,2},{2,0},{4,6},{6,4},{1,3},{3,1},{5,7},{7,5},{8,10},{10,8},{12,... | collective-permute-start | bytes 1572872 | tf_op jit(solution)/shard_map/ppermute | solution.py:41
  75.4 14.5 %collective-permute-start.18 = (bf16[256,1024]{1,0:T(8,128)(2,1)}, bf16[256,1024]{1,0:T(8,128)(2,1)S(1)}, u32[]{:S(2)}, u32[]{:S(2)}) collective-permute-start(bf16[256,1024]{1,0:T(8,128)(2,1)} %get-tuple-element.47), channel_id=1, source_target_pairs={{0,6},{2,4},{4,2},{6,0},{1,7},{3,5},{5,3},{7,1},{8,14},{10,12},{12... | collective-permute-start | bytes 1572872 | tf_op jit(solution)/shard_map/ppermute | solution.py:41
  75.6 1.1 %copy-start.1 = (bf16[384,1024]{1,0:T(8,128)(2,1)S(1)}, bf16[384,1024]{1,0:T(8,128)(2,1)}, u32[]{:S(2)}) copy-start(bf16[384,1024]{1,0:T(8,128)(2,1)} %copy-done) | copy-start | bytes 2359300
  76.7 0.9 copy-start.4
  81.5 13.5 %copy-start.2 = (bf16[384,1024]{1,0:T(8,128)(2,1)S(1)}, bf16[384,1024]{1,0:T(8,128)(2,1)}, u32[]{:S(2)}) copy-start(bf16[384,1024]{1,0:T(8,128)(2,1)} %copy-done) | copy-start | bytes 2359300
  81.5 13.5 %copy-start.10 = (bf16[128,1024]{1,0:T(8,128)(2,1)S(1)}, bf16[128,1024]{1,0:T(8,128)(2,1)}, u32[]{:S(2)}) copy-start(bf16[128,1024]{1,0:T(8,128)(2,1)} %copy-done.9) | copy-start | bytes 786436
  90.9 11.0 %collective-permute-start.19 = (bf16[64,1024]{1,0:T(8,128)(2,1)S(1)}, bf16[64,1024]{1,0:T(8,128)(2,1)S(1)}, u32[]{:S(2)}, u32[]{:S(2)}) collective-permute-start(bf16[64,1024]{1,0:T(8,128)(2,1)S(1)} %get-tuple-element.51), channel_id=1, source_target_pairs={{0,6},{2,4},{4,2},{6,0},{1,7},{3,5},{5,3},{7,1},{8,14},{10,12},{12... | collective-permute-start | bytes 393224 | tf_op jit(solution)/shard_map/ppermute | solution.py:41
  92.4 9.4 %collective-permute-start.20 = (bf16[64,1024]{1,0:T(8,128)(2,1)S(1)}, bf16[64,1024]{1,0:T(8,128)(2,1)S(1)}, u32[]{:S(2)}, u32[]{:S(2)}) collective-permute-start(bf16[64,1024]{1,0:T(8,128)(2,1)S(1)} %get-tuple-element.52), channel_id=1, source_target_pairs={{0,2},{2,0},{4,6},{6,4},{1,3},{3,1},{5,7},{7,5},{8,10},{10,8},{12,... | collective-permute-start | bytes 393224 | tf_op jit(solution)/shard_map/ppermute | solution.py:41
  104.0 3.5 %collective-permute-start.21 = (f32[16,64,256]{2,1,0:T(8,128)S(1)}, f32[16,64,256]{2,1,0:T(8,128)S(1)}, u32[]{:S(2)}, u32[]{:S(2)}) collective-permute-start(f32[16,64,256]{2,1,0:T(8,128)S(1)} %shard_map.24), channel_id=1, source_target_pairs={{0,1},{1,0},{2,3},{3,2},{4,5},{5,4},{6,7},{7,6},{8,9},{9,8},{10,11... | collective-permute-start | bytes 3145736 | tf_op jit(solution)/shard_map/ppermute | solution.py:41
  (5 other events, 4.5 us)

commit v6 on v5

--- a/solution.py
+++ b/solution.py
@@ -243,8 +243,7 @@
     held = jnp.concatenate(quarters, axis=1)
 
     above, below = pull(held, "zh", 1, 4), pull(held, "zh", 3, 4)
-    held_then, slabs = lax.optimization_barrier((held, slabs))
-    own_1, own_3 = swap(held_then, "y", 1, 4), swap(held_then, "y", 3, 4)
+    own_1, own_3 = swap(held, "y", 1, 4), swap(held, "y", 3, 4)
     rows_2 = pull(slabs, "x", 2, 4)
 
     across = pull(after(held, (own_1, own_3)), "zh", 2, 4)

time: 109 us -> 104 us (0.954)
  the two profiles are of different devices: /device:TPU:15 before, /device:TPU:1 now
where the time goes in v6:
time: 104 us
  starting transfers between devices  52.5 us (50%)
  Pallas kernels  22.5 us (22%)
  waiting for transfers between devices  18.5 us (18%)
  local copies, waits for them, and re-layouts  8.45 us (8%)
  other arithmetic  1.26 us (1%)
    ppermute x12, starting transfers between devices, swap(): return lax.ppermute(value, axis, [(i, i ^ bits) for i in range(count)])  25.6 us
    pallas_call x4, Pallas kernels, products(): pl.pallas_call(make_kernel(plan, len(arrays), first, share), out_shape=ha...  19.5 us
    ppermute x4, starting transfers between devices, on_device(): lax.ppermute(block[:, QUARTER * q:QUARTER * (q + 1)], AXES, scatter_pairs...  15.9 us
    ppermute x6, waiting for transfers between devices, pull(): lax.ppermute(value, axis, [((i + offset) % count, i) for i in range(count)])  13.9 us
    ppermute x6, starting transfers between devices, pull(): lax.ppermute(value, axis, [((i + offset) % count, i) for i in range(count)])  10.9 us
    unnamed x33, local copies, waits for them, and re-layouts  7.34 us
    ppermute x12, waiting for transfers between devices, swap(): return lax.ppermute(value, axis, [(i, i ^ bits) for i in range(count)])  2.62 us
    pallas_call x3, Pallas kernels, pack(): pl.pallas_call(copy_kernel, out_shape=[jax.ShapeDtypeStruct((sum((p[2] fo...  2.13 us
  transfers between devices with their start and end apart: 22, of which 6 were waited for; matrix products, arithmetic and copies ran while one was open for 0% of the time, Pallas kernels for 18%

profile of v6, /device:TPU:1, one launch (start us, length us, event | category | flops | bytes accessed | tf_op | source)
XLA Modules:
  0.0 103.5 jit_solution(6300017929994558636)
XLA Ops:
  0.0 1.0 dynamic-slice_bitcast_fusion.1
  1.0 3.3 %collective-permute-start = (bf16[64,1024]{1,0:T(8,128)(2,1)S(1)}, bf16[64,1024]{1,0:T(8,128)(2,1)S(1)}, u32[]{:S(2)}, u32[]{:S(2)}) collective-permute-start(bf16[64,1024]{1,0:T(8,128)(2,1)S(1)} %get-tuple-element.50), channel_id=1, source_target_pairs={{0,1},{1,0},{2,3},{3,2},{4,5},{5,4},{6,7},{7,6},{8,9},{9,8},{10,11... | collective-permute-start | bytes 393224 | tf_op jit(solution)/shard_map/ppermute | solution.py:41
  4.3 1.0 collective-permute-done
  6.2 4.5 %collective-permute-start.2 = (bf16[128,256]{1,0:T(8,128)(2,1)S(1)}, bf16[128,256]{1,0:T(8,128)(2,1)S(1)}, u32[]{:S(2)}, u32[]{:S(2)}) collective-permute-start(bf16[128,256]{1,0:T(8,128)(2,1)S(1)} %get-tuple-element.54), channel_id=1, source_target_pairs={{0,8},{1,9},{2,10},{3,11},{4,40},{5,41},{6,42},{7,43},{8,72},{9,73... | collective-permute-start | bytes 196616 | tf_op jit(solution)/shard_map/ppermute | solution.py:240
  10.7 8.7 %collective-permute-start.3 = (bf16[128,256]{1,0:T(8,128)(2,1)S(1)}, bf16[128,256]{1,0:T(8,128)(2,1)S(1)}, u32[]{:S(2)}, u32[]{:S(2)}) collective-permute-start(bf16[128,256]{1,0:T(8,128)(2,1)S(1)} %get-tuple-element.53), channel_id=1, source_target_pairs={{0,16},{1,17},{2,18},{3,19},{4,48},{5,49},{6,50},{7,51},{8,80},{9,... | collective-permute-start | bytes 196616 | tf_op jit(solution)/shard_map/ppermute | solution.py:240
  19.4 2.1 %collective-permute-start.4 = (bf16[128,256]{1,0:T(8,128)(2,1)S(1)}, bf16[128,256]{1,0:T(8,128)(2,1)S(1)}, u32[]{:S(2)}, u32[]{:S(2)}) collective-permute-start(bf16[128,256]{1,0:T(8,128)(2,1)S(1)} %get-tuple-element.52), channel_id=1, source_target_pairs={{0,24},{1,25},{2,26},{3,27},{4,56},{5,57},{6,58},{7,59},{8,88},{9,... | collective-permute-start | bytes 196616 | tf_op jit(solution)/shard_map/ppermute | solution.py:240
  21.8 2.0 %collective-permute-done.4 = bf16[128,256]{1,0:T(8,128)(2,1)S(1)} collective-permute-done((bf16[128,256]{1,0:T(8,128)(2,1)S(1)}, bf16[128,256]{1,0:T(8,128)(2,1)S(1)}, u32[]{:S(2)}, u32[]{:S(2)}) %collective-permute-start.4) | collective-permute-done | bytes 65568 | tf_op jit(solution)/shard_map/ppermute | solution.py:240
  23.8 1.3 %collective-permute-start.7 = (bf16[128,1024]{1,0:T(8,128)(2,1)S(1)}, bf16[128,1024]{1,0:T(8,128)(2,1)S(1)}, u32[]{:S(2)}, u32[]{:S(2)}) collective-permute-start(bf16[128,1024]{1,0:T(8,128)(2,1)S(1)} %constant_dynamic-update-slice_fusion.refs_5_), channel_id=1, source_target_pairs={{0,2},{2,0},{4,6},{6,4},{1,3},{3,1},{5,7},{7,5},{8,10},{10,8},{12,... | collective-permute-start | bytes 786440 | tf_op jit(solution)/shard_map/ppermute | solution.py:41
  25.1 7.9 %collective-permute-start.8 = (bf16[128,1024]{1,0:T(8,128)(2,1)S(1)}, bf16[128,1024]{1,0:T(8,128)(2,1)S(1)}, u32[]{:S(2)}, u32[]{:S(2)}) collective-permute-start(bf16[128,1024]{1,0:T(8,128)(2,1)S(1)} %constant_dynamic-update-slice_fusion.refs_5_), channel_id=1, source_target_pairs={{0,6},{2,4},{4,2},{6,0},{1,7},{3,5},{5,3},{7,1},{8,14},{10,12},{12... | collective-permute-start | bytes 786440 | tf_op jit(solution)/shard_map/ppermute | solution.py:41
  32.9 2.6 %collective-permute-start.5 = (bf16[128,1024]{1,0:T(8,128)(2,1)S(1)}, bf16[128,1024]{1,0:T(8,128)(2,1)S(1)}, u32[]{:S(2)}, u32[]{:S(2)}) collective-permute-start(bf16[128,1024]{1,0:T(8,128)(2,1)S(1)} %constant_dynamic-update-slice_fusion.refs_5_), channel_id=1, source_target_pairs={{8,0},{16,8},{24,16},{0,24},{9,1},{17,9},{25,17},{1,25},{10,2},{18... | collective-permute-start | bytes 786440 | tf_op jit(solution)/shard_map/ppermute | solution.py:37
  35.6 1.5 %collective-permute-done.8.refs_8_ = bf16[128,1024]{1,0:T(8,128)(2,1)S(1)} collective-permute-done((bf16[128,1024]{1,0:T(8,128)(2,1)S(1)}, bf16[128,1024]{1,0:T(8,128)(2,1)S(1)}, u32[]{:S(2)}, u32[]{:S(2)}) %collective-permute-start.8) | collective-permute-done | bytes 262176 | tf_op jit(solution)/shard_map/ppermute | solution.py:41
  37.7 6.3 %collective-permute-done.5.refs_0_.refs_9_ = bf16[128,1024]{1,0:T(8,128)(2,1)S(1)} collective-permute-done((bf16[128,1024]{1,0:T(8,128)(2,1)S(1)}, bf16[128,1024]{1,0:T(8,128)(2,1)S(1)}, u32[]{:S(2)}, u32[]{:S(2)}) %collective-permute-start.5) | collective-permute-done | bytes 262176 | tf_op jit(solution)/shard_map/ppermute | solution.py:37
  44.8 2.8 %collective-permute-start.14 = (bf16[2,128,1024]{2,1,0:T(8,128)(2,1)S(1)}, bf16[2,128,1024]{2,1,0:T(8,128)(2,1)S(1)}, u32[]{:S(2)}, u32[]{:S(2)}) collective-permute-start(bf16[2,128,1024]{2,1,0:T(8,128)(2,1)S(1)} %pad_maximum_fusion.refs_0_), channel_id=1, source_target_pairs={{64,0},{128,64},{192,128},{0,192},{65,1},{129,65},{193,129},{1,193... | collective-permute-start | bytes 1572872 | tf_op jit(solution)/shard_map/ppermute | solution.py:37
  47.6 1.7 %collective-permute-start.15 = (bf16[2,128,1024]{2,1,0:T(8,128)(2,1)S(1)}, bf16[2,128,1024]{2,1,0:T(8,128)(2,1)S(1)}, u32[]{:S(2)}, u32[]{:S(2)}) collective-permute-start(bf16[2,128,1024]{2,1,0:T(8,128)(2,1)S(1)} %pad_maximum_fusion.refs_0_), channel_id=1, source_target_pairs={{192,0},{0,64},{64,128},{128,192},{193,1},{1,65},{65,129},{129,193... | collective-permute-start | bytes 1572872 | tf_op jit(solution)/shard_map/ppermute | solution.py:37
  49.3 3.7 %collective-permute-start.13 = (bf16[128,1024]{1,0:T(8,128)(2,1)S(1)}, bf16[128,1024]{1,0:T(8,128)(2,1)S(1)}, u32[]{:S(2)}, u32[]{:S(2)}) collective-permute-start(bf16[128,1024]{1,0:T(8,128)(2,1)S(1)} %constant_dynamic-update-slice_fusion.refs_5_), channel_id=1, source_target_pairs={{16,0},{24,8},{0,16},{8,24},{17,1},{25,9},{1,17},{9,25},{18,2},{26... | collective-permute-start | bytes 786440 | tf_op jit(solution)/shard_map/ppermute | solution.py:37
  53.8 7.6 %collective-permute-done.13.refs_0_.refs_8_ = bf16[128,1024]{1,0:T(8,128)(2,1)S(1)} collective-permute-done((bf16[128,1024]{1,0:T(8,128)(2,1)S(1)}, bf16[128,1024]{1,0:T(8,128)(2,1)S(1)}, u32[]{:S(2)}, u32[]{:S(2)}) %collective-permute-start.13) | collective-permute-done | bytes 262176 | tf_op jit(solution)/shard_map/ppermute | solution.py:37
  62.3 5.9 %collective-permute-start.16 = (bf16[8,128,128]{2,1,0:T(8,128)(2,1)}, bf16[8,128,128]{2,1,0:T(8,128)(2,1)S(1)}, u32[]{:S(2)}, u32[]{:S(2)}) collective-permute-start(bf16[8,128,128]{2,1,0:T(8,128)(2,1)} %shard_map.18), channel_id=1, source_target_pairs={{0,1},{1,0},{2,3},{3,2},{4,5},{5,4},{6,7},{7,6},{8,9},{9,8},{10,11... | collective-permute-start | bytes 786440 | tf_op jit(solution)/shard_map/ppermute | solution.py:41
  68.2 1.1 %shard_map.19 = (bf16[256,1024]{1,0:T(8,128)(2,1)}, bf16[256,1024]{1,0:T(8,128)(2,1)}) custom-call(bf16[128,1024]{1,0:T(8,128)(2,1)S(1)} %collective-permute-done.13.refs_0_.refs_8_, bf16[384,1024]{1,0:T(8,128)(2,1)S(1)} %collective-permute-done.12.refs_1_.refs_7_.refs_6_, bf16[256,1024]{1,0:T(8,128)(2,1)S(1)} %collective-permute-done.11.refs_2_.refs_10_), custom_call_target="tpu_custom_call" | custom-call | bytes 1048576 | tf_op jit(solution)/shard_map/pallas_call | solution.py:216
  69.3 2.4 %collective-permute-start.17 = (bf16[256,1024]{1,0:T(8,128)(2,1)}, bf16[256,1024]{1,0:T(8,128)(2,1)}, u32[]{:S(2)}, u32[]{:S(2)}) collective-permute-start(bf16[256,1024]{1,0:T(8,128)(2,1)} %get-tuple-element.42), channel_id=1, source_target_pairs={{0,2},{2,0},{4,6},{6,4},{1,3},{3,1},{5,7},{7,5},{8,10},{10,8},{12,... | collective-permute-start | bytes 1572872 | tf_op jit(solution)/shard_map/ppermute | solution.py:41
  71.7 2.3 %collective-permute-start.18 = (bf16[256,1024]{1,0:T(8,128)(2,1)}, bf16[256,1024]{1,0:T(8,128)(2,1)S(1)}, u32[]{:S(2)}, u32[]{:S(2)}) collective-permute-start(bf16[256,1024]{1,0:T(8,128)(2,1)} %get-tuple-element.43), channel_id=1, source_target_pairs={{0,6},{2,4},{4,2},{6,0},{1,7},{3,5},{5,3},{7,1},{8,14},{10,12},{12... | collective-permute-start | bytes 1572872 | tf_op jit(solution)/shard_map/ppermute | solution.py:41
  74.1 1.1 %copy-done.1 = bf16[384,1024]{1,0:T(8,128)(2,1)S(1)} copy-done((bf16[384,1024]{1,0:T(8,128)(2,1)S(1)}, bf16[384,1024]{1,0:T(8,128)(2,1)}, u32[]{:S(2)}) %copy-start.1) | copy-done | bytes 786456
  75.2 0.9 copy-done.4
  76.1 0.9 copy-done.6
  77.1 0.9 copy-done.8
  78.0 0.9 copy-done.12
  79.0 0.9 copy-done.14
  79.9 8.4 %shard_map.20.refs_9_ = f32[2048,256]{1,0:T(8,128)S(1)} custom-call(s32[5]{0:T(128)S(1)} %stack.30.ix, bf16[2,128,1024]{2,1,0:T(8,128)(2,1)S(1)} %pad_maximum_fusion.refs_0_, bf16[2,128,1024]{2,1,0:T(8,128)(2,1)S(1)} %collective-permute-done.14.refs_1_, bf16[2,128,1024]{2,1,0:T(8,128)(2,1)S(1)} %collective-permute-done.15.refs_2_, ...), custom_call_target="tpu_custom_call" | custom-call | flops 4294967296 | bytes 4194304 | tf_op jit(solution)/shard_map/pallas_call | solution.py:176
  89.9 6.9 %shard_map.22.refs_8_ = f32[2048,256]{1,0:T(8,128)S(1)} custom-call(s32[5]{0:T(128)S(1)} %stack.30.ix, bf16[2,128,1024]{2,1,0:T(8,128)(2,1)S(1)} %pad_maximum_fusion.refs_0_, bf16[2,128,1024]{2,1,0:T(8,128)(2,1)S(1)} %collective-permute-done.14.refs_1_, bf16[2,128,1024]{2,1,0:T(8,128)(2,1)S(1)} %collective-permute-done.15.refs_2_, ...), custom_call_target="tpu_custom_call", output_to_operand_aliasing={{}: (10, {})} | custom-call | flops 3221225472 | bytes 3145728 | tf_op jit(solution)/shard_map/pallas_call | solution.py:176
  96.7 2.1 %shard_map.24 = f32[16,64,256]{2,1,0:T(8,128)S(1)} custom-call(s32[5]{0:T(128)S(1)} %stack.30.ix, bf16[2,128,1024]{2,1,0:T(8,128)(2,1)S(1)} %pad_maximum_fusion.refs_0_, bf16[2,128,1024]{2,1,0:T(8,128)(2,1)S(1)} %collective-permute-done.14.refs_1_, bf16[2,128,1024]{2,1,0:T(8,128)(2,1)S(1)} %collective-permute-done.15.refs_2_, ...), custom_call_target="tpu_custom_call" | custom-call | flops 1073741824 | bytes 1048576 | tf_op jit(solution)/shard_map/pallas_call | solution.py:176
  98.9 1.3 %collective-permute-start.21 = (f32[16,64,256]{2,1,0:T(8,128)S(1)}, f32[16,64,256]{2,1,0:T(8,128)S(1)}, u32[]{:S(2)}, u32[]{:S(2)}) collective-permute-start(f32[16,64,256]{2,1,0:T(8,128)S(1)} %shard_map.24), channel_id=1, source_target_pairs={{0,1},{1,0},{2,3},{3,2},{4,5},{5,4},{6,7},{7,6},{8,9},{9,8},{10,11... | collective-permute-start | bytes 3145736 | tf_op jit(solution)/shard_map/ppermute | solution.py:41
  100.1 2.1 %shard_map.23 = f32[16,64,256]{2,1,0:T(8,128)S(1)} custom-call(s32[5]{0:T(128)S(1)} %stack.30.ix, bf16[2,128,1024]{2,1,0:T(8,128)(2,1)S(1)} %pad_maximum_fusion.refs_0_, bf16[2,128,1024]{2,1,0:T(8,128)(2,1)S(1)} %collective-permute-done.14.refs_1_, bf16[2,128,1024]{2,1,0:T(8,128)(2,1)S(1)} %collective-permute-done.15.refs_2_, ...), custom_call_target="tpu_custom_call" | custom-call | flops 1073741824 | bytes 1048576 | tf_op jit(solution)/shard_map/pallas_call | solution.py:176
  102.4 1.1 %add.11 = f32[16,64,256]{2,1,0:T(8,128)} add(f32[16,64,256]{2,1,0:T(8,128)S(1)} %shard_map.23, f32[16,64,256]{2,1,0:T(8,128)S(1)} %collective-permute-done.21) | non-fusion elementwise | flops 262144 | bytes 3145728 | tf_op jit(solution)/shard_map/add | solution.py:291
  (61 shorter events, 5.8 us)
Async XLA Ops:
  1.0 4.3 %collective-permute-start = (bf16[64,1024]{1,0:T(8,128)(2,1)S(1)}, bf16[64,1024]{1,0:T(8,128)(2,1)S(1)}, u32[]{:S(2)}, u32[]{:S(2)}) collective-permute-start(bf16[64,1024]{1,0:T(8,128)(2,1)S(1)} %get-tuple-element.50), channel_id=1, source_target_pairs={{0,1},{1,0},{2,3},{3,2},{4,5},{5,4},{6,7},{7,6},{8,9},{9,8},{10,11... | collective-permute-start | bytes 393224 | tf_op jit(solution)/shard_map/ppermute | solution.py:41
  5.4 16.2 %collective-permute-start.9 = (bf16[128,1024]{1,0:T(8,128)(2,1)S(1)}, bf16[128,1024]{1,0:T(8,128)(2,1)S(1)}, u32[]{:S(2)}, u32[]{:S(2)}) collective-permute-start(bf16[128,1024]{1,0:T(8,128)(2,1)S(1)} %maximum_select_fusion), channel_id=1, source_target_pairs={{0,32},{32,0},{1,33},{33,1},{2,34},{34,2},{3,35},{35,3},{4,36},{36... | collective-permute-start | bytes 786440 | tf_op jit(solution)/shard_map/ppermute | solution.py:41
  5.5 16.0 %collective-permute-start.1 = (bf16[128,256]{1,0:T(8,128)(2,1)S(1)}, bf16[128,256]{1,0:T(8,128)(2,1)S(1)}, u32[]{:S(2)}, u32[]{:S(2)}) collective-permute-start(bf16[128,256]{1,0:T(8,128)(2,1)S(1)} %get-tuple-element.55), channel_id=1, source_target_pairs={{0,0},{1,1},{2,2},{3,3},{4,32},{5,33},{6,34},{7,35},{8,64},{9,65},... | collective-permute-start | bytes 196616 | tf_op jit(solution)/shard_map/ppermute | solution.py:240
  6.2 15.5 %collective-permute-start.2 = (bf16[128,256]{1,0:T(8,128)(2,1)S(1)}, bf16[128,256]{1,0:T(8,128)(2,1)S(1)}, u32[]{:S(2)}, u32[]{:S(2)}) collective-permute-start(bf16[128,256]{1,0:T(8,128)(2,1)S(1)} %get-tuple-element.54), channel_id=1, source_target_pairs={{0,8},{1,9},{2,10},{3,11},{4,40},{5,41},{6,42},{7,43},{8,72},{9,73... | collective-permute-start | bytes 196616 | tf_op jit(solution)/shard_map/ppermute | solution.py:240
  10.7 11.1 %collective-permute-start.3 = (bf16[128,256]{1,0:T(8,128)(2,1)S(1)}, bf16[128,256]{1,0:T(8,128)(2,1)S(1)}, u32[]{:S(2)}, u32[]{:S(2)}) collective-permute-start(bf16[128,256]{1,0:T(8,128)(2,1)S(1)} %get-tuple-element.53), channel_id=1, source_target_pairs={{0,16},{1,17},{2,18},{3,19},{4,48},{5,49},{6,50},{7,51},{8,80},{9,... | collective-permute-start | bytes 196616 | tf_op jit(solution)/shard_map/ppermute | solution.py:240
  19.4 4.3 %collective-permute-start.4 = (bf16[128,256]{1,0:T(8,128)(2,1)S(1)}, bf16[128,256]{1,0:T(8,128)(2,1)S(1)}, u32[]{:S(2)}, u32[]{:S(2)}) collective-permute-start(bf16[128,256]{1,0:T(8,128)(2,1)S(1)} %get-tuple-element.52), channel_id=1, source_target_pairs={{0,24},{1,25},{2,26},{3,27},{4,56},{5,57},{6,58},{7,59},{8,88},{9,... | collective-permute-start | bytes 196616 | tf_op jit(solution)/shard_map/ppermute | solution.py:240
  21.6 22.4 %collective-permute-start.10 = (bf16[2,128,1024]{2,1,0:T(8,128)(2,1)S(1)}, bf16[2,128,1024]{2,1,0:T(8,128)(2,1)S(1)}, u32[]{:S(2)}, u32[]{:S(2)}) collective-permute-start(bf16[2,128,1024]{2,1,0:T(8,128)(2,1)S(1)} %pad_maximum_fusion.refs_0_), channel_id=1, source_target_pairs={{128,0},{192,64},{0,128},{64,192},{129,1},{193,65},{1,129},{65,193... | collective-permute-start | bytes 1572872 | tf_op jit(solution)/shard_map/ppermute | solution.py:37
  23.8 11.8 %collective-permute-start.7 = (bf16[128,1024]{1,0:T(8,128)(2,1)S(1)}, bf16[128,1024]{1,0:T(8,128)(2,1)S(1)}, u32[]{:S(2)}, u32[]{:S(2)}) collective-permute-start(bf16[128,1024]{1,0:T(8,128)(2,1)S(1)} %constant_dynamic-update-slice_fusion.refs_5_), channel_id=1, source_target_pairs={{0,2},{2,0},{4,6},{6,4},{1,3},{3,1},{5,7},{7,5},{8,10},{10,8},{12,... | collective-permute-start | bytes 786440 | tf_op jit(solution)/shard_map/ppermute | solution.py:41
  25.1 12.0 %collective-permute-start.8 = (bf16[128,1024]{1,0:T(8,128)(2,1)S(1)}, bf16[128,1024]{1,0:T(8,128)(2,1)S(1)}, u32[]{:S(2)}, u32[]{:S(2)}) collective-permute-start(bf16[128,1024]{1,0:T(8,128)(2,1)S(1)} %constant_dynamic-update-slice_fusion.refs_5_), channel_id=1, source_target_pairs={{0,6},{2,4},{4,2},{6,0},{1,7},{3,5},{5,3},{7,1},{8,14},{10,12},{12... | collective-permute-start | bytes 786440 | tf_op jit(solution)/shard_map/ppermute | solution.py:41
  32.9 11.0 %collective-permute-start.5 = (bf16[128,1024]{1,0:T(8,128)(2,1)S(1)}, bf16[128,1024]{1,0:T(8,128)(2,1)S(1)}, u32[]{:S(2)}, u32[]{:S(2)}) collective-permute-start(bf16[128,1024]{1,0:T(8,128)(2,1)S(1)} %constant_dynamic-update-slice_fusion.refs_5_), channel_id=1, source_target_pairs={{8,0},{16,8},{24,16},{0,24},{9,1},{17,9},{25,17},{1,25},{10,2},{18... | collective-permute-start | bytes 786440 | tf_op jit(solution)/shard_map/ppermute | solution.py:37
  35.5 8.4 %collective-permute-start.6 = (bf16[128,1024]{1,0:T(8,128)(2,1)S(1)}, bf16[128,1024]{1,0:T(8,128)(2,1)S(1)}, u32[]{:S(2)}, u32[]{:S(2)}) collective-permute-start(bf16[128,1024]{1,0:T(8,128)(2,1)S(1)} %constant_dynamic-update-slice_fusion.refs_5_), channel_id=1, source_target_pairs={{24,0},{0,8},{8,16},{16,24},{25,1},{1,9},{9,17},{17,25},{26,2},{2,... | collective-permute-start | bytes 786440 | tf_op jit(solution)/shard_map/ppermute | solution.py:37
  35.6 33.7 %copy-start.3 = (bf16[128,1024]{1,0:T(8,128)(2,1)}, bf16[128,1024]{1,0:T(8,128)(2,1)S(1)}, u32[]{:S(2)}) copy-start(bf16[128,1024]{1,0:T(8,128)(2,1)S(1)} %collective-permute-done.7.refs_2_.refs_6_) | copy-start | bytes 786436
  44.0 25.3 %copy-start.5 = (bf16[128,1024]{1,0:T(8,128)(2,1)}, bf16[128,1024]{1,0:T(8,128)(2,1)S(1)}, u32[]{:S(2)}) copy-start(bf16[128,1024]{1,0:T(8,128)(2,1)S(1)} %collective-permute-done.5.refs_0_.refs_9_) | copy-start | bytes 786436
  44.0 17.4 %copy-start.7 = (bf16[128,1024]{1,0:T(8,128)(2,1)}, bf16[128,1024]{1,0:T(8,128)(2,1)S(1)}, u32[]{:S(2)}) copy-start(bf16[128,1024]{1,0:T(8,128)(2,1)S(1)} %collective-permute-done.6.refs_1_.refs_11_) | copy-start | bytes 786436
  44.1 17.3 %collective-permute-start.12 = (bf16[384,1024]{1,0:T(8,128)(2,1)S(1)}, bf16[384,1024]{1,0:T(8,128)(2,1)S(1)}, u32[]{:S(2)}, u32[]{:S(2)}) collective-permute-start(bf16[384,1024]{1,0:T(8,128)(2,1)S(1)} %get-tuple-element.31), channel_id=1, source_target_pairs={{0,6},{2,4},{4,2},{6,0},{1,7},{3,5},{5,3},{7,1},{8,14},{10,12},{12... | collective-permute-start | bytes 2359304 | tf_op jit(solution)/shard_map/ppermute | solution.py:41
  44.2 17.1 %collective-permute-start.11 = (bf16[256,1024]{1,0:T(8,128)(2,1)S(1)}, bf16[256,1024]{1,0:T(8,128)(2,1)S(1)}, u32[]{:S(2)}, u32[]{:S(2)}) collective-permute-start(bf16[256,1024]{1,0:T(8,128)(2,1)S(1)} %get-tuple-element.30), channel_id=1, source_target_pairs={{0,2},{2,0},{4,6},{6,4},{1,3},{3,1},{5,7},{7,5},{8,10},{10,8},{12,... | collective-permute-start | bytes 1572872 | tf_op jit(solution)/shard_map/ppermute | solution.py:41
  44.8 16.6 %collective-permute-start.14 = (bf16[2,128,1024]{2,1,0:T(8,128)(2,1)S(1)}, bf16[2,128,1024]{2,1,0:T(8,128)(2,1)S(1)}, u32[]{:S(2)}, u32[]{:S(2)}) collective-permute-start(bf16[2,128,1024]{2,1,0:T(8,128)(2,1)S(1)} %pad_maximum_fusion.refs_0_), channel_id=1, source_target_pairs={{64,0},{128,64},{192,128},{0,192},{65,1},{129,65},{193,129},{1,193... | collective-permute-start | bytes 1572872 | tf_op jit(solution)/shard_map/ppermute | solution.py:37
  47.6 13.8 %collective-permute-start.15 = (bf16[2,128,1024]{2,1,0:T(8,128)(2,1)S(1)}, bf16[2,128,1024]{2,1,0:T(8,128)(2,1)S(1)}, u32[]{:S(2)}, u32[]{:S(2)}) collective-permute-start(bf16[2,128,1024]{2,1,0:T(8,128)(2,1)S(1)} %pad_maximum_fusion.refs_0_), channel_id=1, source_target_pairs={{192,0},{0,64},{64,128},{128,192},{193,1},{1,65},{65,129},{129,193... | collective-permute-start | bytes 1572872 | tf_op jit(solution)/shard_map/ppermute | solution.py:37
  49.3 12.0 %collective-permute-start.13 = (bf16[128,1024]{1,0:T(8,128)(2,1)S(1)}, bf16[128,1024]{1,0:T(8,128)(2,1)S(1)}, u32[]{:S(2)}, u32[]{:S(2)}) collective-permute-start(bf16[128,1024]{1,0:T(8,128)(2,1)S(1)} %constant_dynamic-update-slice_fusion.refs_5_), channel_id=1, source_target_pairs={{16,0},{24,8},{0,16},{8,24},{17,1},{25,9},{1,17},{9,25},{18,2},{26... | collective-permute-start | bytes 786440 | tf_op jit(solution)/shard_map/ppermute | solution.py:37
  61.4 10.3 %copy-start.9 = (bf16[128,1024]{1,0:T(8,128)(2,1)}, bf16[128,1024]{1,0:T(8,128)(2,1)S(1)}, u32[]{:S(2)}) copy-start(bf16[128,1024]{1,0:T(8,128)(2,1)S(1)} %collective-permute-done.13.refs_0_.refs_8_) | copy-start | bytes 786436
  61.4 10.3 %copy-start = (bf16[384,1024]{1,0:T(8,128)(2,1)}, bf16[384,1024]{1,0:T(8,128)(2,1)S(1)}, u32[]{:S(2)}) copy-start(bf16[384,1024]{1,0:T(8,128)(2,1)S(1)} %collective-permute-done.12.refs_1_.refs_7_.refs_6_) | copy-start | bytes 2359300
  62.3 11.8 %collective-permute-start.16 = (bf16[8,128,128]{2,1,0:T(8,128)(2,1)}, bf16[8,128,128]{2,1,0:T(8,128)(2,1)S(1)}, u32[]{:S(2)}, u32[]{:S(2)}) collective-permute-start(bf16[8,128,128]{2,1,0:T(8,128)(2,1)} %shard_map.18), channel_id=1, source_target_pairs={{0,1},{1,0},{2,3},{3,2},{4,5},{5,4},{6,7},{7,6},{8,9},{9,8},{10,11... | collective-permute-start | bytes 786440 | tf_op jit(solution)/shard_map/ppermute | solution.py:41
  69.3 19.1 %collective-permute-start.17 = (bf16[256,1024]{1,0:T(8,128)(2,1)}, bf16[256,1024]{1,0:T(8,128)(2,1)}, u32[]{:S(2)}, u32[]{:S(2)}) collective-permute-start(bf16[256,1024]{1,0:T(8,128)(2,1)} %get-tuple-element.42), channel_id=1, source_target_pairs={{0,2},{2,0},{4,6},{6,4},{1,3},{3,1},{5,7},{7,5},{8,10},{10,8},{12,... | collective-permute-start | bytes 1572872 | tf_op jit(solution)/shard_map/ppermute | solution.py:41
  71.7 16.7 %collective-permute-start.18 = (bf16[256,1024]{1,0:T(8,128)(2,1)}, bf16[256,1024]{1,0:T(8,128)(2,1)S(1)}, u32[]{:S(2)}, u32[]{:S(2)}) collective-permute-start(bf16[256,1024]{1,0:T(8,128)(2,1)} %get-tuple-element.43), channel_id=1, source_target_pairs={{0,6},{2,4},{4,2},{6,0},{1,7},{3,5},{5,3},{7,1},{8,14},{10,12},{12... | collective-permute-start | bytes 1572872 | tf_op jit(solution)/shard_map/ppermute | solution.py:41
  74.1 1.1 %copy-start.1 = (bf16[384,1024]{1,0:T(8,128)(2,1)S(1)}, bf16[384,1024]{1,0:T(8,128)(2,1)}, u32[]{:S(2)}) copy-start(bf16[384,1024]{1,0:T(8,128)(2,1)} %copy-done) | copy-start | bytes 2359300
  75.2 0.9 copy-start.4
  76.1 0.9 copy-start.6
  79.9 9.9 %copy-start.2 = (bf16[384,1024]{1,0:T(8,128)(2,1)S(1)}, bf16[384,1024]{1,0:T(8,128)(2,1)}, u32[]{:S(2)}) copy-start(bf16[384,1024]{1,0:T(8,128)(2,1)} %copy-done) | copy-start | bytes 2359300
  79.9 9.9 %copy-start.10 = (bf16[128,1024]{1,0:T(8,128)(2,1)S(1)}, bf16[128,1024]{1,0:T(8,128)(2,1)}, u32[]{:S(2)}) copy-start(bf16[128,1024]{1,0:T(8,128)(2,1)} %copy-done.9) | copy-start | bytes 786436
  89.3 7.4 %collective-permute-start.19 = (bf16[64,1024]{1,0:T(8,128)(2,1)S(1)}, bf16[64,1024]{1,0:T(8,128)(2,1)S(1)}, u32[]{:S(2)}, u32[]{:S(2)}) collective-permute-start(bf16[64,1024]{1,0:T(8,128)(2,1)S(1)} %get-tuple-element.47), channel_id=1, source_target_pairs={{0,6},{2,4},{4,2},{6,0},{1,7},{3,5},{5,3},{7,1},{8,14},{10,12},{12... | collective-permute-start | bytes 393224 | tf_op jit(solution)/shard_map/ppermute | solution.py:41
  89.8 6.9 %collective-permute-start.20 = (bf16[64,1024]{1,0:T(8,128)(2,1)S(1)}, bf16[64,1024]{1,0:T(8,128)(2,1)S(1)}, u32[]{:S(2)}, u32[]{:S(2)}) collective-permute-start(bf16[64,1024]{1,0:T(8,128)(2,1)S(1)} %get-tuple-element.48), channel_id=1, source_target_pairs={{0,2},{2,0},{4,6},{6,4},{1,3},{3,1},{5,7},{7,5},{8,10},{10,8},{12,... | collective-permute-start | bytes 393224 | tf_op jit(solution)/shard_map/ppermute | solution.py:41
  98.9 3.6 %collective-permute-start.21 = (f32[16,64,256]{2,1,0:T(8,128)S(1)}, f32[16,64,256]{2,1,0:T(8,128)S(1)}, u32[]{:S(2)}, u32[]{:S(2)}) collective-permute-start(f32[16,64,256]{2,1,0:T(8,128)S(1)} %shard_map.24), channel_id=1, source_target_pairs={{0,1},{1,0},{2,3},{3,2},{4,5},{5,4},{6,7},{7,6},{8,9},{9,8},{10,11... | collective-permute-start | bytes 3145736 | tf_op jit(solution)/shard_map/ppermute | solution.py:41
  (5 other events, 4.3 us)

commit v7 on v6

--- a/solution.py
+++ b/solution.py
@@ -256,7 +256,6 @@
     rows_3 = pull(slabs, "x", 3, 4)
     rows = [slabs, rows_1, rows_3, rows_2]
 
-    via_1, via_3, across, *rows = lax.optimization_barrier((via_1, via_3, across, *rows))
     rows = [*rows, swap(heads_of(rows), "c", 1, 2)]
     to_1, to_3 = pack([(across, 0, CH), (via_3, CH, CH)], [(across, 0, CH), (via_1, 0, CH)])
     late_1, late_3 = swap(to_1, "y", 1, 4), swap(to_3, "y", 3, 4)

time: 104 us -> 103 us (level)
  waiting for transfers between devices: 18.5 us -> 14 us
  starting transfers between devices: 52.5 us -> 55.1 us
    ppermute x12, starting transfers between devices: 25.6 us -> 33.6 us  [swap(): return lax.ppermute(value, axis, [(i, i ^ bits) for i in range(count)])]
    ppermute x6, waiting for transfers between devices: 13.9 us -> 7.09 us  [pull(): lax.ppermute(value, axis, [((i + offset) % count, i) for i in range(count)])]
    ppermute x6, starting transfers between devices: 10.9 us -> 5.53 us  [pull(): lax.ppermute(value, axis, [((i + offset) % count, i) for i in range(count)])]
    ppermute x12, waiting for transfers between devices: 2.62 us -> 4.89 us  [swap(): return lax.ppermute(value, axis, [(i, i ^ bits) for i in range(count)])]
  transfers between devices with their start and end apart: 22 -> 22, of which waited for: 6 -> 6; matrix products, arithmetic and copies ran while one was open for 0% -> 0% of each run, Pallas kernels for 18% -> 19%
where the time goes in v7:
time: 103 us; the launch traced here: 102 us
  starting transfers between devices  55.1 us (53%)
  Pallas kernels  22.5 us (22%)
  waiting for transfers between devices  14 us (14%)
  local copies, waits for them, and re-layouts  8.51 us (8%)
  other arithmetic  1.26 us (1%)
    ppermute x12, starting transfers between devices, swap(): return lax.ppermute(value, axis, [(i, i ^ bits) for i in range(count)])  33.6 us
    pallas_call x4, Pallas kernels, products(): pl.pallas_call(make_kernel(plan, len(arrays), first, share), out_shape=ha...  19.5 us
    ppermute x4, starting transfers between devices, on_device(): lax.ppermute(block[:, QUARTER * q:QUARTER * (q + 1)], AXES, scatter_pairs...  15.9 us
    unnamed x33, local copies, waits for them, and re-layouts  7.4 us
    ppermute x6, waiting for transfers between devices, pull(): lax.ppermute(value, axis, [((i + offset) % count, i) for i in range(count)])  7.09 us
    ppermute x6, starting transfers between devices, pull(): lax.ppermute(value, axis, [((i + offset) % count, i) for i in range(count)])  5.53 us
    ppermute x12, waiting for transfers between devices, swap(): return lax.ppermute(value, axis, [(i, i ^ bits) for i in range(count)])  4.89 us
    pallas_call x3, Pallas kernels, pack(): pl.pallas_call(copy_kernel, out_shape=[jax.ShapeDtypeStruct((sum((p[2] fo...  2.18 us
  transfers between devices with their start and end apart: 22, of which 6 were waited for; matrix products, arithmetic and copies ran while one was open for 0% of the time, Pallas kernels for 19%

profile of v7, /device:TPU:1, one launch (start us, length us, event | category | flops | bytes accessed | tf_op | source)
XLA Modules:
  0.0 101.6 jit_solution(4950277200376096005)
XLA Ops:
  0.0 1.0 dynamic-slice_bitcast_fusion.1
  1.0 3.3 %collective-permute-start = (bf16[64,1024]{1,0:T(8,128)(2,1)S(1)}, bf16[64,1024]{1,0:T(8,128)(2,1)S(1)}, u32[]{:S(2)}, u32[]{:S(2)}) collective-permute-start(bf16[64,1024]{1,0:T(8,128)(2,1)S(1)} %get-tuple-element.36), channel_id=1, source_target_pairs={{0,1},{1,0},{2,3},{3,2},{4,5},{5,4},{6,7},{7,6},{8,9},{9,8},{10,11... | collective-permute-start | bytes 393224 | tf_op jit(solution)/shard_map/ppermute | solution.py:41
  4.3 1.0 collective-permute-done
  6.2 4.5 %collective-permute-start.2 = (bf16[128,256]{1,0:T(8,128)(2,1)S(1)}, bf16[128,256]{1,0:T(8,128)(2,1)S(1)}, u32[]{:S(2)}, u32[]{:S(2)}) collective-permute-start(bf16[128,256]{1,0:T(8,128)(2,1)S(1)} %get-tuple-element.40), channel_id=1, source_target_pairs={{0,8},{1,9},{2,10},{3,11},{4,40},{5,41},{6,42},{7,43},{8,72},{9,73... | collective-permute-start | bytes 196616 | tf_op jit(solution)/shard_map/ppermute | solution.py:240
  10.7 8.7 %collective-permute-start.3 = (bf16[128,256]{1,0:T(8,128)(2,1)S(1)}, bf16[128,256]{1,0:T(8,128)(2,1)S(1)}, u32[]{:S(2)}, u32[]{:S(2)}) collective-permute-start(bf16[128,256]{1,0:T(8,128)(2,1)S(1)} %get-tuple-element.39), channel_id=1, source_target_pairs={{0,16},{1,17},{2,18},{3,19},{4,48},{5,49},{6,50},{7,51},{8,80},{9,... | collective-permute-start | bytes 196616 | tf_op jit(solution)/shard_map/ppermute | solution.py:240
  19.4 2.1 %collective-permute-start.4 = (bf16[128,256]{1,0:T(8,128)(2,1)S(1)}, bf16[128,256]{1,0:T(8,128)(2,1)S(1)}, u32[]{:S(2)}, u32[]{:S(2)}) collective-permute-start(bf16[128,256]{1,0:T(8,128)(2,1)S(1)} %get-tuple-element.38), channel_id=1, source_target_pairs={{0,24},{1,25},{2,26},{3,27},{4,56},{5,57},{6,58},{7,59},{8,88},{9,... | collective-permute-start | bytes 196616 | tf_op jit(solution)/shard_map/ppermute | solution.py:240
  21.8 2.0 %collective-permute-done.4 = bf16[128,256]{1,0:T(8,128)(2,1)S(1)} collective-permute-done((bf16[128,256]{1,0:T(8,128)(2,1)S(1)}, bf16[128,256]{1,0:T(8,128)(2,1)S(1)}, u32[]{:S(2)}, u32[]{:S(2)}) %collective-permute-start.4) | collective-permute-done | bytes 65568 | tf_op jit(solution)/shard_map/ppermute | solution.py:240
  23.8 3.5 %collective-permute-start.5 = (bf16[128,1024]{1,0:T(8,128)(2,1)S(1)}, bf16[128,1024]{1,0:T(8,128)(2,1)S(1)}, u32[]{:S(2)}, u32[]{:S(2)}) collective-permute-start(bf16[128,1024]{1,0:T(8,128)(2,1)S(1)} %constant_dynamic-update-slice_fusion.refs_5_), channel_id=1, source_target_pairs={{8,0},{16,8},{24,16},{0,24},{9,1},{17,9},{25,17},{1,25},{10,2},{18... | collective-permute-start | bytes 786440 | tf_op jit(solution)/shard_map/ppermute | solution.py:37
  27.3 1.4 %collective-permute-start.7 = (bf16[128,1024]{1,0:T(8,128)(2,1)S(1)}, bf16[128,1024]{1,0:T(8,128)(2,1)S(1)}, u32[]{:S(2)}, u32[]{:S(2)}) collective-permute-start(bf16[128,1024]{1,0:T(8,128)(2,1)S(1)} %constant_dynamic-update-slice_fusion.refs_5_), channel_id=1, source_target_pairs={{0,2},{2,0},{4,6},{6,4},{1,3},{3,1},{5,7},{7,5},{8,10},{10,8},{12,... | collective-permute-start | bytes 786440 | tf_op jit(solution)/shard_map/ppermute | solution.py:41
  28.6 13.4 %collective-permute-start.8 = (bf16[128,1024]{1,0:T(8,128)(2,1)S(1)}, bf16[128,1024]{1,0:T(8,128)(2,1)S(1)}, u32[]{:S(2)}, u32[]{:S(2)}) collective-permute-start(bf16[128,1024]{1,0:T(8,128)(2,1)S(1)} %constant_dynamic-update-slice_fusion.refs_5_), channel_id=1, source_target_pairs={{0,6},{2,4},{4,2},{6,0},{1,7},{3,5},{5,3},{7,1},{8,14},{10,12},{12... | collective-permute-start | bytes 786440 | tf_op jit(solution)/shard_map/ppermute | solution.py:41
  42.1 3.7 %collective-permute-done.8.refs_8_ = bf16[128,1024]{1,0:T(8,128)(2,1)S(1)} collective-permute-done((bf16[128,1024]{1,0:T(8,128)(2,1)S(1)}, bf16[128,1024]{1,0:T(8,128)(2,1)S(1)}, u32[]{:S(2)}, u32[]{:S(2)}) %collective-permute-start.8) | collective-permute-done | bytes 262176 | tf_op jit(solution)/shard_map/ppermute | solution.py:41
  46.6 2.9 %collective-permute-start.15 = (bf16[384,1024]{1,0:T(8,128)(2,1)S(1)}, bf16[384,1024]{1,0:T(8,128)(2,1)S(1)}, u32[]{:S(2)}, u32[]{:S(2)}) collective-permute-start(bf16[384,1024]{1,0:T(8,128)(2,1)S(1)} %get-tuple-element.26), channel_id=1, source_target_pairs={{0,6},{2,4},{4,2},{6,0},{1,7},{3,5},{5,3},{7,1},{8,14},{10,12},{12... | collective-permute-start | bytes 2359304 | tf_op jit(solution)/shard_map/ppermute | solution.py:41
  49.5 1.5 %collective-permute-start.12 = (bf16[2,128,1024]{2,1,0:T(8,128)(2,1)S(1)}, bf16[2,128,1024]{2,1,0:T(8,128)(2,1)S(1)}, u32[]{:S(2)}, u32[]{:S(2)}) collective-permute-start(bf16[2,128,1024]{2,1,0:T(8,128)(2,1)S(1)} %pad_maximum_fusion.refs_0_), channel_id=1, source_target_pairs={{192,0},{0,64},{64,128},{128,192},{193,1},{1,65},{65,129},{129,193... | collective-permute-start | bytes 1572872 | tf_op jit(solution)/shard_map/ppermute | solution.py:37
  52.2 5.9 %collective-permute-done.11.refs_1_ = bf16[2,128,1024]{2,1,0:T(8,128)(2,1)S(1)} collective-permute-done((bf16[2,128,1024]{2,1,0:T(8,128)(2,1)S(1)}, bf16[2,128,1024]{2,1,0:T(8,128)(2,1)S(1)}, u32[]{:S(2)}, u32[]{:S(2)}) %collective-permute-start.11) | collective-permute-done | bytes 524320 | tf_op jit(solution)/shard_map/ppermute | solution.py:37
  58.0 1.2 %collective-permute-done.12.refs_2_ = bf16[2,128,1024]{2,1,0:T(8,128)(2,1)S(1)} collective-permute-done((bf16[2,128,1024]{2,1,0:T(8,128)(2,1)S(1)}, bf16[2,128,1024]{2,1,0:T(8,128)(2,1)S(1)}, u32[]{:S(2)}, u32[]{:S(2)}) %collective-permute-start.12) | collective-permute-done | bytes 524320 | tf_op jit(solution)/shard_map/ppermute | solution.py:37
  59.2 0.8 shard_map.17
  60.0 5.9 %collective-permute-start.13 = (bf16[8,128,128]{2,1,0:T(8,128)(2,1)}, bf16[8,128,128]{2,1,0:T(8,128)(2,1)S(1)}, u32[]{:S(2)}, u32[]{:S(2)}) collective-permute-start(bf16[8,128,128]{2,1,0:T(8,128)(2,1)} %shard_map.17), channel_id=1, source_target_pairs={{0,1},{1,0},{2,3},{3,2},{4,5},{5,4},{6,7},{7,6},{8,9},{9,8},{10,11... | collective-permute-start | bytes 786440 | tf_op jit(solution)/shard_map/ppermute | solution.py:41
  66.0 1.1 %shard_map.19 = (bf16[256,1024]{1,0:T(8,128)(2,1)}, bf16[256,1024]{1,0:T(8,128)(2,1)}) custom-call(bf16[128,1024]{1,0:T(8,128)(2,1)S(1)} %collective-permute-done.14.refs_0_.refs_8_, bf16[384,1024]{1,0:T(8,128)(2,1)S(1)} %collective-permute-done.15.refs_1_.refs_7_.refs_6_, bf16[256,1024]{1,0:T(8,128)(2,1)S(1)} %collective-permute-done.16.refs_2_.refs_10_), custom_call_target="tpu_custom_call" | custom-call | bytes 1048576 | tf_op jit(solution)/shard_map/pallas_call | solution.py:216
  67.6 1.1 %copy-done.1 = bf16[384,1024]{1,0:T(8,128)(2,1)S(1)} copy-done((bf16[384,1024]{1,0:T(8,128)(2,1)S(1)}, bf16[384,1024]{1,0:T(8,128)(2,1)}, u32[]{:S(2)}) %copy-start.1) | copy-done | bytes 786456
  68.7 0.9 copy-done.4
  69.7 0.9 copy-done.6
  70.6 0.9 copy-done.8
  71.6 0.9 copy-done.12
  72.5 0.9 copy-done.14
  73.5 8.4 %shard_map.20.refs_9_ = f32[2048,256]{1,0:T(8,128)S(1)} custom-call(s32[5]{0:T(128)S(1)} %stack.30.ix, bf16[2,128,1024]{2,1,0:T(8,128)(2,1)S(1)} %pad_maximum_fusion.refs_0_, bf16[2,128,1024]{2,1,0:T(8,128)(2,1)S(1)} %collective-permute-done.11.refs_1_, bf16[2,128,1024]{2,1,0:T(8,128)(2,1)S(1)} %collective-permute-done.12.refs_2_, ...), custom_call_target="tpu_custom_call" | custom-call | flops 4294967296 | bytes 4194304 | tf_op jit(solution)/shard_map/pallas_call | solution.py:176
  81.9 0.9 shard_map.21
  82.9 2.6 %collective-permute-start.19 = (bf16[64,1024]{1,0:T(8,128)(2,1)S(1)}, bf16[64,1024]{1,0:T(8,128)(2,1)S(1)}, u32[]{:S(2)}, u32[]{:S(2)}) collective-permute-start(bf16[64,1024]{1,0:T(8,128)(2,1)S(1)} %get-tuple-element.33), channel_id=1, source_target_pairs={{0,6},{2,4},{4,2},{6,0},{1,7},{3,5},{5,3},{7,1},{8,14},{10,12},{12... | collective-permute-start | bytes 393224 | tf_op jit(solution)/shard_map/ppermute | solution.py:41
  85.6 6.9 %shard_map.22.refs_8_ = f32[2048,256]{1,0:T(8,128)S(1)} custom-call(s32[5]{0:T(128)S(1)} %stack.30.ix, bf16[2,128,1024]{2,1,0:T(8,128)(2,1)S(1)} %pad_maximum_fusion.refs_0_, bf16[2,128,1024]{2,1,0:T(8,128)(2,1)S(1)} %collective-permute-done.11.refs_1_, bf16[2,128,1024]{2,1,0:T(8,128)(2,1)S(1)} %collective-permute-done.12.refs_2_, ...), custom_call_target="tpu_custom_call", output_to_operand_aliasing={{}: (10, {})} | custom-call | flops 3221225472 | bytes 3145728 | tf_op jit(solution)/shard_map/pallas_call | solution.py:176
  92.5 2.1 %shard_map.24 = f32[16,64,256]{2,1,0:T(8,128)S(1)} custom-call(s32[5]{0:T(128)S(1)} %stack.30.ix, bf16[2,128,1024]{2,1,0:T(8,128)(2,1)S(1)} %pad_maximum_fusion.refs_0_, bf16[2,128,1024]{2,1,0:T(8,128)(2,1)S(1)} %collective-permute-done.11.refs_1_, bf16[2,128,1024]{2,1,0:T(8,128)(2,1)S(1)} %collective-permute-done.12.refs_2_, ...), custom_call_target="tpu_custom_call" | custom-call | flops 1073741824 | bytes 1048576 | tf_op jit(solution)/shard_map/pallas_call | solution.py:176
  94.6 3.6 %collective-permute-start.21 = (f32[16,64,256]{2,1,0:T(8,128)S(1)}, f32[16,64,256]{2,1,0:T(8,128)S(1)}, u32[]{:S(2)}, u32[]{:S(2)}) collective-permute-start(f32[16,64,256]{2,1,0:T(8,128)S(1)} %shard_map.24), channel_id=1, source_target_pairs={{0,1},{1,0},{2,3},{3,2},{4,5},{5,4},{6,7},{7,6},{8,9},{9,8},{10,11... | collective-permute-start | bytes 3145736 | tf_op jit(solution)/shard_map/ppermute | solution.py:41
  98.2 2.1 %shard_map.23 = f32[16,64,256]{2,1,0:T(8,128)S(1)} custom-call(s32[5]{0:T(128)S(1)} %stack.30.ix, bf16[2,128,1024]{2,1,0:T(8,128)(2,1)S(1)} %pad_maximum_fusion.refs_0_, bf16[2,128,1024]{2,1,0:T(8,128)(2,1)S(1)} %collective-permute-done.11.refs_1_, bf16[2,128,1024]{2,1,0:T(8,128)(2,1)S(1)} %collective-permute-done.12.refs_2_, ...), custom_call_target="tpu_custom_call" | custom-call | flops 1073741824 | bytes 1048576 | tf_op jit(solution)/shard_map/pallas_call | solution.py:176
  100.5 1.1 %add.11 = f32[16,64,256]{2,1,0:T(8,128)} add(f32[16,64,256]{2,1,0:T(8,128)S(1)} %shard_map.23, f32[16,64,256]{2,1,0:T(8,128)S(1)} %collective-permute-done.21) | non-fusion elementwise | flops 262144 | bytes 3145728 | tf_op jit(solution)/shard_map/add | solution.py:290
  (61 shorter events, 3.9 us)
Async XLA Ops:
  1.0 4.3 %collective-permute-start = (bf16[64,1024]{1,0:T(8,128)(2,1)S(1)}, bf16[64,1024]{1,0:T(8,128)(2,1)S(1)}, u32[]{:S(2)}, u32[]{:S(2)}) collective-permute-start(bf16[64,1024]{1,0:T(8,128)(2,1)S(1)} %get-tuple-element.36), channel_id=1, source_target_pairs={{0,1},{1,0},{2,3},{3,2},{4,5},{5,4},{6,7},{7,6},{8,9},{9,8},{10,11... | collective-permute-start | bytes 393224 | tf_op jit(solution)/shard_map/ppermute | solution.py:41
  5.4 16.2 %collective-permute-start.9 = (bf16[128,1024]{1,0:T(8,128)(2,1)S(1)}, bf16[128,1024]{1,0:T(8,128)(2,1)S(1)}, u32[]{:S(2)}, u32[]{:S(2)}) collective-permute-start(bf16[128,1024]{1,0:T(8,128)(2,1)S(1)} %maximum_select_fusion), channel_id=1, source_target_pairs={{0,32},{32,0},{1,33},{33,1},{2,34},{34,2},{3,35},{35,3},{4,36},{36... | collective-permute-start | bytes 786440 | tf_op jit(solution)/shard_map/ppermute | solution.py:41
  5.5 16.0 %collective-permute-start.1 = (bf16[128,256]{1,0:T(8,128)(2,1)S(1)}, bf16[128,256]{1,0:T(8,128)(2,1)S(1)}, u32[]{:S(2)}, u32[]{:S(2)}) collective-permute-start(bf16[128,256]{1,0:T(8,128)(2,1)S(1)} %get-tuple-element.41), channel_id=1, source_target_pairs={{0,0},{1,1},{2,2},{3,3},{4,32},{5,33},{6,34},{7,35},{8,64},{9,65},... | collective-permute-start | bytes 196616 | tf_op jit(solution)/shard_map/ppermute | solution.py:240
  6.2 15.5 %collective-permute-start.2 = (bf16[128,256]{1,0:T(8,128)(2,1)S(1)}, bf16[128,256]{1,0:T(8,128)(2,1)S(1)}, u32[]{:S(2)}, u32[]{:S(2)}) collective-permute-start(bf16[128,256]{1,0:T(8,128)(2,1)S(1)} %get-tuple-element.40), channel_id=1, source_target_pairs={{0,8},{1,9},{2,10},{3,11},{4,40},{5,41},{6,42},{7,43},{8,72},{9,73... | collective-permute-start | bytes 196616 | tf_op jit(solution)/shard_map/ppermute | solution.py:240
  10.7 11.1 %collective-permute-start.3 = (bf16[128,256]{1,0:T(8,128)(2,1)S(1)}, bf16[128,256]{1,0:T(8,128)(2,1)S(1)}, u32[]{:S(2)}, u32[]{:S(2)}) collective-permute-start(bf16[128,256]{1,0:T(8,128)(2,1)S(1)} %get-tuple-element.39), channel_id=1, source_target_pairs={{0,16},{1,17},{2,18},{3,19},{4,48},{5,49},{6,50},{7,51},{8,80},{9,... | collective-permute-start | bytes 196616 | tf_op jit(solution)/shard_map/ppermute | solution.py:240
  19.4 4.3 %collective-permute-start.4 = (bf16[128,256]{1,0:T(8,128)(2,1)S(1)}, bf16[128,256]{1,0:T(8,128)(2,1)S(1)}, u32[]{:S(2)}, u32[]{:S(2)}) collective-permute-start(bf16[128,256]{1,0:T(8,128)(2,1)S(1)} %get-tuple-element.38), channel_id=1, source_target_pairs={{0,24},{1,25},{2,26},{3,27},{4,56},{5,57},{6,58},{7,59},{8,88},{9,... | collective-permute-start | bytes 196616 | tf_op jit(solution)/shard_map/ppermute | solution.py:240
  21.6 24.9 %collective-permute-start.10 = (bf16[2,128,1024]{2,1,0:T(8,128)(2,1)S(1)}, bf16[2,128,1024]{2,1,0:T(8,128)(2,1)S(1)}, u32[]{:S(2)}, u32[]{:S(2)}) collective-permute-start(bf16[2,128,1024]{2,1,0:T(8,128)(2,1)S(1)} %pad_maximum_fusion.refs_0_), channel_id=1, source_target_pairs={{128,0},{192,64},{0,128},{64,192},{129,1},{193,65},{1,129},{65,193... | collective-permute-start | bytes 1572872 | tf_op jit(solution)/shard_map/ppermute | solution.py:37
  23.8 18.3 %collective-permute-start.5 = (bf16[128,1024]{1,0:T(8,128)(2,1)S(1)}, bf16[128,1024]{1,0:T(8,128)(2,1)S(1)}, u32[]{:S(2)}, u32[]{:S(2)}) collective-permute-start(bf16[128,1024]{1,0:T(8,128)(2,1)S(1)} %constant_dynamic-update-slice_fusion.refs_5_), channel_id=1, source_target_pairs={{8,0},{16,8},{24,16},{0,24},{9,1},{17,9},{25,17},{1,25},{10,2},{18... | collective-permute-start | bytes 786440 | tf_op jit(solution)/shard_map/ppermute | solution.py:37
  27.3 14.8 %collective-permute-start.6 = (bf16[128,1024]{1,0:T(8,128)(2,1)S(1)}, bf16[128,1024]{1,0:T(8,128)(2,1)S(1)}, u32[]{:S(2)}, u32[]{:S(2)}) collective-permute-start(bf16[128,1024]{1,0:T(8,128)(2,1)S(1)} %constant_dynamic-update-slice_fusion.refs_5_), channel_id=1, source_target_pairs={{24,0},{0,8},{8,16},{16,24},{25,1},{1,9},{9,17},{17,25},{26,2},{2,... | collective-permute-start | bytes 786440 | tf_op jit(solution)/shard_map/ppermute | solution.py:37
  27.3 14.8 %collective-permute-start.7 = (bf16[128,1024]{1,0:T(8,128)(2,1)S(1)}, bf16[128,1024]{1,0:T(8,128)(2,1)S(1)}, u32[]{:S(2)}, u32[]{:S(2)}) collective-permute-start(bf16[128,1024]{1,0:T(8,128)(2,1)S(1)} %constant_dynamic-update-slice_fusion.refs_5_), channel_id=1, source_target_pairs={{0,2},{2,0},{4,6},{6,4},{1,3},{3,1},{5,7},{7,5},{8,10},{10,8},{12,... | collective-permute-start | bytes 786440 | tf_op jit(solution)/shard_map/ppermute | solution.py:41
  28.6 17.1 %collective-permute-start.8 = (bf16[128,1024]{1,0:T(8,128)(2,1)S(1)}, bf16[128,1024]{1,0:T(8,128)(2,1)S(1)}, u32[]{:S(2)}, u32[]{:S(2)}) collective-permute-start(bf16[128,1024]{1,0:T(8,128)(2,1)S(1)} %constant_dynamic-update-slice_fusion.refs_5_), channel_id=1, source_target_pairs={{0,6},{2,4},{4,2},{6,0},{1,7},{3,5},{5,3},{7,1},{8,14},{10,12},{12... | collective-permute-start | bytes 786440 | tf_op jit(solution)/shard_map/ppermute | solution.py:41
  42.0 25.1 %copy-start.3 = (bf16[128,1024]{1,0:T(8,128)(2,1)}, bf16[128,1024]{1,0:T(8,128)(2,1)S(1)}, u32[]{:S(2)}) copy-start(bf16[128,1024]{1,0:T(8,128)(2,1)S(1)} %collective-permute-done.5.refs_0_.refs_9_) | copy-start | bytes 786436
  42.0 25.1 %copy-start.5 = (bf16[128,1024]{1,0:T(8,128)(2,1)}, bf16[128,1024]{1,0:T(8,128)(2,1)S(1)}, u32[]{:S(2)}) copy-start(bf16[128,1024]{1,0:T(8,128)(2,1)S(1)} %collective-permute-done.6.refs_1_.refs_11_) | copy-start | bytes 786436
  42.0 16.0 %copy-start.7 = (bf16[128,1024]{1,0:T(8,128)(2,1)}, bf16[128,1024]{1,0:T(8,128)(2,1)S(1)}, u32[]{:S(2)}) copy-start(bf16[128,1024]{1,0:T(8,128)(2,1)S(1)} %collective-permute-done.7.refs_2_.refs_6_) | copy-start | bytes 786436
  46.6 19.3 %collective-permute-start.15 = (bf16[384,1024]{1,0:T(8,128)(2,1)S(1)}, bf16[384,1024]{1,0:T(8,128)(2,1)S(1)}, u32[]{:S(2)}, u32[]{:S(2)}) collective-permute-start(bf16[384,1024]{1,0:T(8,128)(2,1)S(1)} %get-tuple-element.26), channel_id=1, source_target_pairs={{0,6},{2,4},{4,2},{6,0},{1,7},{3,5},{5,3},{7,1},{8,14},{10,12},{12... | collective-permute-start | bytes 2359304 | tf_op jit(solution)/shard_map/ppermute | solution.py:41
  49.5 8.5 %collective-permute-start.11 = (bf16[2,128,1024]{2,1,0:T(8,128)(2,1)S(1)}, bf16[2,128,1024]{2,1,0:T(8,128)(2,1)S(1)}, u32[]{:S(2)}, u32[]{:S(2)}) collective-permute-start(bf16[2,128,1024]{2,1,0:T(8,128)(2,1)S(1)} %pad_maximum_fusion.refs_0_), channel_id=1, source_target_pairs={{64,0},{128,64},{192,128},{0,192},{65,1},{129,65},{193,129},{1,193... | collective-permute-start | bytes 1572872 | tf_op jit(solution)/shard_map/ppermute | solution.py:37
  49.5 9.7 %collective-permute-start.12 = (bf16[2,128,1024]{2,1,0:T(8,128)(2,1)S(1)}, bf16[2,128,1024]{2,1,0:T(8,128)(2,1)S(1)}, u32[]{:S(2)}, u32[]{:S(2)}) collective-permute-start(bf16[2,128,1024]{2,1,0:T(8,128)(2,1)S(1)} %pad_maximum_fusion.refs_0_), channel_id=1, source_target_pairs={{192,0},{0,64},{64,128},{128,192},{193,1},{1,65},{65,129},{129,193... | collective-permute-start | bytes 1572872 | tf_op jit(solution)/shard_map/ppermute | solution.py:37
  51.0 15.0 %collective-permute-start.16 = (bf16[256,1024]{1,0:T(8,128)(2,1)S(1)}, bf16[256,1024]{1,0:T(8,128)(2,1)S(1)}, u32[]{:S(2)}, u32[]{:S(2)}) collective-permute-start(bf16[256,1024]{1,0:T(8,128)(2,1)S(1)} %get-tuple-element.27), channel_id=1, source_target_pairs={{0,2},{2,0},{4,6},{6,4},{1,3},{3,1},{5,7},{7,5},{8,10},{10,8},{12,... | collective-permute-start | bytes 1572872 | tf_op jit(solution)/shard_map/ppermute | solution.py:41
  51.0 15.0 %collective-permute-start.14 = (bf16[128,1024]{1,0:T(8,128)(2,1)S(1)}, bf16[128,1024]{1,0:T(8,128)(2,1)S(1)}, u32[]{:S(2)}, u32[]{:S(2)}) collective-permute-start(bf16[128,1024]{1,0:T(8,128)(2,1)S(1)} %constant_dynamic-update-slice_fusion.refs_5_), channel_id=1, source_target_pairs={{16,0},{24,8},{0,16},{8,24},{17,1},{25,9},{1,17},{9,25},{18,2},{26... | collective-permute-start | bytes 786440 | tf_op jit(solution)/shard_map/ppermute | solution.py:37
  60.0 7.6 %collective-permute-start.13 = (bf16[8,128,128]{2,1,0:T(8,128)(2,1)}, bf16[8,128,128]{2,1,0:T(8,128)(2,1)S(1)}, u32[]{:S(2)}, u32[]{:S(2)}) collective-permute-start(bf16[8,128,128]{2,1,0:T(8,128)(2,1)} %shard_map.17), channel_id=1, source_target_pairs={{0,1},{1,0},{2,3},{3,2},{4,5},{5,4},{6,7},{7,6},{8,9},{9,8},{10,11... | collective-permute-start | bytes 786440 | tf_op jit(solution)/shard_map/ppermute | solution.py:41
  66.0 1.4 %copy-start.9 = (bf16[128,1024]{1,0:T(8,128)(2,1)}, bf16[128,1024]{1,0:T(8,128)(2,1)S(1)}, u32[]{:S(2)}) copy-start(bf16[128,1024]{1,0:T(8,128)(2,1)S(1)} %collective-permute-done.14.refs_0_.refs_8_) | copy-start | bytes 786436
  66.0 1.3 %copy-start = (bf16[384,1024]{1,0:T(8,128)(2,1)}, bf16[384,1024]{1,0:T(8,128)(2,1)S(1)}, u32[]{:S(2)}) copy-start(bf16[384,1024]{1,0:T(8,128)(2,1)S(1)} %collective-permute-done.15.refs_1_.refs_7_.refs_6_) | copy-start | bytes 2359300
  67.1 14.8 %collective-permute-start.17 = (bf16[256,1024]{1,0:T(8,128)(2,1)}, bf16[256,1024]{1,0:T(8,128)(2,1)}, u32[]{:S(2)}, u32[]{:S(2)}) collective-permute-start(bf16[256,1024]{1,0:T(8,128)(2,1)} %get-tuple-element.28), channel_id=1, source_target_pairs={{0,2},{2,0},{4,6},{6,4},{1,3},{3,1},{5,7},{7,5},{8,10},{10,8},{12,... | collective-permute-start | bytes 1572872 | tf_op jit(solution)/shard_map/ppermute | solution.py:41
  67.3 14.6 %collective-permute-start.18 = (bf16[256,1024]{1,0:T(8,128)(2,1)}, bf16[256,1024]{1,0:T(8,128)(2,1)S(1)}, u32[]{:S(2)}, u32[]{:S(2)}) collective-permute-start(bf16[256,1024]{1,0:T(8,128)(2,1)} %get-tuple-element.29), channel_id=1, source_target_pairs={{0,6},{2,4},{4,2},{6,0},{1,7},{3,5},{5,3},{7,1},{8,14},{10,12},{12... | collective-permute-start | bytes 1572872 | tf_op jit(solution)/shard_map/ppermute | solution.py:41
  67.6 1.1 %copy-start.1 = (bf16[384,1024]{1,0:T(8,128)(2,1)S(1)}, bf16[384,1024]{1,0:T(8,128)(2,1)}, u32[]{:S(2)}) copy-start(bf16[384,1024]{1,0:T(8,128)(2,1)} %copy-done) | copy-start | bytes 2359300
  68.7 0.9 copy-start.4
  69.7 0.9 copy-start.6
  73.5 12.1 %copy-start.2 = (bf16[384,1024]{1,0:T(8,128)(2,1)S(1)}, bf16[384,1024]{1,0:T(8,128)(2,1)}, u32[]{:S(2)}) copy-start(bf16[384,1024]{1,0:T(8,128)(2,1)} %copy-done) | copy-start | bytes 2359300
  73.5 12.1 %copy-start.10 = (bf16[128,1024]{1,0:T(8,128)(2,1)S(1)}, bf16[128,1024]{1,0:T(8,128)(2,1)}, u32[]{:S(2)}) copy-start(bf16[128,1024]{1,0:T(8,128)(2,1)} %copy-done.9) | copy-start | bytes 786436
  82.9 9.6 %collective-permute-start.19 = (bf16[64,1024]{1,0:T(8,128)(2,1)S(1)}, bf16[64,1024]{1,0:T(8,128)(2,1)S(1)}, u32[]{:S(2)}, u32[]{:S(2)}) collective-permute-start(bf16[64,1024]{1,0:T(8,128)(2,1)S(1)} %get-tuple-element.33), channel_id=1, source_target_pairs={{0,6},{2,4},{4,2},{6,0},{1,7},{3,5},{5,3},{7,1},{8,14},{10,12},{12... | collective-permute-start | bytes 393224 | tf_op jit(solution)/shard_map/ppermute | solution.py:41
  85.5 7.0 %collective-permute-start.20 = (bf16[64,1024]{1,0:T(8,128)(2,1)S(1)}, bf16[64,1024]{1,0:T(8,128)(2,1)S(1)}, u32[]{:S(2)}, u32[]{:S(2)}) collective-permute-start(bf16[64,1024]{1,0:T(8,128)(2,1)S(1)} %get-tuple-element.34), channel_id=1, source_target_pairs={{0,2},{2,0},{4,6},{6,4},{1,3},{3,1},{5,7},{7,5},{8,10},{10,8},{12,... | collective-permute-start | bytes 393224 | tf_op jit(solution)/shard_map/ppermute | solution.py:41
  94.6 5.9 %collective-permute-start.21 = (f32[16,64,256]{2,1,0:T(8,128)S(1)}, f32[16,64,256]{2,1,0:T(8,128)S(1)}, u32[]{:S(2)}, u32[]{:S(2)}) collective-permute-start(f32[16,64,256]{2,1,0:T(8,128)S(1)} %shard_map.24), channel_id=1, source_target_pairs={{0,1},{1,0},{2,3},{3,2},{4,5},{5,4},{6,7},{7,6},{8,9},{9,8},{10,11... | collective-permute-start | bytes 3145736 | tf_op jit(solution)/shard_map/ppermute | solution.py:41
  (5 other events, 4.2 us)
